TPU v7x, 32 devices: a whole 2x2x4 slice. The times are simulated.
32 devices in a mesh: lon: 4 (over y, x), lat: 4 (over z), rad: 2 (over core).
Axes of the slice: x: 2, y: 2, z: 4, core: 2. Of those that a mesh axis runs over, the one named last changes fastest.
Arguments:
- adj_now: float32 [16, 128, 512], P('rad', 'lat', 'lon'), may hold values from -6 to 6
- adj_next: float32 [16, 128, 512], P('rad', 'lat', 'lon'), may hold values from -6 to 6
- fwd_now: float32 [16, 128, 512], P('rad', 'lat', 'lon'), may hold values from -6 to 6
- fwd_next: float32 [16, 128, 512], P('rad', 'lat', 'lon'), may hold values from -6 to 6
- stiffness: float32 [16, 128, 512], P('rad', 'lat', 'lon'), may hold values from 0.04 to 0.15
- buoyancy: float32 [16, 128, 512], P('rad', 'lat', 'lon'), may hold values from 0.6 to 1.5
- kernel_bulk_in: float32 [16, 128, 512], P('rad', 'lat', 'lon'), may hold values from -6 to 6
- kernel_density_in: float32 [16, 128, 512], P('rad', 'lat', 'lon'), may hold values from -6 to 6
Outputs:
- adj_out_now: float32 [16, 128, 512], P('rad', 'lat', 'lon')
- adj_out_next: float32 [16, 128, 512], P('rad', 'lat', 'lon')
- fwd_out_now: float32 [16, 128, 512], P('rad', 'lat', 'lon')
- fwd_out_next: float32 [16, 128, 512], P('rad', 'lat', 'lon')
- kernel_bulk: float32 [16, 128, 512], P('rad', 'lat', 'lon')
- kernel_density: float32 [16, 128, 512], P('rad', 'lat', 'lon')
All inputs are finite; a program needn't handle non-finite values.
Results may differ from a plain program's by a relative error of at most 0.00002.
Values sent between devices are 32-bit elements; how exact they have to be, the bound alone decides.
No kernel may reach another device: no remote copies, remote signals or barrier semaphores. Data moves between devices by JAX's collectives and lax.ppermute only.
A program may use at most 64 MiB of HBM per device.

v0:
```python
import jax
import jax.numpy as jnp
from jax import lax
from jax.sharding import PartitionSpec as P

coef_near = 9.0 / 8.0
coef_far = -1.0 / 24.0


def padded_2(block, sides, width, periodic):
    for axis, dim in sides:
        count = lax.axis_size(axis)
        forward = [(i, i + 1) for i in range(count - 1)]
        if periodic:
            forward.append((count - 1, 0))
        backward = [(target, source) for source, target in forward]
        low = lax.ppermute(
            lax.slice_in_dim(block, block.shape[dim] - width, None, axis=dim), axis, forward
        )
        high = lax.ppermute(lax.slice_in_dim(block, 0, width, axis=dim), axis, backward)
        block = jnp.concatenate([low, block, high], axis=dim)
    return block


def piece(field, first, last, axis_num):
    return lax.slice_in_dim(field, first, last, axis=axis_num)


def crop_all(field, width):
    for axis_num in range(3):
        field = piece(field, width, field.shape[axis_num] - width, axis_num)
    return field


def rim_cells(stacked, width):
    wrapped_cells = padded_2(stacked, (("lon", 3),), width, True)
    return padded_2(wrapped_cells, (("lat", 2), ("rad", 1)), width, False)


def operate(adj_pad, fwd_pad, buoy_pad):
    lap_adj = None
    lap_fwd = None
    rho_term = None
    for dim_index in range(3):
        arrays = []
        for source in (adj_pad, fwd_pad, buoy_pad):
            for other in range(3):
                if other != dim_index:
                    source = piece(source, 3, source.shape[other] - 3, other)
            arrays.append(source)
        adj_part, fwd_part, buoy_part = arrays
        length = adj_part.shape[dim_index]

        def faces(field):
            near = piece(field, 2, length - 1, dim_index) - piece(field, 1, length - 2, dim_index)
            far = piece(field, 3, length, dim_index) - piece(field, 0, length - 3, dim_index)
            return coef_near * near + coef_far * far

        face_buoy = 0.5 * (
            piece(buoy_part, 1, length - 2, dim_index) + piece(buoy_part, 2, length - 1, dim_index)
        )
        grad_adj = faces(adj_part)
        grad_fwd = faces(fwd_part)
        count = length - 3

        def diverge(flux):
            near = piece(flux, 2, count - 1, dim_index) - piece(flux, 1, count - 2, dim_index)
            far = piece(flux, 3, count, dim_index) - piece(flux, 0, count - 3, dim_index)
            return coef_near * near + coef_far * far

        term_adj = diverge(face_buoy * grad_adj)
        term_fwd = diverge(face_buoy * grad_fwd)
        product = face_buoy * grad_adj * grad_fwd
        term_rho = 0.5 * (
            piece(product, 2, count - 1, dim_index) + piece(product, 1, count - 2, dim_index)
        )
        if lap_adj is None:
            lap_adj, lap_fwd, rho_term = (term_adj, term_fwd, term_rho)
        else:
            lap_adj = lap_adj + term_adj
            lap_fwd = lap_fwd + term_fwd
            rho_term = rho_term + term_rho
    return (lap_adj, lap_fwd, rho_term)


def shards(
    adj_now, adj_next, fwd_now, fwd_next, stiffness, buoyancy, kernel_bulk_in, kernel_density_in
):
    kernel_bulk = kernel_bulk_in
    kernel_density = kernel_density_in
    stacked = jnp.stack([adj_now, fwd_now, adj_next, fwd_next, stiffness, buoyancy])
    padded = rim_cells(stacked, 6)
    adj_wide = padded[0]
    fwd_wide = padded[1]
    adj_next_wide = padded[2]
    fwd_next_wide = padded[3]
    stiff_wide = padded[4]
    buoy_wide = padded[5]
    lap_adj, lap_fwd, rho_term = operate(adj_wide, fwd_wide, buoy_wide)
    stiff_mid = crop_all(stiff_wide, 3)
    kernel_bulk = kernel_bulk + adj_now * (stiffness * crop_all(lap_fwd, 3))
    kernel_density = kernel_density + crop_all(rho_term, 3)
    first_adj = 2.0 * crop_all(adj_wide, 3) - crop_all(adj_next_wide, 3) + stiff_mid * lap_adj
    first_fwd = 2.0 * crop_all(fwd_wide, 3) - crop_all(fwd_next_wide, 3) + stiff_mid * lap_fwd
    lap_adj, lap_fwd, rho_term = operate(first_adj, first_fwd, crop_all(buoy_wide, 3))
    inner_adj = crop_all(first_adj, 3)
    inner_fwd = crop_all(first_fwd, 3)
    kernel_bulk = kernel_bulk + inner_adj * (stiffness * lap_fwd)
    kernel_density = kernel_density + rho_term
    new_adj = 2.0 * inner_adj - adj_now + stiffness * lap_adj
    new_fwd = 2.0 * inner_fwd - fwd_now + stiffness * lap_fwd
    return (new_adj, inner_adj, new_fwd, inner_fwd, kernel_bulk, kernel_density)


def solution(mesh):
    in_specs = (
        P("rad", "lat", "lon"),
        P("rad", "lat", "lon"),
        P("rad", "lat", "lon"),
        P("rad", "lat", "lon"),
        P("rad", "lat", "lon"),
        P("rad", "lat", "lon"),
        P("rad", "lat", "lon"),
        P("rad", "lat", "lon"),
    )
    out_specs = (
        P("rad", "lat", "lon"),
        P("rad", "lat", "lon"),
        P("rad", "lat", "lon"),
        P("rad", "lat", "lon"),
        P("rad", "lat", "lon"),
        P("rad", "lat", "lon"),
    )
    return jax.shard_map(shards, mesh=mesh, in_specs=in_specs, out_specs=out_specs, check_vma=False)
```

profile of v0, /device:TPU:11, one launch (start us, length us, event | category | flops | bytes accessed | tf_op | source)
XLA Modules:
  0.0 63.5 jit_solution(600044511820056447)
XLA Ops:
  1.5 0.9 %bitcast_dynamic-update-slice_fusion.4 = f32[6,8,32,128]{3,2,1,0:T(8,128)S(1)} fusion(f32[6,8,32,128]{3,2,1,0:T(8,128)S(1)} %bitcast_dynamic-update-slice_fusion.5, f32[8,32,128]{2,1,0:T(8,128)} %param.10), kind=kLoop, calls=%fused_computation.195 | loop fusion | bytes 262144
  2.5 0.9 %bitcast_dynamic-update-slice_fusion.3 = f32[6,8,32,128]{3,2,1,0:T(8,128)S(1)} fusion(f32[6,8,32,128]{3,2,1,0:T(8,128)S(1)} %bitcast_dynamic-update-slice_fusion.4, f32[8,32,128]{2,1,0:T(8,128)} %param.9), kind=kLoop, calls=%fused_computation.194 | loop fusion | bytes 262144
  3.4 0.9 %bitcast_dynamic-update-slice_fusion.2 = f32[6,8,32,128]{3,2,1,0:T(8,128)S(1)} fusion(f32[6,8,32,128]{3,2,1,0:T(8,128)S(1)} %bitcast_dynamic-update-slice_fusion.3, f32[8,32,128]{2,1,0:T(8,128)} %param.11), kind=kLoop, calls=%fused_computation.193 | loop fusion | bytes 262144
  4.3 0.9 %bitcast_dynamic-update-slice_fusion.1 = f32[6,8,32,128]{3,2,1,0:T(8,128)S(1)} fusion(f32[6,8,32,128]{3,2,1,0:T(8,128)S(1)} %bitcast_dynamic-update-slice_fusion.2, f32[8,32,128]{2,1,0:T(8,128)} %param.12), kind=kLoop, calls=%fused_computation.192 | loop fusion | bytes 262144
  5.2 0.9 %bitcast_dynamic-update-slice_fusion = f32[6,8,32,128]{3,2,1,0:T(8,128)S(1)} fusion(f32[6,8,32,128]{3,2,1,0:T(8,128)S(1)} %bitcast_dynamic-update-slice_fusion.1, f32[8,32,128]{2,1,0:T(8,128)} %param.13), kind=kLoop, calls=%fused_computation.191 | loop fusion | bytes 262144 | tf_op jit(solution)/shard_map/stack | solution.py:91
  6.8 1.3 %collective-permute-start = (f32[6,8,32,6]{2,1,3,0:T(8,128)S(1)}, f32[6,8,32,6]{2,1,3,0:T(8,128)S(1)}, u32[]{:S(2)}, u32[]{:S(2)}) collective-permute-start(f32[6,8,32,6]{2,1,3,0:T(8,128)S(1)} %copy.65), channel_id=1, source_target_pairs={{0,8},{8,16},{16,24},{24,0},{1,9},{9,17},{17,25},{25,1},{2,10},{10... | collective-permute-start | bytes 110600 | tf_op jit(solution)/shard_map/ppermute | solution.py:17
  9.2 2.4 %collective-permute-done = f32[6,8,32,6]{2,1,3,0:T(8,128)S(1)} collective-permute-done((f32[6,8,32,6]{2,1,3,0:T(8,128)S(1)}, f32[6,8,32,6]{2,1,3,0:T(8,128)S(1)}, u32[]{:S(2)}, u32[]{:S(2)}) %collective-permute-start) | collective-permute-done | bytes 36896 | tf_op jit(solution)/shard_map/ppermute | solution.py:17
  12.0 3.7 %collective-permute-done.1 = f32[6,8,32,6]{2,1,3,0:T(8,128)S(1)} collective-permute-done((f32[6,8,32,6]{2,1,3,0:T(8,128)S(1)}, f32[6,8,32,6]{2,1,3,0:T(8,128)S(1)}, u32[]{:S(2)}, u32[]{:S(2)}) %collective-permute-start.1) | collective-permute-done | bytes 36896 | tf_op jit(solution)/shard_map/ppermute | solution.py:20
  16.4 3.2 %collective-permute-start.2 = (f32[6,8,6,140]{3,1,2,0:T(8,128)S(1)}, f32[6,8,6,140]{3,1,2,0:T(8,128)S(1)}, u32[]{:S(2)}, u32[]{:S(2)}) collective-permute-start(f32[6,8,6,140]{3,1,2,0:T(8,128)S(1)} %get-tuple-element.49), channel_id=1, source_target_pairs={{0,2},{2,4},{4,6},{1,3},{3,5},{5,7},{8,10},{10,12},{12,14},{9,11},... | collective-permute-start | bytes 483848 | tf_op jit(solution)/shard_map/ppermute | solution.py:17
  19.6 2.1 %collective-permute-start.3 = (f32[6,8,6,140]{3,1,2,0:T(8,128)S(1)}, f32[6,8,6,140]{3,1,2,0:T(8,128)S(1)}, u32[]{:S(2)}, u32[]{:S(2)}) collective-permute-start(f32[6,8,6,140]{3,1,2,0:T(8,128)S(1)} %get-tuple-element.50), channel_id=1, source_target_pairs={{2,0},{4,2},{6,4},{3,1},{5,3},{7,5},{10,8},{12,10},{14,12},{11,9},... | collective-permute-start | bytes 483848 | tf_op jit(solution)/shard_map/ppermute | solution.py:20
  21.7 3.5 %collective-permute-done.2 = f32[6,8,6,140]{3,1,2,0:T(8,128)S(1)} collective-permute-done((f32[6,8,6,140]{3,1,2,0:T(8,128)S(1)}, f32[6,8,6,140]{3,1,2,0:T(8,128)S(1)}, u32[]{:S(2)}, u32[]{:S(2)}) %collective-permute-start.2) | collective-permute-done | bytes 161312 | tf_op jit(solution)/shard_map/ppermute | solution.py:17
  25.2 2.9 %collective-permute-done.3 = f32[6,8,6,140]{3,1,2,0:T(8,128)S(1)} collective-permute-done((f32[6,8,6,140]{3,1,2,0:T(8,128)S(1)}, f32[6,8,6,140]{3,1,2,0:T(8,128)S(1)}, u32[]{:S(2)}, u32[]{:S(2)}) %collective-permute-start.3) | collective-permute-done | bytes 161312 | tf_op jit(solution)/shard_map/ppermute | solution.py:20
  29.8 4.8 %collective-permute-start.5 = (f32[6,6,44,140]{3,2,1,0:T(8,128)S(1)}, f32[6,6,44,140]{3,2,1,0:T(8,128)S(1)}, u32[]{:S(2)}, u32[]{:S(2)}) collective-permute-start(f32[6,6,44,140]{3,2,1,0:T(8,128)S(1)} %copy.48), channel_id=1, source_target_pairs={{1,0},{3,2},{5,4},{7,6},{9,8},{11,10},{13,12},{15,14},{17,16},{19,... | collective-permute-start | bytes 2661128 | tf_op jit(solution)/shard_map/ppermute | solution.py:20
  35.1 1.3 %collective-permute-start.4 = (f32[6,6,44,140]{3,2,1,0:T(8,128)S(1)}, f32[6,6,44,140]{3,2,1,0:T(8,128)S(1)}, u32[]{:S(2)}, u32[]{:S(2)}) collective-permute-start(f32[6,6,44,140]{3,2,1,0:T(8,128)S(1)} %copy.47), channel_id=1, source_target_pairs={{0,1},{2,3},{4,5},{6,7},{8,9},{10,11},{12,13},{14,15},{16,17},{18,... | collective-permute-start | bytes 2661128 | tf_op jit(solution)/shard_map/ppermute | solution.py:17
  36.4 1.4 %collective-permute-done.5 = f32[6,6,44,140]{3,2,1,0:T(8,128)S(1)} collective-permute-done((f32[6,6,44,140]{3,2,1,0:T(8,128)S(1)}, f32[6,6,44,140]{3,2,1,0:T(8,128)S(1)}, u32[]{:S(2)}, u32[]{:S(2)}) %collective-permute-start.5) | collective-permute-done | bytes 887072 | tf_op jit(solution)/shard_map/ppermute | solution.py:20
  37.7 1.0 %copy.50 = f32[6,6,44,140]{3,1,2,0:T(8,128)S(1)} copy(f32[6,6,44,140]{3,2,1,0:T(8,128)S(1)} %collective-permute-done.5) | data formatting | bytes 1774080 | tf_op jit(solution)/shard_map/ppermute | solution.py:20
  38.7 2.0 %collective-permute-done.4 = f32[6,6,44,140]{3,2,1,0:T(8,128)S(1)} collective-permute-done((f32[6,6,44,140]{3,2,1,0:T(8,128)S(1)}, f32[6,6,44,140]{3,2,1,0:T(8,128)S(1)}, u32[]{:S(2)}, u32[]{:S(2)}) %collective-permute-start.4) | collective-permute-done | bytes 887072 | tf_op jit(solution)/shard_map/ppermute | solution.py:17
  40.6 1.0 %copy.49 = f32[6,6,44,140]{3,1,2,0:T(8,128)S(1)} copy(f32[6,6,44,140]{3,2,1,0:T(8,128)S(1)} %collective-permute-done.4) | data formatting | bytes 1774080 | tf_op jit(solution)/shard_map/ppermute | solution.py:17
  41.6 2.8 %pad_maximum_fusion = f32[6,20,44,140]{3,1,2,0:T(8,128)S(1)} fusion(f32[6,6,44,140]{3,1,2,0:T(8,128)S(1)} %copy.50, f32[6,8,6,140]{3,1,2,0:T(8,128)S(1)} %collective-permute-done.3, f32[6,8,32,6]{3,1,2,0:T(8,128)S(1)} %copy.46, f32[6,8,32,128]{3,1,2,0:T(8,128)S(1)} %copy.45, f32[6,8,32,6]{3,1,2,0:T(8,128)S(1)} %copy.44, ...), kind=kLoop, calls=%fused_computation | loop fusion | flops 4435200 | bytes 5913600 | tf_op jit(solution)/shard_map/concatenate | solution.py:21
  45.3 1.4 %fusion.122 = (f32[14,38,137]{2,0,1:T(8,128)S(1)}, f32[14,38,137]{2,0,1:T(8,128)S(1)}, f32[14,38,137]{2,0,1:T(8,128)S(1)}) fusion(f32[14,44,140]{2,0,1:T(8,128)S(1)} %get-tuple-element.42, f32[14,44,140]{2,0,1:T(8,128)S(1)} %get-tuple-element.45, f32[14,44,140]{2,0,1:T(8,128)S(1)} %get-tuple-element.43), kind=kLoop, calls=%fused_computation.204 | loop fusion | flops 1020376 | bytes 3789968 | tf_op jit(solution)/shard_map/mul | solution.py:73
  46.7 1.8 %fusion.119 = (f32[14,41,134]{2,0,1:T(8,128)S(1)}, f32[14,41,134]{2,0,1:T(8,128)S(1)}, f32[14,41,134]{2,0,1:T(8,128)S(1)}) fusion(f32[14,44,140]{2,0,1:T(8,128)S(1)} %get-tuple-element.42, f32[14,44,140]{2,0,1:T(8,128)S(1)} %get-tuple-element.45, f32[14,44,140]{2,0,1:T(8,128)S(1)} %get-tuple-element.43), kind=kLoop, calls=%fused_computation.203 | loop fusion | flops 1076824 | bytes 3999632 | tf_op jit(solution)/shard_map/mul | solution.py:73
  48.5 2.5 %fusion.116 = (f32[17,38,134]{2,0,1:T(8,128)S(1)}, f32[17,38,134]{2,0,1:T(8,128)S(1)}, f32[17,38,134]{2,0,1:T(8,128)S(1)}) fusion(f32[20,44,140]{2,0,1:T(8,128)S(1)} %get-tuple-element.47, f32[20,44,140]{2,0,1:T(8,128)S(1)} %get-tuple-element.48, f32[20,44,140]{2,0,1:T(8,128)S(1)} %get-tuple-element.46), kind=kLoop, calls=%fused_computation.202 | loop fusion | flops 1211896 | bytes 4501328 | tf_op jit(solution)/shard_map/mul | solution.py:73
  52.4 1.1 %fusion.30 = (f32[14,38,134]{2,0,1:T(8,128)S(1)}, f32[14,38,134]{2,0,1:T(8,128)S(1)}) fusion(f32[14,44,140]{2,0,1:T(8,128)S(1)} %get-tuple-element.41, f32[14,44,140]{2,0,1:T(8,128)S(1)} %get-tuple-element.42, f32[14,44,140]{2,0,1:T(8,128)S(1)} %get-tuple-element.44, f32[14,38,137]{2,0,1:T(8,128)S(1)} %fusion.67, f32[14,41,134]{2,0,1:T(8,128)S(1)} %fusion.66, ...), kind=kLoop, calls=%fused_computation.60 | loop fusion | flops 1497048 | bytes 4847584 | tf_op jit(solution)/shard_map/add | solution.py:104
  53.5 1.3 %fusion.140 = (f32[14,38,134]{2,0,1:T(8,128)S(1)}, f32[14,38,134]{2,0,1:T(8,128)S(1)}, f32[14,38,134]{2,0,1:T(8,128)S(1)}) fusion(f32[14,38,137]{2,0,1:T(8,128)S(1)} %get-tuple-element.24, f32[14,38,137]{2,0,1:T(8,128)S(1)} %get-tuple-element.26, f32[14,41,134]{2,0,1:T(8,128)S(1)} %get-tuple-element.23, f32[17,38,134]{2,0,1:T(8,128)S(1)} %get-tuple-element.20, ...), kind=kLoop, calls=%fused_computation.212 | loop fusion | flops 1497048 | bytes 5703040 | tf_op jit(solution)/shard_map/slice | solution.py:26
  (45 shorter events, 16.8 us)
Async XLA Ops:
  6.8 4.8 %collective-permute-start = (f32[6,8,32,6]{2,1,3,0:T(8,128)S(1)}, f32[6,8,32,6]{2,1,3,0:T(8,128)S(1)}, u32[]{:S(2)}, u32[]{:S(2)}) collective-permute-start(f32[6,8,32,6]{2,1,3,0:T(8,128)S(1)} %copy.65), channel_id=1, source_target_pairs={{0,8},{8,16},{16,24},{24,0},{1,9},{9,17},{17,25},{25,1},{2,10},{10... | collective-permute-start | bytes 110600 | tf_op jit(solution)/shard_map/ppermute | solution.py:17
  8.5 7.2 %collective-permute-start.1 = (f32[6,8,32,6]{2,1,3,0:T(8,128)S(1)}, f32[6,8,32,6]{2,1,3,0:T(8,128)S(1)}, u32[]{:S(2)}, u32[]{:S(2)}) collective-permute-start(f32[6,8,32,6]{2,1,3,0:T(8,128)S(1)} %copy.66), channel_id=1, source_target_pairs={{8,0},{16,8},{24,16},{0,24},{9,1},{17,9},{25,17},{1,25},{10,2},{18... | collective-permute-start | bytes 110600 | tf_op jit(solution)/shard_map/ppermute | solution.py:20
  16.4 8.8 %collective-permute-start.2 = (f32[6,8,6,140]{3,1,2,0:T(8,128)S(1)}, f32[6,8,6,140]{3,1,2,0:T(8,128)S(1)}, u32[]{:S(2)}, u32[]{:S(2)}) collective-permute-start(f32[6,8,6,140]{3,1,2,0:T(8,128)S(1)} %get-tuple-element.49), channel_id=1, source_target_pairs={{0,2},{2,4},{4,6},{1,3},{3,5},{5,7},{8,10},{10,12},{12,14},{9,11},... | collective-permute-start | bytes 483848 | tf_op jit(solution)/shard_map/ppermute | solution.py:17
  19.6 8.6 %collective-permute-start.3 = (f32[6,8,6,140]{3,1,2,0:T(8,128)S(1)}, f32[6,8,6,140]{3,1,2,0:T(8,128)S(1)}, u32[]{:S(2)}, u32[]{:S(2)}) collective-permute-start(f32[6,8,6,140]{3,1,2,0:T(8,128)S(1)} %get-tuple-element.50), channel_id=1, source_target_pairs={{2,0},{4,2},{6,4},{3,1},{5,3},{7,5},{10,8},{12,10},{14,12},{11,9},... | collective-permute-start | bytes 483848 | tf_op jit(solution)/shard_map/ppermute | solution.py:20
  29.8 8.0 %collective-permute-start.5 = (f32[6,6,44,140]{3,2,1,0:T(8,128)S(1)}, f32[6,6,44,140]{3,2,1,0:T(8,128)S(1)}, u32[]{:S(2)}, u32[]{:S(2)}) collective-permute-start(f32[6,6,44,140]{3,2,1,0:T(8,128)S(1)} %copy.48), channel_id=1, source_target_pairs={{1,0},{3,2},{5,4},{7,6},{9,8},{11,10},{13,12},{15,14},{17,16},{19,... | collective-permute-start | bytes 2661128 | tf_op jit(solution)/shard_map/ppermute | solution.py:20
  35.1 5.6 %collective-permute-start.4 = (f32[6,6,44,140]{3,2,1,0:T(8,128)S(1)}, f32[6,6,44,140]{3,2,1,0:T(8,128)S(1)}, u32[]{:S(2)}, u32[]{:S(2)}) collective-permute-start(f32[6,6,44,140]{3,2,1,0:T(8,128)S(1)} %copy.47), channel_id=1, source_target_pairs={{0,1},{2,3},{4,5},{6,7},{8,9},{10,11},{12,13},{14,15},{16,17},{18,... | collective-permute-start | bytes 2661128 | tf_op jit(solution)/shard_map/ppermute | solution.py:17
  55.9 1.1 %copy-start = (f32[8,32,128]{2,1,0:T(8,128)S(1)}, f32[8,32,128]{2,1,0:T(8,128)}, u32[]{:S(2)}) copy-start(f32[8,32,128]{2,1,0:T(8,128)} %param.8) | copy-start | bytes 393220
  55.9 1.1 %copy-start.1 = (f32[8,32,128]{2,1,0:T(8,128)S(1)}, f32[8,32,128]{2,1,0:T(8,128)}, u32[]{:S(2)}) copy-start(f32[8,32,128]{2,1,0:T(8,128)} %param.12) | copy-start | bytes 393220
  56.8 1.4 %copy-start.4 = (f32[8,32,128]{2,1,0:T(8,128)S(1)}, f32[8,32,128]{2,1,0:T(8,128)}, u32[]{:S(2)}) copy-start(f32[8,32,128]{2,1,0:T(8,128)} %param.14) | copy-start | bytes 393220
  57.3 1.3 %copy-start.2 = (f32[8,32,128]{2,1,0:T(8,128)S(1)}, f32[8,32,128]{2,1,0:T(8,128)}, u32[]{:S(2)}) copy-start(f32[8,32,128]{2,1,0:T(8,128)} %param.10) | copy-start | bytes 393220
  61.5 0.9 %copy-start.3 = (f32[8,32,128]{2,1,0:T(8,128)S(1)}, f32[8,32,128]{2,1,0:T(8,128)}, u32[]{:S(2)}) copy-start(f32[8,32,128]{2,1,0:T(8,128)} %param.15) | copy-start | bytes 393220
where the time goes:
time: 64.7 us; the launch traced here: 63.5 us
  local copies, waits for them, and re-layouts  17 us (26%)
  other arithmetic  16.8 us (26%)
  waiting for transfers between devices  15.9 us (25%)
  starting transfers between devices  12.9 us (20%)
  between operations  0.9 us (1%)
    unnamed x23, local copies, waits for them, and re-layouts  10.1 us
    ppermute x3, waiting for transfers between devices, padded_2(): lax.ppermute(lax.slice_in_dim(block, 0, width, axis=dim), axis, backward)  8.03 us
    ppermute x3, waiting for transfers between devices, padded_2(): lax.ppermute(lax.slice_in_dim(block, block.shape[dim] - width, None, axis...  7.86 us
    mul x6, other arithmetic, operate(): product = face_buoy * grad_adj * grad_fwd  7.43 us
    ppermute x3, starting transfers between devices, padded_2(): lax.ppermute(lax.slice_in_dim(block, 0, width, axis=dim), axis, backward)  7.16 us
    ppermute x3, starting transfers between devices, padded_2(): lax.ppermute(lax.slice_in_dim(block, block.shape[dim] - width, None, axis...  5.76 us
    concatenate x2, other arithmetic, padded_2(): block = jnp.concatenate([low, block, high], axis=dim)  3.46 us
    mul x6, other arithmetic, operate(): term_fwd = diverge(face_buoy * grad_fwd)  1.94 us
  transfers between devices with their start and end apart: 6, of which 6 were waited for; matrix products, arithmetic and copies ran while one was open for 4% of the time, Pallas kernels for 0%

commit v1 on v0

v1 whole, which is shorter than its diff:
```python
import jax
import jax.numpy as jnp
from jax import lax
from jax.experimental import pallas as pl
from jax.experimental.pallas import tpu as pltpu
from jax.sharding import PartitionSpec as P

F32 = jnp.float32
SUB = 8
LAP_SCALE = 1.0 / 1152.0
RHO_SCALE = 1.0 / 2304.0
WIDTHS = (6, 6, 6, 3, 3, 3)
OFFSETS = (0, 6, 12, 21, 24, 27)
SEGMENT = 32
VMEM = pl.BlockSpec(memory_space=pltpu.VMEM)
PARAMS = pltpu.CompilerParams(vmem_limit_bytes=24 * 1024 * 1024)


def iotas(lanes):
    return (
        lax.broadcasted_iota(jnp.int32, (SUB, lanes), 0),
        lax.broadcasted_iota(jnp.int32, (SUB, lanes), 1),
    )


def rolled(x, shift, axis):
    size = x.shape[axis]
    shift = shift % size
    return x if shift == 0 else pltpu.roll(x, shift, axis)


def lane_shift(here, there, by, lane):
    size = here.shape[1]
    if by > 0:
        return rolled(jnp.where(lane < by, there, here), size - by, 1)
    return rolled(jnp.where(lane >= size + by, there, here), -by, 1)


def row_shift(tiles, t, by, sub):
    if by > 0:
        return rolled(jnp.where(sub < by, tiles[(t + 1) % len(tiles)], tiles[t]), SUB - by, 0)
    return rolled(jnp.where(sub >= SUB + by, tiles[t - 1], tiles[t]), -by, 0)


def slope(ahead, here, ahead2, behind):
    return 27.0 * (ahead - here) - (ahead2 - behind)


def pack_three(a, b, c, low, sub):
    if low:
        return jnp.where(sub < 3, a, jnp.where(sub < 6, rolled(b, 3, 0), rolled(c, 6, 0)))
    return jnp.where(sub >= 5, a, jnp.where(sub >= 2, rolled(b, -3, 0), rolled(c, -6, 0)))


def unpack_three(x, low):
    sign = -1 if low else 1
    return x, rolled(x, 3 * sign, 0), rolled(x, 6 * sign, 0)


def edges_kernel(*refs):
    sources, fields, (to_right, to_left, to_core), sems = refs[:6], refs[6:12], refs[12:15], refs[15]
    copies = [pltpu.make_async_copy(x, y, sems.at[k]) for k, (x, y) in enumerate(zip(sources, fields))]
    for copy in copies:
        copy.start()
    for copy in copies:
        copy.wait()
    layers, rows, lanes = fields[0].shape
    _, lane = iotas(lanes)
    core = lax.axis_index("rad")
    per = lanes // SEGMENT
    for group in range(to_right.shape[0]):
        for t in range(rows // SUB):
            at = pl.ds(t * SUB, SUB)
            right = left = None
            for s in range(per):
                layer = group * per + s
                if layer >= layers:
                    break
                for f, (width, offset) in enumerate(zip(WIDTHS, OFFSETS)):
                    first = s * SEGMENT + offset
                    x = rolled(fields[f][layer, at, :], first + width, 1)
                    second = first + width
                    wrap = second + width - lanes
                    mask = lane >= second
                    if wrap > 0:
                        mask = mask | (lane < wrap)
                    right = x if right is None else jnp.where(lane >= first, x, right)
                    left = x if left is None else jnp.where(mask, x, left)
            to_right[group, at, :] = right
            to_left[group, at, :] = left
    at = 0
    for f, width in enumerate(WIDTHS):
        to_core[at : at + width] = fields[f][pl.ds((layers - width) * (1 - core), width)]
        at += width


def halo_kernel(*refs):
    fields = refs[:6]
    from_left, from_right, from_core = refs[6:9]
    halo, to_first, to_second, to_core = refs[9:]
    layers, rows, lanes = fields[0].shape
    tiles = rows // SUB
    sub, lane = iotas(lanes)
    core = lax.axis_index("rad")
    even = lax.axis_index("lat") % 2 == 0
    per = lanes // SEGMENT
    for layer in range(layers):
        group, s = divmod(layer, per)
        for t in range(tiles):
            at = pl.ds(t * SUB, SUB)
            left, right = from_left[group, at, :], from_right[group, at, :]
            for f, (width, offset) in enumerate(zip(WIDTHS, OFFSETS)):
                first = s * SEGMENT + offset
                mask = (lane >= first) & (lane < first + width)
                halo[f, layer, at, :] = rolled(jnp.where(mask, left, right), -first - width, 1)

    def send(k, low, high):
        to_first[k] = jnp.where(even, high, low)
        to_second[k] = jnp.where(even, low, high)

    bottom, top = pl.ds(0, SUB), pl.ds(rows - SUB, SUB)
    for layer in range(layers):
        adj, fwd, buoy, adj2, fwd2, stiff = (x[layer, bottom, :] for x in fields)
        low = (
            adj,
            fwd,
            jnp.where(sub < 5, buoy, rolled(adj2, 5, 0)),
            jnp.where(sub < 3, fwd2, rolled(stiff, 3, 0)),
        )
        adj, fwd, buoy, adj2, fwd2, stiff = (x[layer, top, :] for x in fields)
        high = (
            adj,
            fwd,
            jnp.where(sub >= 3, buoy, rolled(adj2, 3, 0)),
            jnp.where(sub >= 5, fwd2, rolled(stiff, -3, 0)),
        )
        for k in range(4):
            send(4 * layer + k, low[k], high[k])
    for e in range(3):
        low, high = (
            pack_three(*(from_core[6 * f + 3 * core + e, at, :] for f in range(3)), is_low, sub)
            for at, is_low in ((bottom, True), (top, False))
        )
        send(4 * layers + e, low, high)
    both = []
    for at, is_low in ((bottom, True), (top, False)):
        packed = None
        for layer in range(layers):
            x = pack_three(*(halo[f, layer, at, :] for f in range(3)), is_low, sub)
            x = rolled(x, 16 * layer + 6, 1)
            packed = x if packed is None else jnp.where(lane >= 16 * layer, x, packed)
        both.append(packed)
    send(4 * layers + 3, *both)
    for f in range(3):
        to_core[3 * f : 3 * f + 3] = halo[f, pl.ds((layers - 3) * (1 - core), 3)]


def radial(p_at, b_at, layers):
    flux, rho = [], []
    p = [[p_at(f, k) for k in range(-3, layers + 3)] for f in range(2)]
    b = [b_at(k) for k in range(-2, layers + 2)]
    for k in range(layers + 3):
        buoy = b[k] + b[k + 1]
        grads = [slope(x[k + 2], x[k + 1], x[k + 3], x[k]) for x in p]
        flux.append([buoy * g for g in grads])
        rho.append(flux[k][0] * grads[1])
    out = []
    for k in range(layers):
        laps = [slope(flux[k + 2][f], flux[k + 1][f], flux[k + 3][f], flux[k][f]) for f in range(2)]
        out.append((laps[0], laps[1], rho[k + 1] + rho[k + 2]))
    return out


def longitudinal(here, there, lane, want_there, want_rho):
    flux, rho = [], []
    for x, y in ((here, there), (there, here)):
        buoy = x[2] + lane_shift(x[2], y[2], 1, lane)
        grads = [
            slope(
                lane_shift(x[f], y[f], 1, lane),
                x[f],
                lane_shift(x[f], y[f], 2, lane),
                lane_shift(x[f], y[f], -1, lane),
            )
            for f in range(2)
        ]
        flux.append([buoy * g for g in grads])
        rho.append(flux[-1][0] * grads[1])
    laps = []
    for x, y in ((0, 1), (1, 0))[: 2 if want_there else 1]:
        laps.append(
            [
                slope(
                    flux[x][f],
                    lane_shift(flux[x][f], flux[y][f], -1, lane),
                    lane_shift(flux[x][f], flux[y][f], 1, lane),
                    lane_shift(flux[x][f], flux[y][f], -2, lane),
                )
                for f in range(2)
            ]
        )
    density = rho[0] + lane_shift(rho[0], rho[1], -1, lane) if want_rho else None
    return laps, density


def latitudinal(adj, fwd, buoy, sub, wanted, want_rho):
    count = len(adj)
    flux, rho = ([], []), []
    for t in range(count):
        face = buoy[t] + row_shift(buoy, t, 1, sub)
        grads = [
            slope(row_shift(x, t, 1, sub), x[t], row_shift(x, t, 2, sub), row_shift(x, t, -1, sub))
            for x in (adj, fwd)
        ]
        for f in range(2):
            flux[f].append(face * grads[f])
        rho.append(flux[0][t] * grads[1])
    out = []
    for t in range(wanted):
        laps = [
            slope(x[t], row_shift(x, t, -1, sub), row_shift(x, t, 1, sub), row_shift(x, t, -2, sub))
            for x in flux
        ]
        out.append((laps[0], laps[1], rho[t] + row_shift(rho, t, -1, sub) if want_rho else None))
    return out


def steps_kernel(*refs):
    fields, (bulk_in, density_in) = refs[:6], refs[6:8]
    halo, from_core, from_core2, from_first, from_second = refs[8:13]
    adj_out, adj_out2, fwd_out, fwd_out2, bulk, density = refs[13:19]
    wide, wide_halo, first, first_halo, part, part_halo = refs[19:]
    layers, rows, lanes = fields[0].shape
    tiles = rows // SUB
    sub, lane = iotas(lanes)
    core = lax.axis_index("rad")
    even = lax.axis_index("lat") % 2 == 0
    ahead, behind = tiles, tiles + 1
    zero = jnp.zeros((SUB, lanes), F32)

    def at(t):
        return pl.ds(t * SUB, SUB)

    near = (layers + 6) * (1 - core) + 3 * core
    for f in range(3):
        for layer in range(layers):
            for t in range(tiles):
                wide[f, layer + 6, t] = fields[f][layer, at(t), :]
                wide_halo[f, layer + 3, t] = halo[f, layer, at(t), :]
        for k in range(6):
            for t in range(tiles):
                wide[f, (layers + 6) * (1 - core) + k, t] = from_core[6 * f + k, at(t), :]
        for k in range(3):
            for t in range(tiles):
                wide_halo[f, (layers + 3) * (1 - core) + k, t] = from_core2[3 * f + k, at(t), :]
                wide_halo[f, (layers + 3) * core + k, t] = zero
            for t in range(tiles + 2):
                wide[f, 3 + (layers + 3) * core + k, t] = zero
            for t in range(tiles):
                for g in range(2):
                    first[g, (layers + 3) * core + k, t] = zero

    def received(k):
        one, two = from_first[k], from_second[k]
        return jnp.where(even, one, two), jnp.where(even, two, one)

    for e in range(3):
        low, high = received(4 * layers + e)
        for f, (x, y) in enumerate(zip(unpack_three(low, True), unpack_three(high, False))):
            wide[f, near + e, ahead] = x
            wide[f, near + e, behind] = y
    low, high = received(4 * layers + 3)
    for layer in range(layers):
        x, y = (rolled(z, -6 - 16 * layer, 1) for z in (low, high))
        for f, (u, v) in enumerate(zip(unpack_three(x, True), unpack_three(y, False))):
            wide_halo[f, layer + 3, ahead] = u
            wide_halo[f, layer + 3, behind] = v
        for f in range(3):
            low2, high2 = received(4 * layer + f)
            wide[f, layer + 6, ahead] = low2
            wide[f, layer + 6, behind] = high2

    start = 6 - 3 * core
    for t in range(tiles):
        terms = radial(
            lambda f, k: wide[f, start + k, t], lambda k: wide[2, start + k, t], layers + 3
        )
        for k, term in enumerate(terms):
            for g in range(3):
                part[g, start - 3 + k, t] = term[g]
        terms = radial(
            lambda f, k: wide_halo[f, 3 + k, t], lambda k: wide_halo[2, 3 + k, t], layers
        )
        for k, term in enumerate(terms):
            for g in range(2):
                part_halo[g, k, t] = term[g]
    for t in (ahead, behind):
        terms = radial(lambda f, k: wide[f, 6 + k, t], lambda k: wide[2, 6 + k, t], layers)
        for k, term in enumerate(terms):
            for g in range(2):
                part[g, 3 + k, t] = term[g]

    def own(layer, carry):
        here = [[wide[f, layer + 6, t] for t in range(tiles + 2)] for f in range(3)]
        there = [[wide_halo[f, layer + 3, t] for t in range(tiles + 2)] for f in range(3)]
        lat = latitudinal(*here, sub, tiles + 2, True)
        lat_halo = latitudinal(*there, sub, tiles, False)
        low, high = received(4 * layer + 2)
        low3, high3 = received(4 * layer + 3)
        before = (
            (rolled(low, -5, 0), low3, rolled(low3, -3, 0)),
            (rolled(high, 5, 0), high3, rolled(high3, 3, 0)),
        )
        for t in range(tiles + 2):
            inside = t < tiles
            laps, rho = longitudinal(
                [x[t] for x in here], [x[t] for x in there], lane, inside, inside
            )
            if inside:
                adj2, fwd2, stiff = (fields[f][layer, at(t), :] for f in range(3, 6))
            else:
                adj2, fwd2, stiff = before[t - tiles]
            stiff = stiff * LAP_SCALE
            update = []
            for g, past in enumerate((adj2, fwd2)):
                update.append(stiff * (part[g, layer + 3, t] + lat[t][g] + laps[0][g]))
                first[g, layer + 3, t] = 2.0 * here[g][t] - past + update[g]
            if inside:
                bulk[layer, at(t), :] = bulk_in[layer, at(t), :] + here[0][t] * update[1]
                density[layer, at(t), :] = density_in[layer, at(t), :] + RHO_SCALE * (
                    part[2, layer + 3, t] + lat[t][2] + rho
                )
                stiff = halo[5, layer, at(t), :] * LAP_SCALE
                for g in range(2):
                    first_halo[g, layer, t] = (
                        2.0 * there[g][t]
                        - halo[3 + g, layer, at(t), :]
                        + stiff * (part_halo[g, layer, t] + lat_halo[t][g] + laps[1][g])
                    )
        return carry

    lax.fori_loop(0, layers, own, 0)

    def other(e, carry):
        here = [[wide[f, near + e, t] for t in range(tiles + 2)] for f in range(3)]
        lat = latitudinal(*here, sub, tiles, False)
        for t in range(tiles):
            there = [wide_halo[f, (layers + 3) * (1 - core) + e, t] for f in range(3)]
            laps, _ = longitudinal([x[t] for x in here], there, lane, False, False)
            stiff = from_core[24 + e, at(t), :] * LAP_SCALE
            for g in range(2):
                first[g, near - 3 + e, t] = (
                    2.0 * here[g][t]
                    - from_core[18 + 3 * g + e, at(t), :]
                    + stiff * (part[g, near - 3 + e, t] + lat[t][g] + laps[0][g])
                )
        return carry

    lax.fori_loop(0, 3, other, 0)

    for t in range(tiles):
        terms = radial(lambda f, k: first[f, 3 + k, t], lambda k: wide[2, 6 + k, t], layers)
        for k, term in enumerate(terms):
            for g in range(3):
                part[g, 3 + k, t] = term[g]

    def last(layer, carry):
        here = [[first[f, layer + 3, t] for t in range(tiles + 2)] for f in range(2)]
        here.append([wide[2, layer + 6, t] for t in range(tiles + 2)])
        lat = latitudinal(*here, sub, tiles, True)
        for t in range(tiles):
            there = [first_halo[0, layer, t], first_halo[1, layer, t], wide_halo[2, layer + 3, t]]
            laps, rho = longitudinal([x[t] for x in here], there, lane, False, True)
            stiff = fields[5][layer, at(t), :] * LAP_SCALE
            update = [stiff * (part[g, layer + 3, t] + lat[t][g] + laps[0][g]) for g in range(2)]
            for g, (now, before) in enumerate(((adj_out, adj_out2), (fwd_out, fwd_out2))):
                before[layer, at(t), :] = here[g][t]
                now[layer, at(t), :] = 2.0 * here[g][t] - fields[g][layer, at(t), :] + update[g]
            bulk[layer, at(t), :] += here[0][t] * update[1]
            density[layer, at(t), :] += RHO_SCALE * (part[2, layer + 3, t] + lat[t][2] + rho)
        return carry

    lax.fori_loop(0, layers, last, 0)


def pairs(count, start):
    firsts = range(start, count - 1, 2)
    return [p for i in firsts for p in ((i, i + 1), (i + 1, i))]


def shards(
    adj_now, adj_next, fwd_now, fwd_next, stiffness, buoyancy, kernel_bulk_in, kernel_density_in
):
    layers, rows, lanes = adj_now.shape
    tiles = rows // SUB
    fields = (adj_now, fwd_now, buoyancy, adj_next, fwd_next, stiffness)
    groups = -(-layers // (lanes // SEGMENT))
    edge = pltpu.VMEM((groups, rows, lanes), F32)
    *fields, to_right, to_left, to_core = pl.pallas_call(
        edges_kernel,
        out_shape=(pltpu.VMEM((layers, rows, lanes), F32),) * 6
        + (edge, edge, pltpu.VMEM((sum(WIDTHS), rows, lanes), F32)),
        in_specs=[pl.BlockSpec(memory_space=pltpu.HBM)] * 6,
        out_specs=(VMEM,) * 9,
        scratch_shapes=[pltpu.SemaphoreType.DMA((6,))],
        compiler_params=PARAMS,
    )(*(pltpu.with_memory_space_constraint(x, pltpu.HBM) for x in fields))
    around = lax.axis_size("lon")
    ring = [(i, (i + 1) % around) for i in range(around)]
    swap = [(0, 1), (1, 0)]
    from_left = lax.ppermute(to_right, "lon", ring)
    from_right = lax.ppermute(to_left, "lon", [(b, a) for a, b in ring])
    from_core = lax.ppermute(to_core, "rad", swap)
    lat_edge = pltpu.VMEM((4 * layers + 4, SUB, lanes), F32)
    halo, to_first, to_second, to_core = pl.pallas_call(
        halo_kernel,
        out_shape=(
            pltpu.VMEM((6, layers, rows, lanes), F32),
            lat_edge,
            lat_edge,
            pltpu.VMEM((9, rows, lanes), F32),
        ),
        in_specs=[VMEM] * 9,
        out_specs=(VMEM,) * 4,
        compiler_params=PARAMS,
    )(*fields, from_left, from_right, from_core)
    count = lax.axis_size("lat")
    from_first = lax.ppermute(to_first, "lat", pairs(count, 0))
    from_second = lax.ppermute(to_second, "lat", pairs(count, 1))
    from_core2 = lax.ppermute(to_core, "rad", swap)
    block = jax.ShapeDtypeStruct((layers, rows, lanes), F32)
    return pl.pallas_call(
        steps_kernel,
        out_shape=(block,) * 6,
        in_specs=[VMEM] * 13,
        out_specs=(VMEM,) * 6,
        scratch_shapes=[
            pltpu.VMEM((3, layers + 12, tiles + 2, SUB, lanes), F32),
            pltpu.VMEM((3, layers + 6, tiles + 2, SUB, lanes), F32),
            pltpu.VMEM((2, layers + 6, tiles + 2, SUB, lanes), F32),
            pltpu.VMEM((2, layers, tiles, SUB, lanes), F32),
            pltpu.VMEM((3, layers + 6, tiles + 2, SUB, lanes), F32),
            pltpu.VMEM((2, layers, tiles, SUB, lanes), F32),
        ],
        compiler_params=PARAMS,
    )(
        *fields,
        kernel_bulk_in,
        kernel_density_in,
        halo,
        from_core,
        from_core2,
        from_first,
        from_second,
    )


def solution(mesh):
    spec = P("rad", "lat", "lon")
    return jax.shard_map(
        shards, mesh=mesh, in_specs=(spec,) * 8, out_specs=(spec,) * 6, check_vma=False
    )
```

time: 64.7 us -> 25.1 us (0.39); the launches traced: 63.5 us -> 24.6 us
  local copies, waits for them, and re-layouts: 17 us -> 0.01 us
  other arithmetic: 16.8 us -> 0 us
  waiting for transfers between devices: 15.9 us -> 7.34 us
  Pallas kernels: 0 us -> 8.3 us
  starting transfers between devices: 12.9 us -> 8.27 us
    unnamed x23 -> x4, local copies, waits for them, and re-layouts: 10.1 us -> 0.01 us
    mul x12 -> x0, other arithmetic: 9.38 us -> none  [the longest x6 7.43 us: operate(): product = face_buoy * grad_adj * grad_fwd]
    ppermute x6, waiting for transfers between devices: 15.9 us -> 7.34 us  [the longest x1 3.02 us: shards(): from_second = lax.ppermute(to_second, 'lat', pairs(count, 1))]
    pallas_call x0 -> x3, Pallas kernels: none -> 8.3 us  [the longest x1 6.44 us: shards(): pl.pallas_call(steps_kernel, out_shape=(block,) * 6, in_specs=[VMEM] * 13...]
    ppermute x6, starting transfers between devices: 12.9 us -> 8.27 us  [the longest x1 4.32 us: shards(): from_second = lax.ppermute(to_second, 'lat', pairs(count, 1))]
    concatenate x2 -> x0, other arithmetic: 3.46 us -> none  [padded_2(): block = jnp.concatenate([low, block, high], axis=dim)]
    ppermute x4 -> x0, local copies, waits for them, and re-layouts: 2.67 us -> none  [the longest x2 1.34 us: padded_2(): lax.ppermute(lax.slice_in_dim(block, block.shape[dim] - width, None, axis...]
    slice x6 -> x0, local copies, waits for them, and re-layouts: 2.61 us -> none  [the longest x3 1.19 us: padded_2(): lax.slice_in_dim(block, block.shape[dim] - width, None, axis=dim)]
  transfers between devices with their start and end apart: 6 -> 6, of which waited for: 6 -> 4; matrix products, arithmetic and copies ran while one was open for 4% -> 0% of each run, Pallas kernels for 0% -> 0%
where the time goes in v1:
time: 25.1 us; the launch traced here: 24.6 us
  Pallas kernels  8.3 us (33%)
  starting transfers between devices  8.27 us (33%)
  waiting for transfers between devices  7.34 us (29%)
  between operations  0.67 us (3%)
    pallas_call x1, Pallas kernels, shards(): pl.pallas_call(steps_kernel, out_shape=(block,) * 6, in_specs=[VMEM] * 13...  6.44 us
    ppermute x1, starting transfers between devices, shards(): from_second = lax.ppermute(to_second, 'lat', pairs(count, 1))  4.32 us
    ppermute x1, waiting for transfers between devices, shards(): from_second = lax.ppermute(to_second, 'lat', pairs(count, 1))  3.02 us
    ppermute x1, waiting for transfers between devices, shards(): from_right = lax.ppermute(to_left, 'lon', [(b, a) for a, b in ring])  2.11 us
    ppermute x1, starting transfers between devices, shards(): from_core2 = lax.ppermute(to_core, 'rad', swap)  1.56 us
    pallas_call x1, Pallas kernels, shards(): pl.pallas_call(edges_kernel, out_shape=(pltpu.VMEM((layers, rows, lanes),...  1.54 us
    ppermute x1, waiting for transfers between devices, shards(): from_left = lax.ppermute(to_right, 'lon', ring)  1.3 us
    ppermute x1, starting transfers between devices, shards(): from_left = lax.ppermute(to_right, 'lon', ring)  1.21 us
  transfers between devices with their start and end apart: 6, of which 4 were waited for; matrix products, arithmetic and copies ran while one was open for 0% of the time, Pallas kernels for 0%

profile of v1, /device:TPU:11, one launch (start us, length us, event | category | flops | bytes accessed | tf_op | source)
XLA Modules:
  0.0 24.6 jit_solution(2004984358109429933)
XLA Ops:
  0.6 1.5 %shard_map.127 = (f32[8,32,128]{2,1,0:T(8,128)S(1)}, f32[8,32,128]{2,1,0:T(8,128)S(1)}, f32[8,32,128]{2,1,0:T(8,128)S(1)}, f32[8,32,128]{2,1,0:T(8,128)S(1)}, f3...) custom-call(f32[8,32,128]{2,1,0:T(8,128)} %refs_0_.1, ...), custom_call_target="tpu_custom_call" | custom-call | tf_op jit(solution)/shard_map/pallas_call | solution.py:399
  2.2 0.7 %collective-permute-start.2 = (f32[27,32,128]{2,1,0:T(8,128)S(1)}, f32[27,32,128]{2,1,0:T(8,128)S(1)}, u32[]{:S(2)}, u32[]{:S(2)}) collective-permute-start(f32[27,32,128]{2,1,0:T(8,128)S(1)} %get-tuple-element.27), channel_id=1, source_target_pairs={{0,1},{1,0},{2,3},{3,2},{4,5},{5,4},{6,7},{7,6},{8,9},{9,8},{10,11... | collective-permute-start | bytes 1327112 | tf_op jit(solution)/shard_map/ppermute | solution.py:413
  2.9 1.2 %collective-permute-start = (f32[2,32,128]{2,1,0:T(8,128)S(1)}, f32[2,32,128]{2,1,0:T(8,128)S(1)}, u32[]{:S(2)}, u32[]{:S(2)}) collective-permute-start(f32[2,32,128]{2,1,0:T(8,128)S(1)} %get-tuple-element.25), channel_id=1, source_target_pairs={{0,8},{8,16},{16,24},{24,0},{1,9},{9,17},{17,25},{25,1},{2,10},{10... | collective-permute-start | bytes 98312 | tf_op jit(solution)/shard_map/ppermute | solution.py:411
  4.1 0.3 %collective-permute-start.1 = (f32[2,32,128]{2,1,0:T(8,128)S(1)}, f32[2,32,128]{2,1,0:T(8,128)S(1)}, u32[]{:S(2)}, u32[]{:S(2)}) collective-permute-start(f32[2,32,128]{2,1,0:T(8,128)S(1)} %get-tuple-element.26), channel_id=1, source_target_pairs={{8,0},{16,8},{24,16},{0,24},{9,1},{17,9},{25,17},{1,25},{10,2},{18... | collective-permute-start | bytes 98312 | tf_op jit(solution)/shard_map/ppermute | solution.py:412
  4.4 1.3 %collective-permute-done.refs_6_ = f32[2,32,128]{2,1,0:T(8,128)S(1)} collective-permute-done((f32[2,32,128]{2,1,0:T(8,128)S(1)}, f32[2,32,128]{2,1,0:T(8,128)S(1)}, u32[]{:S(2)}, u32[]{:S(2)}) %collective-permute-start) | collective-permute-done | bytes 32800 | tf_op jit(solution)/shard_map/ppermute | solution.py:411
  5.7 2.1 %collective-permute-done.1.refs_7_ = f32[2,32,128]{2,1,0:T(8,128)S(1)} collective-permute-done((f32[2,32,128]{2,1,0:T(8,128)S(1)}, f32[2,32,128]{2,1,0:T(8,128)S(1)}, u32[]{:S(2)}, u32[]{:S(2)}) %collective-permute-start.1) | collective-permute-done | bytes 32800 | tf_op jit(solution)/shard_map/ppermute | solution.py:412
  7.8 0.0 collective-permute-done.2.refs_8_.refs_9_
  7.8 0.0 copy-start
  7.8 0.0 copy-start.1
  7.8 0.3 %shard_map.128 = (f32[6,8,32,128]{3,2,1,0:T(8,128)S(1)}, f32[36,8,128]{2,1,0:T(8,128)S(1)}, f32[36,8,128]{2,1,0:T(8,128)S(1)}, f32[9,32,128]{2,1,0:T(8,128)S(1)}) custom-call(f32[8,32,128]{2,1,0:T(8,128)S(1)} %get-tuple-element.19.refs_0_, f32[8,32,128]{2,1,0:T(8,128)S(1)} %get-tuple-element.20.refs_1_, f32[8,32,128]{2,1,0:T(8,128)S(1)} %get-tuple-element.21.refs_2_, ...), custom_call_target="tpu_custom_call" | custom-call | tf_op jit(solution)/shard_map/pallas_call | solution.py:415
  8.1 1.6 %collective-permute-start.3 = (f32[9,32,128]{2,1,0:T(8,128)S(1)}, f32[9,32,128]{2,1,0:T(8,128)S(1)}, u32[]{:S(2)}, u32[]{:S(2)}) collective-permute-start(f32[9,32,128]{2,1,0:T(8,128)S(1)} %get-tuple-element.29), channel_id=1, source_target_pairs={{0,1},{1,0},{2,3},{3,2},{4,5},{5,4},{6,7},{7,6},{8,9},{9,8},{10,11... | collective-permute-start | bytes 442376 | tf_op jit(solution)/shard_map/ppermute | solution.py:430
  9.7 0.2 collective-permute-start.4
  9.9 4.3 %collective-permute-start.5 = (f32[36,8,128]{2,1,0:T(8,128)S(1)}, f32[36,8,128]{2,1,0:T(8,128)S(1)}, u32[]{:S(2)}, u32[]{:S(2)}) collective-permute-start(f32[36,8,128]{2,1,0:T(8,128)S(1)} %get-tuple-element.31), channel_id=1, source_target_pairs={{2,4},{4,2},{3,5},{5,3},{10,12},{12,10},{11,13},{13,11},{18,20},{2... | collective-permute-start | bytes 442376 | tf_op jit(solution)/shard_map/ppermute | solution.py:429
  14.2 0.0 collective-permute-done.3.refs_10_
  14.2 0.9 %collective-permute-done.4.refs_11_ = f32[36,8,128]{2,1,0:T(8,128)S(1)} collective-permute-done((f32[36,8,128]{2,1,0:T(8,128)S(1)}, f32[36,8,128]{2,1,0:T(8,128)S(1)}, u32[]{:S(2)}, u32[]{:S(2)}) %collective-permute-start.4) | collective-permute-done | bytes 147488 | tf_op jit(solution)/shard_map/ppermute | solution.py:428
  15.1 3.0 %collective-permute-done.5.refs_12_ = f32[36,8,128]{2,1,0:T(8,128)S(1)} collective-permute-done((f32[36,8,128]{2,1,0:T(8,128)S(1)}, f32[36,8,128]{2,1,0:T(8,128)S(1)}, u32[]{:S(2)}, u32[]{:S(2)}) %collective-permute-start.5) | collective-permute-done | bytes 147488 | tf_op jit(solution)/shard_map/ppermute | solution.py:429
  18.1 0.0 copy-done
  18.2 0.0 copy-done.1
  18.2 6.4 %shard_map.129 = (f32[8,32,128]{2,1,0:T(8,128)}, f32[8,32,128]{2,1,0:T(8,128)}, f32[8,32,128]{2,1,0:T(8,128)}, f32[8,32,128]{2,1,0:T(8,128)}, f32[8,32,128]{2,1,0:T(8,128)}, /*index=5*/f32[8,32,128]{2,1,0:T(8,128)}) custom-call(f32[8,32,128]{2,1,0:T(8,128)S(1)} %get-tuple-element.19.refs_0_, f32[8,32,128]{2,1,0:T(8,128)S(1)} %get-tuple-element.20.refs_1_, ...), custom_call_target="tpu_custom_call" | custom-call | tf_op jit(solution)/shard_map/pallas_call | solution.py:432
Async XLA Ops:
  2.2 5.6 %collective-permute-start.2 = (f32[27,32,128]{2,1,0:T(8,128)S(1)}, f32[27,32,128]{2,1,0:T(8,128)S(1)}, u32[]{:S(2)}, u32[]{:S(2)}) collective-permute-start(f32[27,32,128]{2,1,0:T(8,128)S(1)} %get-tuple-element.27), channel_id=1, source_target_pairs={{0,1},{1,0},{2,3},{3,2},{4,5},{5,4},{6,7},{7,6},{8,9},{9,8},{10,11... | collective-permute-start | bytes 1327112 | tf_op jit(solution)/shard_map/ppermute | solution.py:413
  2.9 2.8 %collective-permute-start = (f32[2,32,128]{2,1,0:T(8,128)S(1)}, f32[2,32,128]{2,1,0:T(8,128)S(1)}, u32[]{:S(2)}, u32[]{:S(2)}) collective-permute-start(f32[2,32,128]{2,1,0:T(8,128)S(1)} %get-tuple-element.25), channel_id=1, source_target_pairs={{0,8},{8,16},{16,24},{24,0},{1,9},{9,17},{17,25},{25,1},{2,10},{10... | collective-permute-start | bytes 98312 | tf_op jit(solution)/shard_map/ppermute | solution.py:411
  4.1 3.7 %collective-permute-start.1 = (f32[2,32,128]{2,1,0:T(8,128)S(1)}, f32[2,32,128]{2,1,0:T(8,128)S(1)}, u32[]{:S(2)}, u32[]{:S(2)}) collective-permute-start(f32[2,32,128]{2,1,0:T(8,128)S(1)} %get-tuple-element.26), channel_id=1, source_target_pairs={{8,0},{16,8},{24,16},{0,24},{9,1},{17,9},{25,17},{1,25},{10,2},{18... | collective-permute-start | bytes 98312 | tf_op jit(solution)/shard_map/ppermute | solution.py:412
  7.8 10.3 %copy-start = (f32[8,32,128]{2,1,0:T(8,128)S(1)}, f32[8,32,128]{2,1,0:T(8,128)}, u32[]{:S(2)}) copy-start(f32[8,32,128]{2,1,0:T(8,128)} %refs_6_.1) | copy-start | bytes 393220
  7.8 10.3 %copy-start.1 = (f32[8,32,128]{2,1,0:T(8,128)S(1)}, f32[8,32,128]{2,1,0:T(8,128)}, u32[]{:S(2)}) copy-start(f32[8,32,128]{2,1,0:T(8,128)} %refs_7_.1) | copy-start | bytes 393220
  8.1 6.1 %collective-permute-start.3 = (f32[9,32,128]{2,1,0:T(8,128)S(1)}, f32[9,32,128]{2,1,0:T(8,128)S(1)}, u32[]{:S(2)}, u32[]{:S(2)}) collective-permute-start(f32[9,32,128]{2,1,0:T(8,128)S(1)} %get-tuple-element.29), channel_id=1, source_target_pairs={{0,1},{1,0},{2,3},{3,2},{4,5},{5,4},{6,7},{7,6},{8,9},{9,8},{10,11... | collective-permute-start | bytes 442376 | tf_op jit(solution)/shard_map/ppermute | solution.py:430
  9.7 5.4 %collective-permute-start.4 = (f32[36,8,128]{2,1,0:T(8,128)S(1)}, f32[36,8,128]{2,1,0:T(8,128)S(1)}, u32[]{:S(2)}, u32[]{:S(2)}) collective-permute-start(f32[36,8,128]{2,1,0:T(8,128)S(1)} %get-tuple-element.30), channel_id=1, source_target_pairs={{0,2},{2,0},{4,6},{6,4},{1,3},{3,1},{5,7},{7,5},{8,10},{10,8},{12,... | collective-permute-start | bytes 442376 | tf_op jit(solution)/shard_map/ppermute | solution.py:428
  9.9 8.3 %collective-permute-start.5 = (f32[36,8,128]{2,1,0:T(8,128)S(1)}, f32[36,8,128]{2,1,0:T(8,128)S(1)}, u32[]{:S(2)}, u32[]{:S(2)}) collective-permute-start(f32[36,8,128]{2,1,0:T(8,128)S(1)} %get-tuple-element.31), channel_id=1, source_target_pairs={{2,4},{4,2},{3,5},{5,3},{10,12},{12,10},{11,13},{13,11},{18,20},{2... | collective-permute-start | bytes 442376 | tf_op jit(solution)/shard_map/ppermute | solution.py:429

commit v2 on v1

v2 whole, which is shorter than its diff:
```python
import jax
import jax.numpy as jnp
from jax import lax
from jax.experimental import pallas as pl
from jax.experimental.pallas import tpu as pltpu
from jax.sharding import PartitionSpec as P

F32 = jnp.float32
SUB = 8
LAP_SCALE = 1.0 / 1152.0
RHO_SCALE = 1.0 / 2304.0
WIDTHS = (6, 6, 6, 3, 3, 3)
OFFSETS = (0, 6, 12, 21, 24, 27)
SEGMENT = 32
VMEM = pl.BlockSpec(memory_space=pltpu.VMEM)
PARAMS = pltpu.CompilerParams(vmem_limit_bytes=24 * 1024 * 1024)
HEAVY = pl.CostEstimate(flops=4000000000, bytes_accessed=1000000, transcendentals=0)


def iotas(lanes):
    return (
        lax.broadcasted_iota(jnp.int32, (SUB, lanes), 0),
        lax.broadcasted_iota(jnp.int32, (SUB, lanes), 1),
    )


def rolled(x, shift, axis):
    size = x.shape[axis]
    shift = shift % size
    return x if shift == 0 else pltpu.roll(x, shift, axis)


def lane_shift(here, there, by, lane):
    size = here.shape[1]
    if by > 0:
        return rolled(jnp.where(lane < by, there, here), size - by, 1)
    return rolled(jnp.where(lane >= size + by, there, here), -by, 1)


def row_shift(tiles, t, by, sub):
    if by > 0:
        return rolled(jnp.where(sub < by, tiles[(t + 1) % len(tiles)], tiles[t]), SUB - by, 0)
    return rolled(jnp.where(sub >= SUB + by, tiles[t - 1], tiles[t]), -by, 0)


def slope(ahead, here, ahead2, behind):
    return 27.0 * (ahead - here) - (ahead2 - behind)


def pack_three(a, b, c, low, sub):
    if low:
        return jnp.where(sub < 3, a, jnp.where(sub < 6, rolled(b, 3, 0), rolled(c, 6, 0)))
    return jnp.where(sub >= 5, a, jnp.where(sub >= 2, rolled(b, -3, 0), rolled(c, -6, 0)))


def unpack_three(x, low):
    sign = -1 if low else 1
    return x, rolled(x, 3 * sign, 0), rolled(x, 6 * sign, 0)


def edges_kernel(*refs):
    sources, fields, (to_right, to_left, to_core), sems = refs[:6], refs[6:12], refs[12:15], refs[15]
    copies = [pltpu.make_async_copy(x, y, sems.at[k]) for k, (x, y) in enumerate(zip(sources, fields))]
    for copy in copies:
        copy.start()
    for copy in copies:
        copy.wait()
    layers, rows, lanes = fields[0].shape
    _, lane = iotas(lanes)
    core = lax.axis_index("rad")
    per = lanes // SEGMENT
    for group in range(to_right.shape[0]):
        for t in range(rows // SUB):
            at = pl.ds(t * SUB, SUB)
            right = left = None
            for s in range(per):
                layer = group * per + s
                if layer >= layers:
                    break
                for f, (width, offset) in enumerate(zip(WIDTHS, OFFSETS)):
                    first = s * SEGMENT + offset
                    x = rolled(fields[f][layer, at, :], first + width, 1)
                    second = first + width
                    wrap = second + width - lanes
                    mask = lane >= second
                    if wrap > 0:
                        mask = mask | (lane < wrap)
                    right = x if right is None else jnp.where(lane >= first, x, right)
                    left = x if left is None else jnp.where(mask, x, left)
            to_right[group, at, :] = right
            to_left[group, at, :] = left
    at = 0
    for f, width in enumerate(WIDTHS):
        to_core[at : at + width] = fields[f][pl.ds((layers - width) * (1 - core), width)]
        at += width


def radial(p_at, b_at, layers):
    flux, rho = [], []
    p = [[p_at(f, k) for k in range(-3, layers + 3)] for f in range(2)]
    b = [b_at(k) for k in range(-2, layers + 2)]
    for k in range(layers + 3):
        buoy = b[k] + b[k + 1]
        grads = [slope(x[k + 2], x[k + 1], x[k + 3], x[k]) for x in p]
        flux.append([buoy * g for g in grads])
        rho.append(flux[k][0] * grads[1])
    out = []
    for k in range(layers):
        laps = [slope(flux[k + 2][f], flux[k + 1][f], flux[k + 3][f], flux[k][f]) for f in range(2)]
        out.append((laps[0], laps[1], rho[k + 1] + rho[k + 2]))
    return out


def longitudinal(here, there, lane, want_there, want_rho):
    flux, rho = [], []
    for x, y in ((here, there), (there, here)):
        buoy = x[2] + lane_shift(x[2], y[2], 1, lane)
        grads = [
            slope(
                lane_shift(x[f], y[f], 1, lane),
                x[f],
                lane_shift(x[f], y[f], 2, lane),
                lane_shift(x[f], y[f], -1, lane),
            )
            for f in range(2)
        ]
        flux.append([buoy * g for g in grads])
        rho.append(flux[-1][0] * grads[1])
    laps = []
    for x, y in ((0, 1), (1, 0))[: 2 if want_there else 1]:
        laps.append(
            [
                slope(
                    flux[x][f],
                    lane_shift(flux[x][f], flux[y][f], -1, lane),
                    lane_shift(flux[x][f], flux[y][f], 1, lane),
                    lane_shift(flux[x][f], flux[y][f], -2, lane),
                )
                for f in range(2)
            ]
        )
    density = rho[0] + lane_shift(rho[0], rho[1], -1, lane) if want_rho else None
    return laps, density


def unpacked(left, right, f, s, lane):
    width, offset = WIDTHS[f], OFFSETS[f]
    first = s * SEGMENT + offset
    mask = (lane >= first) & (lane < first + width)
    return rolled(jnp.where(mask, left, right), -first - width, 1)


def lat_flux(ring, t, sub):
    adj, fwd, buoy = ring
    face = buoy[t] + row_shift(buoy, t, 1, sub)
    grads = [
        slope(row_shift(x, t, 1, sub), x[t], row_shift(x, t, 2, sub), row_shift(x, t, -1, sub))
        for x in (adj, fwd)
    ]
    flux = [face * g for g in grads]
    return flux[0], flux[1], flux[0] * grads[1]


def lat_terms(flux, t, sub, want_rho):
    adj, fwd, rho = ([x[k] for x in flux] for k in range(3))
    laps = [
        slope(x[t], row_shift(x, t, -1, sub), row_shift(x, t, 1, sub), row_shift(x, t, -2, sub))
        for x in (adj, fwd)
    ]
    return laps[0], laps[1], rho[t] + row_shift(rho, t, -1, sub) if want_rho else None


def lat_inner(ring, sub, want_rho):
    count = len(ring[0])
    flux = [list(lat_flux(ring, t, sub)) for t in range(count)]
    zero = jnp.zeros_like(ring[0][0])
    for k in range(3):
        flux[0][k] = jnp.where(sub >= 1, flux[0][k], zero)
        flux[-1][k] = jnp.where(sub < SUB - 2, flux[-1][k], zero)
    flux.append([zero] * 3)
    return [lat_terms(flux, t, sub, want_rho) for t in range(count)]


def lat_outer(adj, fwd, buoy, sub):
    ring = ([adj], [fwd], [buoy])
    mask = (sub >= SUB - 2) | (sub < 1)
    flux = [[jnp.where(mask, x, 0.0) for x in lat_flux(ring, 0, sub)]]
    return lat_terms(flux, 0, sub, True)


def places(core, layers):
    return (layers + 3) * (1 - core), (layers + 3) * core


def inner_kernel(*refs):
    fields, from_core = refs[:6], refs[6]
    wide, part, to_first, to_second = refs[7:]
    layers, rows, lanes = fields[0].shape
    tiles = rows // SUB
    sub, lane = iotas(lanes)
    core = lax.axis_index("rad")
    even = lax.axis_index("lat") % 2 == 0
    near, border = places(core, layers)
    zero = jnp.zeros((SUB, lanes), F32)

    def at(t):
        return pl.ds(t * SUB, SUB)

    for f in range(3):
        for t in range(tiles):
            for layer in range(layers):
                wide[f, layer + 6, t] = fields[f][layer, at(t), :]
            for k in range(6):
                wide[f, (layers + 6) * (1 - core) + k, t] = from_core[6 * f + k, at(t), :]
            for k in range(3):
                wide[f, border + 3 + k, t] = zero

    def send(k, low, high):
        to_first[k] = jnp.where(even, high, low)
        to_second[k] = jnp.where(even, low, high)

    ends = ((0, True), (tiles - 1, False))
    third = [None, None]
    for layer in range(layers):
        send(
            layers + layer,
            *(pack_three(*(x[layer, at(t), :] for x in fields[:3]), low, sub) for t, low in ends),
        )
        for k, row in enumerate((2, SUB - 3)):
            x = rolled(fields[5][layer, at(ends[k][0]), :], layer - row, 0)
            third[k] = x if layer == 0 else jnp.where(sub == layer, x, third[k])
    send(2 * layers, *third)
    for e in range(3):
        send(
            2 * layers + 1 + e,
            *(pack_three(*(wide[f, near + 3 + e, t] for f in range(3)), low, sub) for t, low in ends),
        )

    start = 6 - 3 * core
    for t in range(tiles):
        terms = radial(
            lambda f, k: wide[f, start + k, t], lambda k: wide[2, start + k, t], layers + 3
        )
        for k, term in enumerate(terms):
            for g in range(3):
                part[g, start - 3 + k, t] = term[g]

    def own(layer, carry):
        terms = lat_inner([[wide[f, layer + 6, t] for t in range(tiles)] for f in range(3)], sub, True)
        for t in range(tiles):
            for g in range(3):
                part[g, layer + 3, t] += terms[t][g]
        return carry

    lax.fori_loop(0, layers, own, 0, unroll=True)

    def other(e, carry):
        terms = lat_inner(
            [[wide[f, near + 3 + e, t] for t in range(tiles)] for f in range(3)], sub, False
        )
        for t in range(tiles):
            for g in range(2):
                part[g, near + e, t] += terms[t][g]
        return carry

    lax.fori_loop(0, 3, other, 0, unroll=True)


def turn_kernel(*refs):
    fields, from_left, from_right, part = refs[:6], refs[6], refs[7], refs[8]
    to_first, to_second, to_core, edges = refs[11:]
    layers, rows, lanes = fields[0].shape
    tiles = rows // SUB
    sub, lane = iotas(lanes)
    core = lax.axis_index("rad")
    even = lax.axis_index("lat") % 2 == 0
    per = lanes // SEGMENT

    def send(k, low, high):
        to_first[k] = jnp.where(even, high, low)
        to_second[k] = jnp.where(even, low, high)

    def ends(ref, *index):
        low, high = (ref[(*index, pl.ds(t * SUB, SUB), slice(None))] for t in (0, tiles - 1))
        return jnp.where(sub < 4, low, high)

    group = (from_left.shape[0] - 1) * (1 - core)
    for k, ref in enumerate((from_left, from_right)):
        to_core[k] = ref[group]
    packed = [None, None]
    for g in range(from_left.shape[0]):
        left, right = ends(from_left, g), ends(from_right, g)
        for s in range(min(per, layers - g * per)):
            layer = g * per + s
            here = [ends(x, layer) for x in fields]
            there = [unpacked(left, right, f, s, lane) for f in range(3)]
            laps, _ = longitudinal(here[:3], there, lane, False, False)
            stiff = here[5] * LAP_SCALE
            made = []
            for f in range(2):
                before = jnp.where(sub < 4, part[f, layer + 3, 0], part[f, layer + 3, tiles - 1])
                made.append(2.0 * here[f] - here[3 + f] + stiff * (before + laps[0][f]))
            send(layer, *(pack_three(*made, here[5], low, sub) for low in (True, False)))
            for k, low in enumerate((True, False)):
                x = rolled(pack_three(*there, low, sub), 16 * layer + 6, 1)
                packed[k] = x if layer == 0 else jnp.where(lane >= 16 * layer, x, packed[k])
    send(2 * layers + 4, *packed)
    for k in range(2):
        edges[k] = packed[k]


def middle_kernel(*refs):
    fields, (bulk_in, density_in) = refs[:6], refs[6:8]
    from_left, from_right, from_core, from_core2, wide, part = refs[8:14]
    first, first_halo, rest_halo, flux_out, sums, done = refs[14:20]
    halo, wide_halo, part_halo = refs[20:]
    layers, rows, lanes = fields[0].shape
    tiles = rows // SUB
    sub, lane = iotas(lanes)
    core = lax.axis_index("rad")
    near, border = places(core, layers)
    per = lanes // SEGMENT
    zero = jnp.zeros((SUB, lanes), F32)
    inside = range(1, tiles - 1)

    def at(t):
        return pl.ds(t * SUB, SUB)

    for t in range(tiles):
        for layer in range(layers):
            group, s = divmod(layer, per)
            left, right = from_left[group, at(t), :], from_right[group, at(t), :]
            for f in range(6):
                x = unpacked(left, right, f, s, lane)
                if f < 3:
                    wide_halo[f, layer + 3, t] = x
                else:
                    halo[f - 3, layer, t] = x
                if f in (2, 5):
                    rest_halo[f // 3, layer, t] = x
        left, right = from_core2[0, at(t), :], from_core2[1, at(t), :]
        for f in range(3):
            for e in range(3):
                x, y = (unpacked(left, right, f, e + skip, lane) for skip in (0, per - 3))
                wide_halo[f, near + e, t] = jnp.where(core == 0, x, y)
                wide_halo[f, border + e, t] = zero
        for g in range(2):
            for k in range(3):
                first[g, border + k, t] = zero
        terms = radial(
            lambda f, k: wide_halo[f, 3 + k, t], lambda k: wide_halo[2, 3 + k, t], layers
        )
        for k, term in enumerate(terms):
            for g in range(2):
                part_halo[g, k, t] = term[g]

    def own(layer, carry):
        here = [[wide[f, layer + 6, t] for t in range(tiles)] for f in range(3)]
        there = [[wide_halo[f, layer + 3, t] for t in range(tiles)] for f in range(3)]
        lat_halo = lat_inner(there, sub, False)
        for t in range(tiles):
            laps, rho = longitudinal([x[t] for x in here], [x[t] for x in there], lane, True, True)
            stiff = fields[5][layer, at(t), :] * LAP_SCALE
            stiff_halo = halo[2, layer, t] * LAP_SCALE
            for g in range(2):
                update = stiff * (part[g, layer + 3, t] + laps[0][g])
                first[g, layer + 3, t] = 2.0 * here[g][t] - fields[3 + g][layer, at(t), :] + update
                first_halo[g, layer, t] = (
                    2.0 * there[g][t]
                    - halo[g, layer, t]
                    + stiff_halo * (part_halo[g, layer, t] + lat_halo[t][g] + laps[1][g])
                )
            sums[0, layer, t] = bulk_in[layer, at(t), :] + here[0][t] * update
            sums[1, layer, t] = density_in[layer, at(t), :] + RHO_SCALE * (
                part[2, layer + 3, t] + rho
            )
        return carry

    lax.fori_loop(0, layers, own, 0)

    def other(e, carry):
        for t in range(tiles):
            here = [wide[f, near + 3 + e, t] for f in range(3)]
            there = [wide_halo[f, near + e, t] for f in range(3)]
            laps, _ = longitudinal(here, there, lane, False, False)
            stiff = from_core[24 + e, at(t), :] * LAP_SCALE
            for g in range(2):
                first[g, near + e, t] = (
                    2.0 * here[g]
                    - from_core[18 + 3 * g + e, at(t), :]
                    + stiff * (part[g, near + e, t] + laps[0][g])
                )
        return carry

    lax.fori_loop(0, 3, other, 0, unroll=True)

    for t in inside:
        terms = radial(lambda f, k: first[f, 3 + k, t], lambda k: wide[2, 6 + k, t], layers)
        for k, term in enumerate(terms):
            for g in range(3):
                part_halo[g, k, t] = term[g]

    def last(layer, carry):
        here = [[first[f, layer + 3, t] for t in range(tiles)] for f in range(2)]
        here.append([wide[2, layer + 6, t] for t in range(tiles)])
        flux = [lat_flux(here, t, sub) for t in range(tiles)]
        for k in range(3):
            for n, t in enumerate((1, tiles - 2)):
                flux_out[k, n, layer] = flux[t][k]
        for t in inside:
            lat = lat_terms(flux, t, sub, True)
            there = [first_halo[0, layer, t], first_halo[1, layer, t], wide_halo[2, layer + 3, t]]
            laps, rho = longitudinal([x[t] for x in here], there, lane, False, True)
            stiff = fields[5][layer, at(t), :] * LAP_SCALE
            for g in range(2):
                update = stiff * (part_halo[g, layer, t] + lat[g] + laps[0][g])
                done[2 * g, layer, at(t - 1), :] = (
                    2.0 * here[g][t] - fields[g][layer, at(t), :] + update
                )
                done[2 * g + 1, layer, at(t - 1), :] = here[g][t]
            done[4, layer, at(t - 1), :] = sums[0, layer, t] + here[0][t] * update
            done[5, layer, at(t - 1), :] = sums[1, layer, t] + RHO_SCALE * (
                part_halo[2, layer, t] + lat[2] + rho
            )
        return carry

    lax.fori_loop(0, layers, last, 0, unroll=4)


def last_kernel(*refs):
    fields, from_core = refs[:6], refs[6]
    wide, first, first_halo, rest_halo, flux_in, sums, done = refs[7:14]
    edges, from_first, from_second = refs[14:17]
    outs = refs[17:23]
    fixed, fixed_halo, ring_buoy, part, made, sems = refs[23:]
    layers, rows, lanes = fields[0].shape
    tiles = rows // SUB
    sub, lane = iotas(lanes)
    core = lax.axis_index("rad")
    even = lax.axis_index("lat") % 2 == 0
    near, border = places(core, layers)
    zero = jnp.zeros((SUB, lanes), F32)
    ends = ((0, sub < 3), (tiles - 1, sub >= SUB - 3))
    copies = [
        pltpu.make_async_copy(done.at[k], out.at[:, pl.ds(SUB, rows - 2 * SUB), :], sems.at[k, 0])
        for k, out in enumerate(outs)
    ]
    for copy in copies:
        copy.start()

    def at(t):
        return pl.ds(t * SUB, SUB)

    def received(k):
        one, two = from_first[k], from_second[k]
        return jnp.where(even, two, one), jnp.where(even, one, two)

    def join(behind, ahead):
        return jnp.where(sub < 4, ahead, behind)

    def three(k):
        behind, ahead = received(k)
        return list(zip(unpack_three(behind, False), unpack_three(ahead, True)))

    def outer(own, halos):
        low = [jnp.where(sub < 4, x[0], h[0]) for x, h in zip(own, halos)]
        high = [jnp.where(sub < 4, h[1], x[1]) for x, h in zip(own, halos)]
        return lat_outer(*low, sub), lat_outer(*high, sub)

    for g in range(2):
        for k in range(3):
            for n in range(2):
                fixed[g, border + k, n] = zero

    halos = three(2 * layers + 4)
    mine = list(zip(unpack_three(edges[0], True), unpack_three(edges[1], False)))
    side = outer(mine, halos)
    for layer in range(layers):
        for n, (t, mask) in enumerate(ends):
            stiff = rest_halo[1, layer, t] * LAP_SCALE
            for g in range(2):
                lap = jnp.where(mask, rolled(side[n][g], -16 * layer - 6, 1), 0.0)
                fixed_halo[g, layer, n] = first_halo[g, layer, t] + stiff * lap

    for e in range(3):
        halos = three(2 * layers + 1 + e)
        mine = [(wide[f, near + 3 + e, 0], wide[f, near + 3 + e, tiles - 1]) for f in range(3)]
        side = outer(mine, halos)
        for n, (t, mask) in enumerate(ends):
            stiff = from_core[24 + e, at(t), :] * LAP_SCALE
            for g in range(2):
                lap = jnp.where(mask, side[n][g], 0.0)
                fixed[g, near + e, n] = first[g, near + e, t] + stiff * lap

    third = received(2 * layers)
    for layer in range(layers):
        halos = three(layers + layer)
        mine = [(x[layer, at(0), :], x[layer, at(tiles - 1), :]) for x in fields[:3]]
        side = outer(mine, halos)
        for n, (t, mask) in enumerate(ends):
            stiff = fields[5][layer, at(t), :] * LAP_SCALE
            for g in range(2):
                update = stiff * jnp.where(mask, side[n][g], 0.0)
                fixed[g, layer + 3, n] = first[g, layer + 3, t] + update
            made[4, layer, n] = sums[0, layer, t] + mine[0][n] * update
            made[5, layer, n] = sums[1, layer, t] + RHO_SCALE * jnp.where(mask, side[n][2], 0.0)
        adj, fwd, stiff = three(layer)
        low, high = (rolled(third[k], row - layer, 0) for k, row in enumerate((SUB - 3, 2)))
        stiff = jnp.where(
            sub < 4,
            jnp.where(sub == 2, high, stiff[1]),
            jnp.where(sub == SUB - 3, low, stiff[0]),
        )
        for g, x in enumerate((adj, fwd)):
            lap = join(side[0][g], side[1][g])
            fixed[g, layer + 3, 2] = join(*x) + stiff * LAP_SCALE * lap
        ring_buoy[layer] = join(*halos[2])

    for n, (t, _) in enumerate(ends):
        terms = radial(lambda f, k: fixed[f, 3 + k, n], lambda k: wide[2, 6 + k, t], layers)
        for k, term in enumerate(terms):
            for g in range(3):
                part[g, k, n] = term[g]

    def last(layer, carry):
        buoys = [wide[2, layer + 6, t] for t in (0, 1, tiles - 2, tiles - 1)]
        rings = [
            [fixed[f, layer + 3, 2], fixed[f, layer + 3, 0], first[f, layer + 3, 1]]
            + [first[f, layer + 3, tiles - 2], fixed[f, layer + 3, 1]]
            for f in range(2)
        ] + [[ring_buoy[layer], *buoys]]
        flux = [None] * 5
        for t in (0, 1, 4):
            flux[t] = lat_flux(rings, t, sub)
        for n in range(2):
            flux[2 + n] = [flux_in[k, n, layer] for k in range(3)]
        for n, (t, _) in enumerate(ends):
            k = (1, 4)[n]
            here = [x[k] for x in rings]
            lat = lat_terms(flux, k, sub, True)
            there = [fixed_halo[0, layer, n], fixed_halo[1, layer, n], rest_halo[0, layer, t]]
            laps, rho = longitudinal(here, there, lane, False, True)
            stiff = fields[5][layer, at(t), :] * LAP_SCALE
            for g in range(2):
                update = stiff * (part[g, layer, n] + lat[g] + laps[0][g])
                made[2 * g, layer, n] = 2.0 * here[g] - fields[g][layer, at(t), :] + update
                made[2 * g + 1, layer, n] = here[g]
            made[4, layer, n] += here[0] * update
            made[5, layer, n] += RHO_SCALE * (part[2, layer, n] + lat[2] + rho)
        return carry

    lax.fori_loop(0, layers, last, 0, unroll=True)
    for k, out in enumerate(outs):
        for n, (t, _) in enumerate(ends):
            copy = pltpu.make_async_copy(made.at[k, :, n], out.at[:, at(t), :], sems.at[k, 1 + n])
            copy.start()
            copies.append(copy)
    for copy in copies:
        copy.wait()


def pairs(count, start):
    firsts = range(start, count - 1, 2)
    return [p for i in firsts for p in ((i, i + 1), (i + 1, i))]


def call(kernel, out_shape, args, in_specs=None, out_specs=None, **more):
    return pl.pallas_call(
        kernel,
        out_shape=out_shape,
        in_specs=in_specs or [VMEM] * len(args),
        out_specs=out_specs or (VMEM,) * len(out_shape),
        compiler_params=PARAMS,
        **more,
    )(*args)


def shards(
    adj_now, adj_next, fwd_now, fwd_next, stiffness, buoyancy, kernel_bulk_in, kernel_density_in
):
    layers, rows, lanes = adj_now.shape
    tiles = rows // SUB
    fields = (adj_now, fwd_now, buoyancy, adj_next, fwd_next, stiffness)
    groups = -(-layers // (lanes // SEGMENT))
    around, count = lax.axis_size("lon"), lax.axis_size("lat")
    ring = [(i, (i + 1) % around) for i in range(around)]
    swap = [(0, 1), (1, 0)]

    def made(*shape):
        return pltpu.VMEM(shape, F32)

    block = (layers, rows, lanes)
    edge = made(groups, rows, lanes)
    hbm = pl.BlockSpec(memory_space=pltpu.HBM)
    *fields, to_right, to_left, to_core = call(
        edges_kernel,
        (made(*block),) * 6 + (edge, edge, made(sum(WIDTHS), rows, lanes)),
        [pltpu.with_memory_space_constraint(x, pltpu.HBM) for x in fields],
        in_specs=[hbm] * 6,
        scratch_shapes=[pltpu.SemaphoreType.DMA((6,))],
    )
    from_left = lax.ppermute(to_right, "lon", ring)
    from_right = lax.ppermute(to_left, "lon", [(b, a) for a, b in ring])
    from_core = lax.ppermute(to_core, "rad", swap)
    lat_edge = made(2 * layers + 5, SUB, lanes)
    wide, part, to_first, to_second = call(
        inner_kernel,
        (
            made(3, layers + 12, tiles, SUB, lanes),
            made(3, layers + 6, tiles, SUB, lanes),
            lat_edge,
            lat_edge,
        ),
        [*fields, from_core],
    )
    to_first, to_second, to_core, edges = call(
        turn_kernel,
        (lat_edge, lat_edge, made(2, rows, lanes), made(2, SUB, lanes)),
        [*fields, from_left, from_right, part, to_first, to_second],
        input_output_aliases={9: 0, 10: 1},
    )
    from_first = lax.ppermute(to_first, "lat", pairs(count, 0))
    from_second = lax.ppermute(to_second, "lat", pairs(count, 1))
    from_core2 = lax.ppermute(to_core, "rad", swap)
    first, first_halo, rest_halo, flux, sums, done = call(
        middle_kernel,
        (
            made(2, layers + 6, tiles, SUB, lanes),
            made(2, layers, tiles, SUB, lanes),
            made(2, layers, tiles, SUB, lanes),
            made(3, 2, layers, SUB, lanes),
            made(2, layers, tiles, SUB, lanes),
            made(6, layers, rows - 2 * SUB, lanes),
        ),
        [
            *fields,
            kernel_bulk_in,
            kernel_density_in,
            from_left,
            from_right,
            from_core,
            from_core2,
            wide,
            part,
        ],
        cost_estimate=HEAVY,
        scratch_shapes=[
            made(3, layers, tiles, SUB, lanes),
            made(3, layers + 6, tiles, SUB, lanes),
            made(3, layers, tiles, SUB, lanes),
        ],
    )
    return call(
        last_kernel,
        (jax.ShapeDtypeStruct(block, F32),) * 6,
        [
            *fields,
            from_core,
            wide,
            first,
            first_halo,
            rest_halo,
            flux,
            sums,
            done,
            edges,
            from_first,
            from_second,
        ],
        out_specs=(hbm,) * 6,
        scratch_shapes=[
            made(2, layers + 6, 3, SUB, lanes),
            made(2, layers, 2, SUB, lanes),
            made(layers, SUB, lanes),
            made(3, layers, 2, SUB, lanes),
            made(6, layers, 2, SUB, lanes),
            pltpu.SemaphoreType.DMA((6, 3)),
        ],
    )


def solution(mesh):
    spec = P("rad", "lat", "lon")
    return jax.shard_map(
        shards, mesh=mesh, in_specs=(spec,) * 8, out_specs=(spec,) * 6, check_vma=False
    )
```

time: 25.1 us -> 20.4 us (0.81); the launches traced: 24.6 us -> 20.2 us
  waiting for transfers between devices: 7.34 us -> 2.86 us
    ppermute x1, waiting for transfers between devices: 3.02 us -> 0.01 us  [shards(): from_second = lax.ppermute(to_second, 'lat', pairs(count, 1))]
    ppermute x1, waiting for transfers between devices: 0.9 us -> 0.01 us  [shards(): from_first = lax.ppermute(to_first, 'lat', pairs(count, 0))]
    ppermute x1, waiting for transfers between devices: 1.3 us -> 0.74 us  [shards(): from_left = lax.ppermute(to_right, 'lon', ring)]
    pallas_call x3 -> x5, Pallas kernels: 8.3 us -> 8.39 us  [call(): pl.pallas_call(kernel, out_shape=out_shape, in_specs=in_specs or [VMEM] *...]
  transfers between devices with their start and end apart: 6 -> 6, of which waited for: 4 -> 2; matrix products, arithmetic and copies ran while one was open for 0% -> 0% of each run, Pallas kernels for 0% -> 22%
where the time goes in v2:
time: 20.4 us; the launch traced here: 20.2 us
  Pallas kernels  8.39 us (41%)
  starting transfers between devices  8.27 us (41%)
  waiting for transfers between devices  2.86 us (14%)
  between operations  0.72 us (4%)
    pallas_call x5, Pallas kernels, call(): pl.pallas_call(kernel, out_shape=out_shape, in_specs=in_specs or [VMEM] *...  8.39 us
    ppermute x1, starting transfers between devices, shards(): from_second = lax.ppermute(to_second, 'lat', pairs(count, 1))  4.32 us
    ppermute x1, waiting for transfers between devices, shards(): from_right = lax.ppermute(to_left, 'lon', [(b, a) for a, b in ring])  2.11 us
    ppermute x1, starting transfers between devices, shards(): from_core2 = lax.ppermute(to_core, 'rad', swap)  1.56 us
    ppermute x1, starting transfers between devices, shards(): from_left = lax.ppermute(to_right, 'lon', ring)  1.21 us
    ppermute x1, starting transfers between devices, shards(): from_core = lax.ppermute(to_core, 'rad', swap)  0.74 us
    ppermute x1, waiting for transfers between devices, shards(): from_left = lax.ppermute(to_right, 'lon', ring)  0.74 us
  transfers between devices with their start and end apart: 6, of which 2 were waited for; matrix products, arithmetic and copies ran while one was open for 0% of the time, Pallas kernels for 22%

profile of v2, /device:TPU:11, one launch (start us, length us, event | category | flops | bytes accessed | tf_op | source)
XLA Modules:
  0.0 20.2 jit_solution(18190378667491113196)
XLA Ops:
  0.6 1.5 %shard_map.127 = (f32[8,32,128]{2,1,0:T(8,128)S(1)}, f32[8,32,128]{2,1,0:T(8,128)S(1)}, f32[8,32,128]{2,1,0:T(8,128)S(1)}, f32[8,32,128]{2,1,0:T(8,128)S(1)}, f3...) custom-call(f32[8,32,128]{2,1,0:T(8,128)} %refs_0_.1, ...), custom_call_target="tpu_custom_call" | custom-call | tf_op jit(solution)/shard_map/pallas_call | solution.py:568
  2.2 0.7 %collective-permute-start = (f32[27,32,128]{2,1,0:T(8,128)S(1)}, f32[27,32,128]{2,1,0:T(8,128)S(1)}, u32[]{:S(2)}, u32[]{:S(2)}) collective-permute-start(f32[27,32,128]{2,1,0:T(8,128)S(1)} %get-tuple-element.35), channel_id=1, source_target_pairs={{0,1},{1,0},{2,3},{3,2},{4,5},{5,4},{6,7},{7,6},{8,9},{9,8},{10,11... | collective-permute-start | bytes 1327112 | tf_op jit(solution)/shard_map/ppermute | solution.py:604
  2.9 1.2 %collective-permute-start.1 = (f32[2,32,128]{2,1,0:T(8,128)S(1)}, f32[2,32,128]{2,1,0:T(8,128)S(1)}, u32[]{:S(2)}, u32[]{:S(2)}) collective-permute-start(f32[2,32,128]{2,1,0:T(8,128)S(1)} %get-tuple-element.37), channel_id=1, source_target_pairs={{0,8},{8,16},{16,24},{24,0},{1,9},{9,17},{17,25},{25,1},{2,10},{10... | collective-permute-start | bytes 98312 | tf_op jit(solution)/shard_map/ppermute | solution.py:602
  4.1 0.3 %collective-permute-start.2 = (f32[2,32,128]{2,1,0:T(8,128)S(1)}, f32[2,32,128]{2,1,0:T(8,128)S(1)}, u32[]{:S(2)}, u32[]{:S(2)}) collective-permute-start(f32[2,32,128]{2,1,0:T(8,128)S(1)} %get-tuple-element.38), channel_id=1, source_target_pairs={{8,0},{16,8},{24,16},{0,24},{9,1},{17,9},{25,17},{1,25},{10,2},{18... | collective-permute-start | bytes 98312 | tf_op jit(solution)/shard_map/ppermute | solution.py:603
  4.4 0.0 collective-permute-done.refs_6_.refs_10_
  4.4 0.5 %shard_map.128 = (f32[3,20,4,8,128]{4,3,2,1,0:T(8,128)S(1)}, f32[3,14,4,8,128]{4,3,2,1,0:T(8,128)S(1)}, f32[21,8,128]{2,1,0:T(8,128)S(1)}, f32[21,8,128]{2,1,0:T(8,128)S(1)}) custom-call(f32[8,32,128]{2,1,0:T(8,128)S(1)} %get-tuple-element.29.refs_0_, f32[8,32,128]{2,1,0:T(8,128)S(1)} %get-tuple-element.30.refs_1_, ...), custom_call_target="tpu_custom_call" | custom-call | tf_op jit(solution)/shard_map/pallas_call | solution.py:568
  5.0 0.7 %collective-permute-done.1.refs_6_.refs_8_ = f32[2,32,128]{2,1,0:T(8,128)S(1)} collective-permute-done((f32[2,32,128]{2,1,0:T(8,128)S(1)}, f32[2,32,128]{2,1,0:T(8,128)S(1)}, u32[]{:S(2)}, u32[]{:S(2)}) %collective-permute-start.1) | collective-permute-done | bytes 32800 | tf_op jit(solution)/shard_map/ppermute | solution.py:602
  5.7 2.1 %collective-permute-done.2.refs_7_.refs_9_ = f32[2,32,128]{2,1,0:T(8,128)S(1)} collective-permute-done((f32[2,32,128]{2,1,0:T(8,128)S(1)}, f32[2,32,128]{2,1,0:T(8,128)S(1)}, u32[]{:S(2)}, u32[]{:S(2)}) %collective-permute-start.2) | collective-permute-done | bytes 32800 | tf_op jit(solution)/shard_map/ppermute | solution.py:603
  7.8 0.0 copy-start
  7.8 0.0 copy-start.1
  7.8 0.4 %shard_map.129 = (f32[21,8,128]{2,1,0:T(8,128)S(1)}, f32[21,8,128]{2,1,0:T(8,128)S(1)}, f32[2,32,128]{2,1,0:T(8,128)S(1)}, f32[2,8,128]{2,1,0:T(8,128)S(1)}) custom-call(f32[8,32,128]{2,1,0:T(8,128)S(1)} %get-tuple-element.29.refs_0_, f32[8,32,128]{2,1,0:T(8,128)S(1)} %get-tuple-element.30.refs_1_, ...), custom_call_target="tpu_custom_call", output_to_operand_aliasing={{0}: (9, {}), {1}: (10, {})} | custom-call | tf_op jit(solution)/shard_map/pallas_call | solution.py:568
  8.3 1.6 %collective-permute-start.3 = (f32[2,32,128]{2,1,0:T(8,128)S(1)}, f32[2,32,128]{2,1,0:T(8,128)S(1)}, u32[]{:S(2)}, u32[]{:S(2)}) collective-permute-start(f32[2,32,128]{2,1,0:T(8,128)S(1)} %get-tuple-element.42), channel_id=1, source_target_pairs={{0,1},{1,0},{2,3},{3,2},{4,5},{5,4},{6,7},{7,6},{8,9},{9,8},{10,11... | collective-permute-start | bytes 98312 | tf_op jit(solution)/shard_map/ppermute | solution.py:624
  9.8 0.2 collective-permute-start.4
  10.0 4.3 %collective-permute-start.5 = (f32[21,8,128]{2,1,0:T(8,128)S(1)}, f32[21,8,128]{2,1,0:T(8,128)S(1)}, u32[]{:S(2)}, u32[]{:S(2)}) collective-permute-start(f32[21,8,128]{2,1,0:T(8,128)S(1)} %get-tuple-element.51), channel_id=1, source_target_pairs={{2,4},{4,2},{3,5},{5,3},{10,12},{12,10},{11,13},{13,11},{18,20},{2... | collective-permute-start | bytes 258056 | tf_op jit(solution)/shard_map/ppermute | solution.py:623
  14.3 0.0 collective-permute-done.3.refs_11_
  14.3 0.0 copy-done
  14.3 0.0 copy-done.1
  14.4 3.9 %shard_map.130 = (f32[2,14,4,8,128]{4,3,2,1,0:T(8,128)S(1)}, f32[2,8,4,8,128]{4,3,2,1,0:T(8,128)S(1)}, f32[2,8,4,8,128]{4,3,2,1,0:T(8,128)S(1)}, f32[3,2,8,8,128...) custom-call(f32[8,32,128]{2,1,0:T(8,128)S(1)} %get-tuple-element.29.refs_0_, ...), custom_call_target="tpu_custom_call" | custom-call | flops 4000000000 | bytes 1000000 | tf_op jit(solution)/shard_map/pallas_call | solution.py:568
  18.2 0.0 collective-permute-done.4.refs_15_
  18.2 0.0 collective-permute-done.5.refs_16_
  18.3 2.0 %shard_map.131 = (f32[8,32,128]{2,1,0:T(8,128)}, f32[8,32,128]{2,1,0:T(8,128)}, f32[8,32,128]{2,1,0:T(8,128)}, f32[8,32,128]{2,1,0:T(8,128)}, f32[8,32,128]{2,1,0:T(8,128)}, /*index=5*/f32[8,32,128]{2,1,0:T(8,128)}) custom-call(f32[8,32,128]{2,1,0:T(8,128)S(1)} %get-tuple-element.29.refs_0_, f32[8,32,128]{2,1,0:T(8,128)S(1)} %get-tuple-element.30.refs_1_, ...), custom_call_target="tpu_custom_call" | custom-call | tf_op jit(solution)/shard_map/pallas_call | solution.py:568
Async XLA Ops:
  2.2 2.2 %collective-permute-start = (f32[27,32,128]{2,1,0:T(8,128)S(1)}, f32[27,32,128]{2,1,0:T(8,128)S(1)}, u32[]{:S(2)}, u32[]{:S(2)}) collective-permute-start(f32[27,32,128]{2,1,0:T(8,128)S(1)} %get-tuple-element.35), channel_id=1, source_target_pairs={{0,1},{1,0},{2,3},{3,2},{4,5},{5,4},{6,7},{7,6},{8,9},{9,8},{10,11... | collective-permute-start | bytes 1327112 | tf_op jit(solution)/shard_map/ppermute | solution.py:604
  2.9 2.8 %collective-permute-start.1 = (f32[2,32,128]{2,1,0:T(8,128)S(1)}, f32[2,32,128]{2,1,0:T(8,128)S(1)}, u32[]{:S(2)}, u32[]{:S(2)}) collective-permute-start(f32[2,32,128]{2,1,0:T(8,128)S(1)} %get-tuple-element.37), channel_id=1, source_target_pairs={{0,8},{8,16},{16,24},{24,0},{1,9},{9,17},{17,25},{25,1},{2,10},{10... | collective-permute-start | bytes 98312 | tf_op jit(solution)/shard_map/ppermute | solution.py:602
  4.1 3.7 %collective-permute-start.2 = (f32[2,32,128]{2,1,0:T(8,128)S(1)}, f32[2,32,128]{2,1,0:T(8,128)S(1)}, u32[]{:S(2)}, u32[]{:S(2)}) collective-permute-start(f32[2,32,128]{2,1,0:T(8,128)S(1)} %get-tuple-element.38), channel_id=1, source_target_pairs={{8,0},{16,8},{24,16},{0,24},{9,1},{17,9},{25,17},{1,25},{10,2},{18... | collective-permute-start | bytes 98312 | tf_op jit(solution)/shard_map/ppermute | solution.py:603
  7.8 6.5 %copy-start = (f32[8,32,128]{2,1,0:T(8,128)S(1)}, f32[8,32,128]{2,1,0:T(8,128)}, u32[]{:S(2)}) copy-start(f32[8,32,128]{2,1,0:T(8,128)} %refs_6_.1) | copy-start | bytes 393220
  7.8 6.5 %copy-start.1 = (f32[8,32,128]{2,1,0:T(8,128)S(1)}, f32[8,32,128]{2,1,0:T(8,128)}, u32[]{:S(2)}) copy-start(f32[8,32,128]{2,1,0:T(8,128)} %refs_7_.1) | copy-start | bytes 393220
  8.3 6.1 %collective-permute-start.3 = (f32[2,32,128]{2,1,0:T(8,128)S(1)}, f32[2,32,128]{2,1,0:T(8,128)S(1)}, u32[]{:S(2)}, u32[]{:S(2)}) collective-permute-start(f32[2,32,128]{2,1,0:T(8,128)S(1)} %get-tuple-element.42), channel_id=1, source_target_pairs={{0,1},{1,0},{2,3},{3,2},{4,5},{5,4},{6,7},{7,6},{8,9},{9,8},{10,11... | collective-permute-start | bytes 98312 | tf_op jit(solution)/shard_map/ppermute | solution.py:624
  9.8 8.4 %collective-permute-start.4 = (f32[21,8,128]{2,1,0:T(8,128)S(1)}, f32[21,8,128]{2,1,0:T(8,128)S(1)}, u32[]{:S(2)}, u32[]{:S(2)}) collective-permute-start(f32[21,8,128]{2,1,0:T(8,128)S(1)} %get-tuple-element.50), channel_id=1, source_target_pairs={{0,2},{2,0},{4,6},{6,4},{1,3},{3,1},{5,7},{7,5},{8,10},{10,8},{12,... | collective-permute-start | bytes 258056 | tf_op jit(solution)/shard_map/ppermute | solution.py:622
  10.0 8.2 %collective-permute-start.5 = (f32[21,8,128]{2,1,0:T(8,128)S(1)}, f32[21,8,128]{2,1,0:T(8,128)S(1)}, u32[]{:S(2)}, u32[]{:S(2)}) collective-permute-start(f32[21,8,128]{2,1,0:T(8,128)S(1)} %get-tuple-element.51), channel_id=1, source_target_pairs={{2,4},{4,2},{3,5},{5,3},{10,12},{12,10},{11,13},{13,11},{18,20},{2... | collective-permute-start | bytes 258056 | tf_op jit(solution)/shard_map/ppermute | solution.py:623

commit v3 on v2

--- a/solution.py
+++ b/solution.py
@@ -437,7 +437,8 @@
     tiles = rows // SUB
     sub, lane = iotas(lanes)
     core = lax.axis_index("rad")
-    even = lax.axis_index("lat") % 2 == 0
+    place, count = lax.axis_index("lat"), lax.axis_size("lat")
+    even = place % 2 == 0
     near, border = places(core, layers)
     zero = jnp.zeros((SUB, lanes), F32)
     ends = ((0, sub < 3), (tiles - 1, sub >= SUB - 3))
@@ -453,7 +454,8 @@
 
     def received(k):
         one, two = from_first[k], from_second[k]
-        return jnp.where(even, two, one), jnp.where(even, one, two)
+        behind, ahead = jnp.where(even, two, one), jnp.where(even, one, two)
+        return jnp.where(place > 0, behind, 0.0), jnp.where(place < count - 1, ahead, 0.0)
 
     def join(behind, ahead):
         return jnp.where(sub < 4, ahead, behind)
@@ -560,8 +562,14 @@
 
 
 def pairs(count, start):
-    firsts = range(start, count - 1, 2)
-    return [p for i in firsts for p in ((i, i + 1), (i + 1, i))]
+    partner = {i: i for i in range(count)}
+    for i in range(start, count - 1, 2):
+        partner[i], partner[i + 1] = i + 1, i
+    return [
+        (2 * i + core, 2 * j + (core if i != j else 1 - core))
+        for i, j in partner.items()
+        for core in range(2)
+    ]
 
 
 def call(kernel, out_shape, args, in_specs=None, out_specs=None, **more):
@@ -619,8 +627,8 @@
         [*fields, from_left, from_right, part, to_first, to_second],
         input_output_aliases={9: 0, 10: 1},
     )
-    from_first = lax.ppermute(to_first, "lat", pairs(count, 0))
-    from_second = lax.ppermute(to_second, "lat", pairs(count, 1))
+    from_first = lax.ppermute(to_first, ("lat", "rad"), pairs(count, 0))
+    from_second = lax.ppermute(to_second, ("lat", "rad"), pairs(count, 1))
     from_core2 = lax.ppermute(to_core, "rad", swap)
     first, first_halo, rest_halo, flux, sums, done = call(
         middle_kernel,

time: 20.4 us -> 18.4 us (0.902)
  starting transfers between devices: 8.27 us -> 6.37 us
    ppermute x2, starting transfers between devices: 4.5 us -> 2.61 us  [the longest x1 2.42 us: shards(): from_second = lax.ppermute(to_second, ('lat', 'rad'), pairs(count, 1))]
  transfers between devices with their start and end apart: 6 -> 6, of which waited for: 2 -> 2; matrix products, arithmetic and copies ran while one was open for 0% -> 0% of each run, Pallas kernels for 22% -> 24%
where the time goes in v3:
time: 18.4 us; the launch traced here: 18.3 us
  Pallas kernels  8.35 us (45%)
  starting transfers between devices  6.37 us (35%)
  waiting for transfers between devices  2.86 us (16%)
  between operations  0.69 us (4%)
    pallas_call x5, Pallas kernels, call(): pl.pallas_call(kernel, out_shape=out_shape, in_specs=in_specs or [VMEM] *...  8.35 us
    ppermute x1, starting transfers between devices, shards(): from_second = lax.ppermute(to_second, ('lat', 'rad'), pairs(count, 1))  2.42 us
    ppermute x1, waiting for transfers between devices, shards(): from_right = lax.ppermute(to_left, 'lon', [(b, a) for a, b in ring])  2.11 us
    ppermute x1, starting transfers between devices, shards(): from_core2 = lax.ppermute(to_core, 'rad', swap)  1.56 us
    ppermute x1, starting transfers between devices, shards(): from_left = lax.ppermute(to_right, 'lon', ring)  1.21 us
    ppermute x1, starting transfers between devices, shards(): from_core = lax.ppermute(to_core, 'rad', swap)  0.74 us
    ppermute x1, waiting for transfers between devices, shards(): from_left = lax.ppermute(to_right, 'lon', ring)  0.74 us
  transfers between devices with their start and end apart: 6, of which 2 were waited for; matrix products, arithmetic and copies ran while one was open for 0% of the time, Pallas kernels for 24%

profile of v3, /device:TPU:11, one launch (start us, length us, event | category | flops | bytes accessed | tf_op | source)
XLA Modules:
  0.0 18.3 jit_solution(6748570470559144483)
XLA Ops:
  0.6 1.5 %shard_map.127 = (f32[8,32,128]{2,1,0:T(8,128)S(1)}, f32[8,32,128]{2,1,0:T(8,128)S(1)}, f32[8,32,128]{2,1,0:T(8,128)S(1)}, f32[8,32,128]{2,1,0:T(8,128)S(1)}, f3...) custom-call(f32[8,32,128]{2,1,0:T(8,128)} %refs_0_.1, ...), custom_call_target="tpu_custom_call" | custom-call | tf_op jit(solution)/shard_map/pallas_call | solution.py:576
  2.2 0.7 %collective-permute-start = (f32[27,32,128]{2,1,0:T(8,128)S(1)}, f32[27,32,128]{2,1,0:T(8,128)S(1)}, u32[]{:S(2)}, u32[]{:S(2)}) collective-permute-start(f32[27,32,128]{2,1,0:T(8,128)S(1)} %get-tuple-element.35), channel_id=1, source_target_pairs={{0,1},{1,0},{2,3},{3,2},{4,5},{5,4},{6,7},{7,6},{8,9},{9,8},{10,11... | collective-permute-start | bytes 1327112 | tf_op jit(solution)/shard_map/ppermute | solution.py:612
  2.9 1.2 %collective-permute-start.1 = (f32[2,32,128]{2,1,0:T(8,128)S(1)}, f32[2,32,128]{2,1,0:T(8,128)S(1)}, u32[]{:S(2)}, u32[]{:S(2)}) collective-permute-start(f32[2,32,128]{2,1,0:T(8,128)S(1)} %get-tuple-element.37), channel_id=1, source_target_pairs={{0,8},{8,16},{16,24},{24,0},{1,9},{9,17},{17,25},{25,1},{2,10},{10... | collective-permute-start | bytes 98312 | tf_op jit(solution)/shard_map/ppermute | solution.py:610
  4.1 0.3 %collective-permute-start.2 = (f32[2,32,128]{2,1,0:T(8,128)S(1)}, f32[2,32,128]{2,1,0:T(8,128)S(1)}, u32[]{:S(2)}, u32[]{:S(2)}) collective-permute-start(f32[2,32,128]{2,1,0:T(8,128)S(1)} %get-tuple-element.38), channel_id=1, source_target_pairs={{8,0},{16,8},{24,16},{0,24},{9,1},{17,9},{25,17},{1,25},{10,2},{18... | collective-permute-start | bytes 98312 | tf_op jit(solution)/shard_map/ppermute | solution.py:611
  4.4 0.0 collective-permute-done.refs_6_.refs_10_
  4.4 0.5 %shard_map.128 = (f32[3,20,4,8,128]{4,3,2,1,0:T(8,128)S(1)}, f32[3,14,4,8,128]{4,3,2,1,0:T(8,128)S(1)}, f32[21,8,128]{2,1,0:T(8,128)S(1)}, f32[21,8,128]{2,1,0:T(8,128)S(1)}) custom-call(f32[8,32,128]{2,1,0:T(8,128)S(1)} %get-tuple-element.29.refs_0_, f32[8,32,128]{2,1,0:T(8,128)S(1)} %get-tuple-element.30.refs_1_, ...), custom_call_target="tpu_custom_call" | custom-call | tf_op jit(solution)/shard_map/pallas_call | solution.py:576
  5.0 0.7 %collective-permute-done.1.refs_6_.refs_8_ = f32[2,32,128]{2,1,0:T(8,128)S(1)} collective-permute-done((f32[2,32,128]{2,1,0:T(8,128)S(1)}, f32[2,32,128]{2,1,0:T(8,128)S(1)}, u32[]{:S(2)}, u32[]{:S(2)}) %collective-permute-start.1) | collective-permute-done | bytes 32800 | tf_op jit(solution)/shard_map/ppermute | solution.py:610
  5.7 2.1 %collective-permute-done.2.refs_7_.refs_9_ = f32[2,32,128]{2,1,0:T(8,128)S(1)} collective-permute-done((f32[2,32,128]{2,1,0:T(8,128)S(1)}, f32[2,32,128]{2,1,0:T(8,128)S(1)}, u32[]{:S(2)}, u32[]{:S(2)}) %collective-permute-start.2) | collective-permute-done | bytes 32800 | tf_op jit(solution)/shard_map/ppermute | solution.py:611
  7.8 0.0 copy-start
  7.8 0.0 copy-start.1
  7.8 0.4 %shard_map.129 = (f32[21,8,128]{2,1,0:T(8,128)S(1)}, f32[21,8,128]{2,1,0:T(8,128)S(1)}, f32[2,32,128]{2,1,0:T(8,128)S(1)}, f32[2,8,128]{2,1,0:T(8,128)S(1)}) custom-call(f32[8,32,128]{2,1,0:T(8,128)S(1)} %get-tuple-element.29.refs_0_, f32[8,32,128]{2,1,0:T(8,128)S(1)} %get-tuple-element.30.refs_1_, ...), custom_call_target="tpu_custom_call", output_to_operand_aliasing={{0}: (9, {}), {1}: (10, {})} | custom-call | tf_op jit(solution)/shard_map/pallas_call | solution.py:576
  8.3 1.6 %collective-permute-start.3 = (f32[2,32,128]{2,1,0:T(8,128)S(1)}, f32[2,32,128]{2,1,0:T(8,128)S(1)}, u32[]{:S(2)}, u32[]{:S(2)}) collective-permute-start(f32[2,32,128]{2,1,0:T(8,128)S(1)} %get-tuple-element.42), channel_id=1, source_target_pairs={{0,1},{1,0},{2,3},{3,2},{4,5},{5,4},{6,7},{7,6},{8,9},{9,8},{10,11... | collective-permute-start | bytes 98312 | tf_op jit(solution)/shard_map/ppermute | solution.py:632
  9.8 0.2 %collective-permute-start.4 = (f32[21,8,128]{2,1,0:T(8,128)S(1)}, f32[21,8,128]{2,1,0:T(8,128)S(1)}, u32[]{:S(2)}, u32[]{:S(2)}) collective-permute-start(f32[21,8,128]{2,1,0:T(8,128)S(1)} %get-tuple-element.50), channel_id=1, source_target_pairs={{0,2},{1,3},{2,0},{3,1},{4,6},{5,7},{6,4},{7,5},{8,10},{9,11},{10,... | collective-permute-start | bytes 258056 | tf_op jit(solution)/shard_map/ppermute | solution.py:630
  10.0 2.4 %collective-permute-start.5 = (f32[21,8,128]{2,1,0:T(8,128)S(1)}, f32[21,8,128]{2,1,0:T(8,128)S(1)}, u32[]{:S(2)}, u32[]{:S(2)}) collective-permute-start(f32[21,8,128]{2,1,0:T(8,128)S(1)} %get-tuple-element.51), channel_id=1, source_target_pairs={{0,1},{1,0},{2,4},{3,5},{4,2},{5,3},{6,7},{7,6},{8,9},{9,8},{10,12... | collective-permute-start | bytes 258056 | tf_op jit(solution)/shard_map/ppermute | solution.py:631
  12.4 0.0 collective-permute-done.3.refs_11_
  12.4 0.0 copy-done
  12.4 0.0 copy-done.1
  12.4 3.9 %shard_map.130 = (f32[2,14,4,8,128]{4,3,2,1,0:T(8,128)S(1)}, f32[2,8,4,8,128]{4,3,2,1,0:T(8,128)S(1)}, f32[2,8,4,8,128]{4,3,2,1,0:T(8,128)S(1)}, f32[3,2,8,8,128...) custom-call(f32[8,32,128]{2,1,0:T(8,128)S(1)} %get-tuple-element.29.refs_0_, ...), custom_call_target="tpu_custom_call" | custom-call | flops 4000000000 | bytes 1000000 | tf_op jit(solution)/shard_map/pallas_call | solution.py:576
  16.3 0.0 collective-permute-done.4.refs_15_
  16.3 0.0 collective-permute-done.5.refs_16_
  16.3 1.9 %shard_map.131 = (f32[8,32,128]{2,1,0:T(8,128)}, f32[8,32,128]{2,1,0:T(8,128)}, f32[8,32,128]{2,1,0:T(8,128)}, f32[8,32,128]{2,1,0:T(8,128)}, f32[8,32,128]{2,1,0:T(8,128)}, /*index=5*/f32[8,32,128]{2,1,0:T(8,128)}) custom-call(f32[8,32,128]{2,1,0:T(8,128)S(1)} %get-tuple-element.29.refs_0_, f32[8,32,128]{2,1,0:T(8,128)S(1)} %get-tuple-element.30.refs_1_, ...), custom_call_target="tpu_custom_call" | custom-call | tf_op jit(solution)/shard_map/pallas_call | solution.py:576
Async XLA Ops:
  2.2 2.2 %collective-permute-start = (f32[27,32,128]{2,1,0:T(8,128)S(1)}, f32[27,32,128]{2,1,0:T(8,128)S(1)}, u32[]{:S(2)}, u32[]{:S(2)}) collective-permute-start(f32[27,32,128]{2,1,0:T(8,128)S(1)} %get-tuple-element.35), channel_id=1, source_target_pairs={{0,1},{1,0},{2,3},{3,2},{4,5},{5,4},{6,7},{7,6},{8,9},{9,8},{10,11... | collective-permute-start | bytes 1327112 | tf_op jit(solution)/shard_map/ppermute | solution.py:612
  2.9 2.8 %collective-permute-start.1 = (f32[2,32,128]{2,1,0:T(8,128)S(1)}, f32[2,32,128]{2,1,0:T(8,128)S(1)}, u32[]{:S(2)}, u32[]{:S(2)}) collective-permute-start(f32[2,32,128]{2,1,0:T(8,128)S(1)} %get-tuple-element.37), channel_id=1, source_target_pairs={{0,8},{8,16},{16,24},{24,0},{1,9},{9,17},{17,25},{25,1},{2,10},{10... | collective-permute-start | bytes 98312 | tf_op jit(solution)/shard_map/ppermute | solution.py:610
  4.1 3.7 %collective-permute-start.2 = (f32[2,32,128]{2,1,0:T(8,128)S(1)}, f32[2,32,128]{2,1,0:T(8,128)S(1)}, u32[]{:S(2)}, u32[]{:S(2)}) collective-permute-start(f32[2,32,128]{2,1,0:T(8,128)S(1)} %get-tuple-element.38), channel_id=1, source_target_pairs={{8,0},{16,8},{24,16},{0,24},{9,1},{17,9},{25,17},{1,25},{10,2},{18... | collective-permute-start | bytes 98312 | tf_op jit(solution)/shard_map/ppermute | solution.py:611
  7.8 4.6 %copy-start = (f32[8,32,128]{2,1,0:T(8,128)S(1)}, f32[8,32,128]{2,1,0:T(8,128)}, u32[]{:S(2)}) copy-start(f32[8,32,128]{2,1,0:T(8,128)} %refs_6_.1) | copy-start | bytes 393220
  7.8 4.6 %copy-start.1 = (f32[8,32,128]{2,1,0:T(8,128)S(1)}, f32[8,32,128]{2,1,0:T(8,128)}, u32[]{:S(2)}) copy-start(f32[8,32,128]{2,1,0:T(8,128)} %refs_7_.1) | copy-start | bytes 393220
  8.3 4.2 %collective-permute-start.3 = (f32[2,32,128]{2,1,0:T(8,128)S(1)}, f32[2,32,128]{2,1,0:T(8,128)S(1)}, u32[]{:S(2)}, u32[]{:S(2)}) collective-permute-start(f32[2,32,128]{2,1,0:T(8,128)S(1)} %get-tuple-element.42), channel_id=1, source_target_pairs={{0,1},{1,0},{2,3},{3,2},{4,5},{5,4},{6,7},{7,6},{8,9},{9,8},{10,11... | collective-permute-start | bytes 98312 | tf_op jit(solution)/shard_map/ppermute | solution.py:632
  9.8 6.5 %collective-permute-start.4 = (f32[21,8,128]{2,1,0:T(8,128)S(1)}, f32[21,8,128]{2,1,0:T(8,128)S(1)}, u32[]{:S(2)}, u32[]{:S(2)}) collective-permute-start(f32[21,8,128]{2,1,0:T(8,128)S(1)} %get-tuple-element.50), channel_id=1, source_target_pairs={{0,2},{1,3},{2,0},{3,1},{4,6},{5,7},{6,4},{7,5},{8,10},{9,11},{10,... | collective-permute-start | bytes 258056 | tf_op jit(solution)/shard_map/ppermute | solution.py:630
  10.0 6.3 %collective-permute-start.5 = (f32[21,8,128]{2,1,0:T(8,128)S(1)}, f32[21,8,128]{2,1,0:T(8,128)S(1)}, u32[]{:S(2)}, u32[]{:S(2)}) collective-permute-start(f32[21,8,128]{2,1,0:T(8,128)S(1)} %get-tuple-element.51), channel_id=1, source_target_pairs={{0,1},{1,0},{2,4},{3,5},{4,2},{5,3},{6,7},{7,6},{8,9},{9,8},{10,12... | collective-permute-start | bytes 258056 | tf_op jit(solution)/shard_map/ppermute | solution.py:631

commit v4 on v3

--- a/solution.py
+++ b/solution.py
@@ -63,36 +63,32 @@
     copies = [pltpu.make_async_copy(x, y, sems.at[k]) for k, (x, y) in enumerate(zip(sources, fields))]
     for copy in copies:
         copy.start()
-    for copy in copies:
-        copy.wait()
     layers, rows, lanes = fields[0].shape
     _, lane = iotas(lanes)
     core = lax.axis_index("rad")
     per = lanes // SEGMENT
-    for group in range(to_right.shape[0]):
-        for t in range(rows // SUB):
-            at = pl.ds(t * SUB, SUB)
-            right = left = None
-            for s in range(per):
-                layer = group * per + s
-                if layer >= layers:
-                    break
-                for f, (width, offset) in enumerate(zip(WIDTHS, OFFSETS)):
-                    first = s * SEGMENT + offset
-                    x = rolled(fields[f][layer, at, :], first + width, 1)
-                    second = first + width
-                    wrap = second + width - lanes
-                    mask = lane >= second
-                    if wrap > 0:
-                        mask = mask | (lane < wrap)
-                    right = x if right is None else jnp.where(lane >= first, x, right)
-                    left = x if left is None else jnp.where(mask, x, left)
-            to_right[group, at, :] = right
-            to_left[group, at, :] = left
-    at = 0
-    for f, width in enumerate(WIDTHS):
-        to_core[at : at + width] = fields[f][pl.ds((layers - width) * (1 - core), width)]
-        at += width
+    row = 0
+    packed = {}
+    for f, (width, offset) in enumerate(zip(WIDTHS, OFFSETS)):
+        copies[f].wait()
+        for layer in range(layers):
+            group, s = divmod(layer, per)
+            first = s * SEGMENT + offset
+            second = first + width
+            mask = lane >= second
+            if second + width > lanes:
+                mask = mask | (lane < second + width - lanes)
+            mine = (lane >= first) & (lane < second)
+            theirs = mask & (lane < second + width) if second + width <= lanes else mask
+            for t in range(rows // SUB):
+                x = rolled(fields[f][layer, pl.ds(t * SUB, SUB), :], second, 1)
+                right, left = packed.get((group, t), (x, x))
+                packed[group, t] = jnp.where(mine, x, right), jnp.where(theirs, x, left)
+        to_core[row : row + width] = fields[f][pl.ds((layers - width) * (1 - core), width)]
+        row += width
+    for (group, t), (right, left) in packed.items():
+        to_right[group, pl.ds(t * SUB, SUB), :] = right
+        to_left[group, pl.ds(t * SUB, SUB), :] = left
 
 
 def radial(p_at, b_at, layers):
@@ -143,11 +139,82 @@
     return laps, density
 
 
-def unpacked(left, right, f, s, lane):
-    width, offset = WIDTHS[f], OFFSETS[f]
-    first = s * SEGMENT + offset
-    mask = (lane >= first) & (lane < first + width)
-    return rolled(jnp.where(mask, left, right), -first - width, 1)
+def windows(from_left, from_right, to_left, to_right, f, seg):
+    offset = OFFSETS[f]
+    mask = (seg >= offset) & (seg < offset + WIDTHS[f])
+    return (
+        rolled(jnp.where(mask, from_left, to_left), -offset, 1),
+        rolled(jnp.where(mask, to_right, from_right), -offset, 1),
+    )
+
+
+def lon_flux(adj, fwd, buoy):
+    face = buoy + rolled(buoy, -1, 1)
+    grads = [slope(rolled(x, -1, 1), x, rolled(x, -2, 1), rolled(x, 1, 1)) for x in (adj, fwd)]
+    flux = [face * g for g in grads]
+    return flux[0], flux[1], flux[0] * grads[1]
+
+
+def lon_terms(adj, fwd, buoy, want_rho):
+    flux = lon_flux(adj, fwd, buoy)
+    terms = [slope(x, rolled(x, 1, 1), rolled(x, -1, 1), rolled(x, 2, 1)) for x in flux[:2]]
+    return terms + [flux[2] + rolled(flux[2], 1, 1)] if want_rho else terms
+
+
+def edge_terms(wins, seg, want_rho):
+    left = lon_terms(*(x[0] for x in wins), want_rho)
+    right = lon_terms(*(x[1] for x in wins), want_rho)
+    valid = (seg >= 3) & (seg < 9)
+    own = [jnp.where(valid, jnp.where(seg < 6, y, x), 0.0) for x, y in zip(left, right)]
+    return own, [jnp.where(seg < 6, x, y) for x, y in zip(left[:2], right[:2])]
+
+
+def halos_of(wins, seg):
+    return [jnp.where(seg < 6, x, y) for x, y in wins]
+
+
+def spread(x, s):
+    return rolled(x, -s * SEGMENT - 6, 1)
+
+
+def at_ends(x, s, lane):
+    return jnp.where((lane < 3) | (lane >= x.shape[1] - 3), spread(x, s), 0.0)
+
+
+def merged(tiles, seg):
+    half = SEGMENT // 2
+    out = []
+    for k in range(0, len(tiles), 2):
+        x = tiles[k]
+        if k + 1 < len(tiles):
+            x = jnp.where(seg < half, x, rolled(tiles[k + 1], half, 1))
+        out.append(x)
+    return out
+
+
+def unmerged(x, group):
+    return rolled(x, -(SEGMENT // 2) * (group % 2), 1)
+
+
+def packed_radial(groups, lane):
+    size = lane.shape[1]
+
+    def shift(x, i, by):
+        step = by * SEGMENT
+        if by > 0:
+            return rolled(jnp.where(lane < step, x[min(i + 1, len(x) - 1)], x[i]), -step, 1)
+        return rolled(jnp.where(lane >= size + step, x[max(i - 1, 0)], x[i]), -step, 1)
+
+    adj, fwd, buoy = ([x[f] for x in groups] for f in range(3))
+    flux = ([], [])
+    for i in range(len(groups)):
+        face = buoy[i] + shift(buoy, i, 1)
+        for f, x in enumerate((adj, fwd)):
+            flux[f].append(face * slope(shift(x, i, 1), x[i], shift(x, i, 2), shift(x, i, -1)))
+    return [
+        [slope(x[i], shift(x, i, -1), shift(x, i, 1), shift(x, i, -2)) for x in flux]
+        for i in range(1, len(groups) - 1)
+    ]
 
 
 def lat_flux(ring, t, sub):
@@ -202,6 +269,7 @@
     even = lax.axis_index("lat") % 2 == 0
     near, border = places(core, layers)
     zero = jnp.zeros((SUB, lanes), F32)
+    away = (lane >= 3) & (lane < lanes - 3)
 
     def at(t):
         return pl.ds(t * SUB, SUB)
@@ -246,35 +314,39 @@
                 part[g, start - 3 + k, t] = term[g]
 
     def own(layer, carry):
-        terms = lat_inner([[wide[f, layer + 6, t] for t in range(tiles)] for f in range(3)], sub, True)
+        here = [[wide[f, layer + 6, t] for t in range(tiles)] for f in range(3)]
+        terms = lat_inner(here, sub, True)
         for t in range(tiles):
+            lon = lon_terms(*(x[t] for x in here), True)
             for g in range(3):
-                part[g, layer + 3, t] += terms[t][g]
+                part[g, layer + 3, t] += terms[t][g] + jnp.where(away, lon[g], 0.0)
         return carry
 
-    lax.fori_loop(0, layers, own, 0, unroll=True)
+    lax.fori_loop(0, layers, own, 0, unroll=2)
 
     def other(e, carry):
-        terms = lat_inner(
-            [[wide[f, near + 3 + e, t] for t in range(tiles)] for f in range(3)], sub, False
-        )
+        here = [[wide[f, near + 3 + e, t] for t in range(tiles)] for f in range(3)]
+        terms = lat_inner(here, sub, False)
         for t in range(tiles):
-            for g in range(2):
-                part[g, near + e, t] += terms[t][g]
+            lon = lon_terms(*(x[t] for x in here), False)
+            for g in range(2):
+                part[g, near + e, t] += terms[t][g] + jnp.where(away, lon[g], 0.0)
         return carry
 
     lax.fori_loop(0, 3, other, 0, unroll=True)
 
 
 def turn_kernel(*refs):
-    fields, from_left, from_right, part = refs[:6], refs[6], refs[7], refs[8]
-    to_first, to_second, to_core, edges = refs[11:]
+    fields, packs, part = refs[:6], refs[6:10], refs[10]
+    to_first, to_second, to_core, edges = refs[13:]
     layers, rows, lanes = fields[0].shape
     tiles = rows // SUB
     sub, lane = iotas(lanes)
+    seg = lane % SEGMENT
     core = lax.axis_index("rad")
     even = lax.axis_index("lat") % 2 == 0
     per = lanes // SEGMENT
+    groups = packs[0].shape[0]
 
     def send(k, low, high):
         to_first[k] = jnp.where(even, high, low)
@@ -284,121 +356,123 @@
         low, high = (ref[(*index, pl.ds(t * SUB, SUB), slice(None))] for t in (0, tiles - 1))
         return jnp.where(sub < 4, low, high)
 
-    group = (from_left.shape[0] - 1) * (1 - core)
-    for k, ref in enumerate((from_left, from_right)):
-        to_core[k] = ref[group]
-    packed = [None, None]
-    for g in range(from_left.shape[0]):
-        left, right = ends(from_left, g), ends(from_right, g)
+    for k, ref in enumerate(packs):
+        to_core[k] = ref[(groups - 1) * (1 - core)]
+    halos = []
+    for g in range(groups):
+        pack = [ends(x, g) for x in packs]
+        wins = [windows(*pack, f, seg) for f in range(3)]
+        laps, _ = edge_terms(wins, seg, False)
+        halos.append(halos_of(wins, seg))
         for s in range(min(per, layers - g * per)):
             layer = g * per + s
             here = [ends(x, layer) for x in fields]
-            there = [unpacked(left, right, f, s, lane) for f in range(3)]
-            laps, _ = longitudinal(here[:3], there, lane, False, False)
             stiff = here[5] * LAP_SCALE
             made = []
             for f in range(2):
                 before = jnp.where(sub < 4, part[f, layer + 3, 0], part[f, layer + 3, tiles - 1])
-                made.append(2.0 * here[f] - here[3 + f] + stiff * (before + laps[0][f]))
+                lap = before + at_ends(laps[f], s, lane)
+                made.append(2.0 * here[f] - here[3 + f] + stiff * lap)
             send(layer, *(pack_three(*made, here[5], low, sub) for low in (True, False)))
-            for k, low in enumerate((True, False)):
-                x = rolled(pack_three(*there, low, sub), 16 * layer + 6, 1)
-                packed[k] = x if layer == 0 else jnp.where(lane >= 16 * layer, x, packed[k])
-    send(2 * layers + 4, *packed)
-    for k in range(2):
-        edges[k] = packed[k]
+    both = [merged([pack_three(*x, low, sub) for x in halos], seg) for low in (True, False)]
+    for k, (low, high) in enumerate(zip(*both)):
+        send(2 * layers + 4 + k, low, high)
+        edges[0, k] = low
+        edges[1, k] = high
 
 
 def middle_kernel(*refs):
     fields, (bulk_in, density_in) = refs[:6], refs[6:8]
-    from_left, from_right, from_core, from_core2, wide, part = refs[8:14]
-    first, first_halo, rest_halo, flux_out, sums, done = refs[14:20]
-    halo, wide_halo, part_halo = refs[20:]
+    packs, from_core, from_core2, wide, part = refs[8:12], refs[12], refs[13], refs[14], refs[15]
+    first, first_pack, stiff_pack, buoy_halo, flux_out, sums, done = refs[16:23]
+    first_halo, own_pack, part_last, halo_pack, lap_pack = refs[23:]
     layers, rows, lanes = fields[0].shape
     tiles = rows // SUB
     sub, lane = iotas(lanes)
+    seg = lane % SEGMENT
     core = lax.axis_index("rad")
     near, border = places(core, layers)
     per = lanes // SEGMENT
+    groups = packs[0].shape[0]
     zero = jnp.zeros((SUB, lanes), F32)
     inside = range(1, tiles - 1)
 
     def at(t):
-        return pl.ds(t * SUB, SUB)
-
-    for t in range(tiles):
+        return pl.ds(pl.multiple_of(t * SUB, SUB), SUB)
+
+    def edges_at(t, carry):
+        sources = [[x[group, at(t), :] for x in packs] for group in range(groups)]
+        sources.append([from_core2[k, at(t), :] for k in range(4)])
+        wins = [[windows(*x, f, seg) for f in range(3)] for x in sources]
+        halos = [halos_of(x, seg) for x in wins]
+        before = [jnp.where(core == 0, 0.0, x) for x in halos[-1]]
+        after = [jnp.where(core == 0, x, 0.0) for x in halos[-1]]
+        radials = packed_radial([before, *halos[:-1], after], lane)
+        terms = [edge_terms(x, seg, k < groups) for k, x in enumerate(wins)]
+        own = [x for x, _ in terms]
+        own[groups] = [
+            jnp.where(core == 0, x, rolled(x, -(per - 3) * SEGMENT, 1)) for x in own[groups]
+        ]
+        for group in range(groups):
+            for f in range(3):
+                halo_pack[f, group, t] = halos[group][f]
+            for g in range(2):
+                lap_pack[g, group, t] = terms[group][1][g] + radials[group][g]
+        for group in range(groups + 1):
+            for g, x in enumerate(own[group]):
+                own_pack[g, group, t] = x
+        return carry
+
+    lax.fori_loop(0, tiles, edges_at, 0)
+    for group in range(groups):
+        halo = [[halo_pack[f, group, t] for t in range(tiles)] for f in range(3)]
+        lat = lat_inner(halo, sub, False)
+        for t in range(tiles):
+            rest = []
+            for f in range(3, 6):
+                offset = OFFSETS[f]
+                mask = (seg >= offset) & (seg < offset + WIDTHS[f])
+                x = jnp.where(mask, packs[0][group, at(t), :], packs[1][group, at(t), :])
+                rest.append(rolled(x, 3 - offset, 1))
+            stiff = rest[2] * LAP_SCALE
+            stiff_pack[group, t] = stiff
+            for g in range(2):
+                lap = lap_pack[g, group, t] + lat[t][g]
+                first_pack[g, group, t] = 2.0 * halo[g][t] - rest[g] + stiff * lap
+    for g in range(2):
+        for k in range(3):
+            for t in range(tiles):
+                first[g, border + k, t] = zero
+
+    def first_at(t, carry):
         for layer in range(layers):
             group, s = divmod(layer, per)
-            left, right = from_left[group, at(t), :], from_right[group, at(t), :]
-            for f in range(6):
-                x = unpacked(left, right, f, s, lane)
-                if f < 3:
-                    wide_halo[f, layer + 3, t] = x
-                else:
-                    halo[f - 3, layer, t] = x
-                if f in (2, 5):
-                    rest_halo[f // 3, layer, t] = x
-        left, right = from_core2[0, at(t), :], from_core2[1, at(t), :]
-        for f in range(3):
-            for e in range(3):
-                x, y = (unpacked(left, right, f, e + skip, lane) for skip in (0, per - 3))
-                wide_halo[f, near + e, t] = jnp.where(core == 0, x, y)
-                wide_halo[f, border + e, t] = zero
-        for g in range(2):
-            for k in range(3):
-                first[g, border + k, t] = zero
-        terms = radial(
-            lambda f, k: wide_halo[f, 3 + k, t], lambda k: wide_halo[2, 3 + k, t], layers
-        )
-        for k, term in enumerate(terms):
-            for g in range(2):
-                part_halo[g, k, t] = term[g]
-
-    def own(layer, carry):
-        here = [[wide[f, layer + 6, t] for t in range(tiles)] for f in range(3)]
-        there = [[wide_halo[f, layer + 3, t] for t in range(tiles)] for f in range(3)]
-        lat_halo = lat_inner(there, sub, False)
-        for t in range(tiles):
-            laps, rho = longitudinal([x[t] for x in here], [x[t] for x in there], lane, True, True)
+            buoy_halo[layer, t] = spread(halo_pack[2, group, t], s)
             stiff = fields[5][layer, at(t), :] * LAP_SCALE
-            stiff_halo = halo[2, layer, t] * LAP_SCALE
-            for g in range(2):
-                update = stiff * (part[g, layer + 3, t] + laps[0][g])
-                first[g, layer + 3, t] = 2.0 * here[g][t] - fields[3 + g][layer, at(t), :] + update
-                first_halo[g, layer, t] = (
-                    2.0 * there[g][t]
-                    - halo[g, layer, t]
-                    + stiff_halo * (part_halo[g, layer, t] + lat_halo[t][g] + laps[1][g])
-                )
-            sums[0, layer, t] = bulk_in[layer, at(t), :] + here[0][t] * update
-            sums[1, layer, t] = density_in[layer, at(t), :] + RHO_SCALE * (
-                part[2, layer + 3, t] + rho
-            )
+            here = [wide[f, layer + 6, t] for f in range(2)]
+            for g in range(2):
+                first_halo[g, layer, t] = spread(first_pack[g, group, t], s)
+                lap = part[g, layer + 3, t] + at_ends(own_pack[g, group, t], s, lane)
+                update = stiff * lap
+                first[g, layer + 3, t] = 2.0 * here[g] - fields[3 + g][layer, at(t), :] + update
+            sums[0, layer, t] = bulk_in[layer, at(t), :] + here[0] * update
+            rho = part[2, layer + 3, t] + at_ends(own_pack[2, group, t], s, lane)
+            sums[1, layer, t] = density_in[layer, at(t), :] + RHO_SCALE * rho
+        for e in range(3):
+            stiff = from_core[24 + e, at(t), :] * LAP_SCALE
+            for g in range(2):
+                lap = part[g, near + e, t] + at_ends(own_pack[g, groups, t], e, lane)
+                past = from_core[18 + 3 * g + e, at(t), :]
+                first[g, near + e, t] = 2.0 * wide[g, near + 3 + e, t] - past + stiff * lap
         return carry
 
-    lax.fori_loop(0, layers, own, 0)
-
-    def other(e, carry):
-        for t in range(tiles):
-            here = [wide[f, near + 3 + e, t] for f in range(3)]
-            there = [wide_halo[f, near + e, t] for f in range(3)]
-            laps, _ = longitudinal(here, there, lane, False, False)
-            stiff = from_core[24 + e, at(t), :] * LAP_SCALE
-            for g in range(2):
-                first[g, near + e, t] = (
-                    2.0 * here[g]
-                    - from_core[18 + 3 * g + e, at(t), :]
-                    + stiff * (part[g, near + e, t] + laps[0][g])
-                )
-        return carry
-
-    lax.fori_loop(0, 3, other, 0, unroll=True)
+    lax.fori_loop(0, tiles, first_at, 0)
 
     for t in inside:
         terms = radial(lambda f, k: first[f, 3 + k, t], lambda k: wide[2, 6 + k, t], layers)
         for k, term in enumerate(terms):
             for g in range(3):
-                part_halo[g, k, t] = term[g]
+                part_last[g, k, t - 1] = term[g]
 
     def last(layer, carry):
         here = [[first[f, layer + 3, t] for t in range(tiles)] for f in range(2)]
@@ -409,18 +483,18 @@
                 flux_out[k, n, layer] = flux[t][k]
         for t in inside:
             lat = lat_terms(flux, t, sub, True)
-            there = [first_halo[0, layer, t], first_halo[1, layer, t], wide_halo[2, layer + 3, t]]
+            there = [first_halo[0, layer, t], first_halo[1, layer, t], buoy_halo[layer, t]]
             laps, rho = longitudinal([x[t] for x in here], there, lane, False, True)
             stiff = fields[5][layer, at(t), :] * LAP_SCALE
             for g in range(2):
-                update = stiff * (part_halo[g, layer, t] + lat[g] + laps[0][g])
+                update = stiff * (part_last[g, layer, t - 1] + lat[g] + laps[0][g])
                 done[2 * g, layer, at(t - 1), :] = (
                     2.0 * here[g][t] - fields[g][layer, at(t), :] + update
                 )
                 done[2 * g + 1, layer, at(t - 1), :] = here[g][t]
             done[4, layer, at(t - 1), :] = sums[0, layer, t] + here[0][t] * update
             done[5, layer, at(t - 1), :] = sums[1, layer, t] + RHO_SCALE * (
-                part_halo[2, layer, t] + lat[2] + rho
+                part_last[2, layer, t - 1] + lat[2] + rho
             )
         return carry
 
@@ -429,10 +503,10 @@
 
 def last_kernel(*refs):
     fields, from_core = refs[:6], refs[6]
-    wide, first, first_halo, rest_halo, flux_in, sums, done = refs[7:14]
-    edges, from_first, from_second = refs[14:17]
-    outs = refs[17:23]
-    fixed, fixed_halo, ring_buoy, part, made, sems = refs[23:]
+    wide, first, first_pack, stiff_pack, buoy_halo, flux_in, sums, done = refs[7:15]
+    edges, from_first, from_second = refs[15:18]
+    outs = refs[18:24]
+    fixed, fixed_halo, ring_buoy, part, made, sems = refs[24:]
     layers, rows, lanes = fields[0].shape
     tiles = rows // SUB
     sub, lane = iotas(lanes)
@@ -474,15 +548,18 @@
             for n in range(2):
                 fixed[g, border + k, n] = zero
 
-    halos = three(2 * layers + 4)
-    mine = list(zip(unpack_three(edges[0], True), unpack_three(edges[1], False)))
-    side = outer(mine, halos)
-    for layer in range(layers):
+    per = lanes // SEGMENT
+    for group in range(stiff_pack.shape[0]):
+        if group % 2 == 0:
+            k = group // 2
+            mine = list(zip(unpack_three(edges[0, k], True), unpack_three(edges[1, k], False)))
+            side = outer(mine, three(2 * layers + 4 + k))
         for n, (t, mask) in enumerate(ends):
-            stiff = rest_halo[1, layer, t] * LAP_SCALE
-            for g in range(2):
-                lap = jnp.where(mask, rolled(side[n][g], -16 * layer - 6, 1), 0.0)
-                fixed_halo[g, layer, n] = first_halo[g, layer, t] + stiff * lap
+            for g in range(2):
+                lap = jnp.where(mask, unmerged(side[n][g], group), 0.0)
+                x = first_pack[g, group, t] + stiff_pack[group, t] * lap
+                for s in range(min(per, layers - group * per)):
+                    fixed_halo[g, group * per + s, n] = spread(x, s)
 
     for e in range(3):
         halos = three(2 * layers + 1 + e)
@@ -540,7 +617,7 @@
             k = (1, 4)[n]
             here = [x[k] for x in rings]
             lat = lat_terms(flux, k, sub, True)
-            there = [fixed_halo[0, layer, n], fixed_halo[1, layer, n], rest_halo[0, layer, t]]
+            there = [fixed_halo[0, layer, n], fixed_halo[1, layer, n], buoy_halo[layer, t]]
             laps, rho = longitudinal(here, there, lane, False, True)
             stiff = fields[5][layer, at(t), :] * LAP_SCALE
             for g in range(2):
@@ -610,7 +687,9 @@
     from_left = lax.ppermute(to_right, "lon", ring)
     from_right = lax.ppermute(to_left, "lon", [(b, a) for a, b in ring])
     from_core = lax.ppermute(to_core, "rad", swap)
-    lat_edge = made(2 * layers + 5, SUB, lanes)
+    pairs_of_groups = -(-groups // 2)
+    lat_edge = made(2 * layers + 4 + pairs_of_groups, SUB, lanes)
+    packs = [from_left, from_right, to_left, to_right]
     wide, part, to_first, to_second = call(
         inner_kernel,
         (
@@ -623,19 +702,20 @@
     )
     to_first, to_second, to_core, edges = call(
         turn_kernel,
-        (lat_edge, lat_edge, made(2, rows, lanes), made(2, SUB, lanes)),
-        [*fields, from_left, from_right, part, to_first, to_second],
-        input_output_aliases={9: 0, 10: 1},
+        (lat_edge, lat_edge, made(4, rows, lanes), made(2, pairs_of_groups, SUB, lanes)),
+        [*fields, *packs, part, to_first, to_second],
+        input_output_aliases={11: 0, 12: 1},
     )
     from_first = lax.ppermute(to_first, ("lat", "rad"), pairs(count, 0))
     from_second = lax.ppermute(to_second, ("lat", "rad"), pairs(count, 1))
     from_core2 = lax.ppermute(to_core, "rad", swap)
-    first, first_halo, rest_halo, flux, sums, done = call(
+    first, first_pack, stiff_pack, buoy_halo, flux, sums, done = call(
         middle_kernel,
         (
             made(2, layers + 6, tiles, SUB, lanes),
-            made(2, layers, tiles, SUB, lanes),
-            made(2, layers, tiles, SUB, lanes),
+            made(2, groups, tiles, SUB, lanes),
+            made(groups, tiles, SUB, lanes),
+            made(layers, tiles, SUB, lanes),
             made(3, 2, layers, SUB, lanes),
             made(2, layers, tiles, SUB, lanes),
             made(6, layers, rows - 2 * SUB, lanes),
@@ -644,8 +724,7 @@
             *fields,
             kernel_bulk_in,
             kernel_density_in,
-            from_left,
-            from_right,
+            *packs,
             from_core,
             from_core2,
             wide,
@@ -653,9 +732,11 @@
         ],
         cost_estimate=HEAVY,
         scratch_shapes=[
-            made(3, layers, tiles, SUB, lanes),
-            made(3, layers + 6, tiles, SUB, lanes),
-            made(3, layers, tiles, SUB, lanes),
+            made(2, layers, tiles, SUB, lanes),
+            made(3, groups + 1, tiles, SUB, lanes),
+            made(3, layers, tiles - 2, SUB, lanes),
+            made(3, groups, tiles, SUB, lanes),
+            made(2, groups, tiles, SUB, lanes),
         ],
     )
     return call(
@@ -666,8 +747,9 @@
             from_core,
             wide,
             first,
-            first_halo,
-            rest_halo,
+            first_pack,
+            stiff_pack,
+            buoy_halo,
             flux,
             sums,
             done,

time: 18.4 us -> 17.5 us (0.951)
  waiting for transfers between devices: 2.86 us -> 1.72 us
    ppermute x1, waiting for transfers between devices: 0.74 us -> 0.01 us  [shards(): from_left = lax.ppermute(to_right, 'lon', ring)]
    ppermute x1, waiting for transfers between devices: 2.11 us -> 1.7 us  [shards(): from_right = lax.ppermute(to_left, 'lon', [(b, a) for a, b in ring])]
  transfers between devices with their start and end apart: 6 -> 6, of which waited for: 2 -> 1; matrix products, arithmetic and copies ran while one was open for 0% -> 0% of each run, Pallas kernels for 24% -> 26%
where the time goes in v4:
time: 17.5 us; the launch traced here: 17.2 us
  Pallas kernels  8.43 us (48%)
  starting transfers between devices  6.37 us (36%)
  waiting for transfers between devices  1.72 us (10%)
  between operations  0.7 us (4%)
    pallas_call x5, Pallas kernels, call(): pl.pallas_call(kernel, out_shape=out_shape, in_specs=in_specs or [VMEM] *...  8.43 us
    ppermute x1, starting transfers between devices, shards(): from_second = lax.ppermute(to_second, ('lat', 'rad'), pairs(count, 1))  2.42 us
    ppermute x1, waiting for transfers between devices, shards(): from_right = lax.ppermute(to_left, 'lon', [(b, a) for a, b in ring])  1.7 us
    ppermute x1, starting transfers between devices, shards(): from_core2 = lax.ppermute(to_core, 'rad', swap)  1.56 us
    ppermute x1, starting transfers between devices, shards(): from_left = lax.ppermute(to_right, 'lon', ring)  1.21 us
    ppermute x1, starting transfers between devices, shards(): from_core = lax.ppermute(to_core, 'rad', swap)  0.74 us
  transfers between devices with their start and end apart: 6, of which 1 were waited for; matrix products, arithmetic and copies ran while one was open for 0% of the time, Pallas kernels for 26%

profile of v4, /device:TPU:11, one launch (start us, length us, event | category | flops | bytes accessed | tf_op | source)
XLA Modules:
  0.0 17.2 jit_solution(17583479625557265540)
XLA Ops:
  0.6 1.6 %shard_map.127 = (f32[8,32,128]{2,1,0:T(8,128)S(1)}, f32[8,32,128]{2,1,0:T(8,128)S(1)}, f32[8,32,128]{2,1,0:T(8,128)S(1)}, f32[8,32,128]{2,1,0:T(8,128)S(1)}, f3...) custom-call(f32[8,32,128]{2,1,0:T(8,128)} %refs_0_.1, ...), custom_call_target="tpu_custom_call" | custom-call | tf_op jit(solution)/shard_map/pallas_call | solution.py:653
  2.2 0.7 %collective-permute-start = (f32[27,32,128]{2,1,0:T(8,128)S(1)}, f32[27,32,128]{2,1,0:T(8,128)S(1)}, u32[]{:S(2)}, u32[]{:S(2)}) collective-permute-start(f32[27,32,128]{2,1,0:T(8,128)S(1)} %get-tuple-element.36), channel_id=1, source_target_pairs={{0,1},{1,0},{2,3},{3,2},{4,5},{5,4},{6,7},{7,6},{8,9},{9,8},{10,11... | collective-permute-start | bytes 1327112 | tf_op jit(solution)/shard_map/ppermute | solution.py:689
  3.0 1.2 %collective-permute-start.1 = (f32[2,32,128]{2,1,0:T(8,128)S(1)}, f32[2,32,128]{2,1,0:T(8,128)S(1)}, u32[]{:S(2)}, u32[]{:S(2)}) collective-permute-start(f32[2,32,128]{2,1,0:T(8,128)S(1)} %get-tuple-element.38.refs_9_.refs_11_), channel_id=1, source_target_pairs={{0,8},{8,16},{16,24},{24,0},{1,9},{9,17},{17,25},{25,1},{2,10},{10... | collective-permute-start | bytes 98312 | tf_op jit(solution)/shard_map/ppermute | solution.py:687
  4.2 0.3 %collective-permute-start.2 = (f32[2,32,128]{2,1,0:T(8,128)S(1)}, f32[2,32,128]{2,1,0:T(8,128)S(1)}, u32[]{:S(2)}, u32[]{:S(2)}) collective-permute-start(f32[2,32,128]{2,1,0:T(8,128)S(1)} %get-tuple-element.39.refs_8_.refs_10_), channel_id=1, source_target_pairs={{8,0},{16,8},{24,16},{0,24},{9,1},{17,9},{25,17},{1,25},{10,2},{18... | collective-permute-start | bytes 98312 | tf_op jit(solution)/shard_map/ppermute | solution.py:688
  4.4 0.0 collective-permute-done.refs_6_.refs_12_
  4.4 1.7 %shard_map.128 = (f32[3,20,4,8,128]{4,3,2,1,0:T(8,128)S(1)}, f32[3,14,4,8,128]{4,3,2,1,0:T(8,128)S(1)}, f32[21,8,128]{2,1,0:T(8,128)S(1)}, f32[21,8,128]{2,1,0:T(8,128)S(1)}) custom-call(f32[8,32,128]{2,1,0:T(8,128)S(1)} %get-tuple-element.30.refs_0_, f32[8,32,128]{2,1,0:T(8,128)S(1)} %get-tuple-element.31.refs_1_, ...), custom_call_target="tpu_custom_call" | custom-call | tf_op jit(solution)/shard_map/pallas_call | solution.py:653
  6.1 0.0 collective-permute-done.1.refs_6_.refs_8_
  6.1 1.7 %collective-permute-done.2.refs_7_.refs_9_ = f32[2,32,128]{2,1,0:T(8,128)S(1)} collective-permute-done((f32[2,32,128]{2,1,0:T(8,128)S(1)}, f32[2,32,128]{2,1,0:T(8,128)S(1)}, u32[]{:S(2)}, u32[]{:S(2)}) %collective-permute-start.2) | collective-permute-done | bytes 32800 | tf_op jit(solution)/shard_map/ppermute | solution.py:688
  7.8 0.0 copy-start
  7.8 0.0 copy-start.1
  7.8 0.3 %shard_map.129 = (f32[21,8,128]{2,1,0:T(8,128)S(1)}, f32[21,8,128]{2,1,0:T(8,128)S(1)}, f32[4,32,128]{2,1,0:T(8,128)S(1)}, f32[2,1,8,128]{3,2,1,0:T(8,128)S(1)}) custom-call(f32[8,32,128]{2,1,0:T(8,128)S(1)} %get-tuple-element.30.refs_0_, f32[8,32,128]{2,1,0:T(8,128)S(1)} %get-tuple-element.31.refs_1_, ...), custom_call_target="tpu_custom_call", output_to_operand_aliasing={{0}: (11, {}), {1}: (12, {})} | custom-call | tf_op jit(solution)/shard_map/pallas_call | solution.py:653
  8.2 1.6 %collective-permute-start.3 = (f32[4,32,128]{2,1,0:T(8,128)S(1)}, f32[4,32,128]{2,1,0:T(8,128)S(1)}, u32[]{:S(2)}, u32[]{:S(2)}) collective-permute-start(f32[4,32,128]{2,1,0:T(8,128)S(1)} %get-tuple-element.43), channel_id=1, source_target_pairs={{0,1},{1,0},{2,3},{3,2},{4,5},{5,4},{6,7},{7,6},{8,9},{9,8},{10,11... | collective-permute-start | bytes 196616 | tf_op jit(solution)/shard_map/ppermute | solution.py:711
  9.8 0.2 %collective-permute-start.4 = (f32[21,8,128]{2,1,0:T(8,128)S(1)}, f32[21,8,128]{2,1,0:T(8,128)S(1)}, u32[]{:S(2)}, u32[]{:S(2)}) collective-permute-start(f32[21,8,128]{2,1,0:T(8,128)S(1)} %get-tuple-element.52), channel_id=1, source_target_pairs={{0,2},{1,3},{2,0},{3,1},{4,6},{5,7},{6,4},{7,5},{8,10},{9,11},{10,... | collective-permute-start | bytes 258056 | tf_op jit(solution)/shard_map/ppermute | solution.py:709
  9.9 2.4 %collective-permute-start.5 = (f32[21,8,128]{2,1,0:T(8,128)S(1)}, f32[21,8,128]{2,1,0:T(8,128)S(1)}, u32[]{:S(2)}, u32[]{:S(2)}) collective-permute-start(f32[21,8,128]{2,1,0:T(8,128)S(1)} %get-tuple-element.53), channel_id=1, source_target_pairs={{0,1},{1,0},{2,4},{3,5},{4,2},{5,3},{6,7},{7,6},{8,9},{9,8},{10,12... | collective-permute-start | bytes 258056 | tf_op jit(solution)/shard_map/ppermute | solution.py:710
  12.4 0.0 collective-permute-done.3.refs_13_
  12.4 0.0 copy-done
  12.4 0.0 copy-done.1
  12.4 2.8 %shard_map.130 = (f32[2,14,4,8,128]{4,3,2,1,0:T(8,128)S(1)}, f32[2,2,4,8,128]{4,3,2,1,0:T(8,128)S(1)}, f32[2,4,8,128]{3,2,1,0:T(8,128)S(1)}, f32[8,4,8,128]{3,2,...) custom-call(f32[8,32,128]{2,1,0:T(8,128)S(1)} %get-tuple-element.30., ...), custom_call_target="tpu_custom_call" | custom-call | flops 4000000000 | bytes 1000000 | tf_op jit(solution)/shard_map/pallas_call | solution.py:653
  15.2 0.0 collective-permute-done.4.refs_16_
  15.2 0.0 collective-permute-done.5.refs_17_
  15.2 2.0 %shard_map.131 = (f32[8,32,128]{2,1,0:T(8,128)}, f32[8,32,128]{2,1,0:T(8,128)}, f32[8,32,128]{2,1,0:T(8,128)}, f32[8,32,128]{2,1,0:T(8,128)}, f32[8,32,128]{2,1,0:T(8,128)}, /*index=5*/f32[8,32,128]{2,1,0:T(8,128)}) custom-call(f32[8,32,128]{2,1,0:T(8,128)S(1)} %get-tuple-element.30.refs_0_, f32[8,32,128]{2,1,0:T(8,128)S(1)} %get-tuple-element.31.refs_1_, ...), custom_call_target="tpu_custom_call" | custom-call | tf_op jit(solution)/shard_map/pallas_call | solution.py:653
Async XLA Ops:
  2.2 2.2 %collective-permute-start = (f32[27,32,128]{2,1,0:T(8,128)S(1)}, f32[27,32,128]{2,1,0:T(8,128)S(1)}, u32[]{:S(2)}, u32[]{:S(2)}) collective-permute-start(f32[27,32,128]{2,1,0:T(8,128)S(1)} %get-tuple-element.36), channel_id=1, source_target_pairs={{0,1},{1,0},{2,3},{3,2},{4,5},{5,4},{6,7},{7,6},{8,9},{9,8},{10,11... | collective-permute-start | bytes 1327112 | tf_op jit(solution)/shard_map/ppermute | solution.py:689
  3.0 3.2 %collective-permute-start.1 = (f32[2,32,128]{2,1,0:T(8,128)S(1)}, f32[2,32,128]{2,1,0:T(8,128)S(1)}, u32[]{:S(2)}, u32[]{:S(2)}) collective-permute-start(f32[2,32,128]{2,1,0:T(8,128)S(1)} %get-tuple-element.38.refs_9_.refs_11_), channel_id=1, source_target_pairs={{0,8},{8,16},{16,24},{24,0},{1,9},{9,17},{17,25},{25,1},{2,10},{10... | collective-permute-start | bytes 98312 | tf_op jit(solution)/shard_map/ppermute | solution.py:687
  4.2 3.7 %collective-permute-start.2 = (f32[2,32,128]{2,1,0:T(8,128)S(1)}, f32[2,32,128]{2,1,0:T(8,128)S(1)}, u32[]{:S(2)}, u32[]{:S(2)}) collective-permute-start(f32[2,32,128]{2,1,0:T(8,128)S(1)} %get-tuple-element.39.refs_8_.refs_10_), channel_id=1, source_target_pairs={{8,0},{16,8},{24,16},{0,24},{9,1},{17,9},{25,17},{1,25},{10,2},{18... | collective-permute-start | bytes 98312 | tf_op jit(solution)/shard_map/ppermute | solution.py:688
  7.8 4.5 %copy-start = (f32[8,32,128]{2,1,0:T(8,128)S(1)}, f32[8,32,128]{2,1,0:T(8,128)}, u32[]{:S(2)}) copy-start(f32[8,32,128]{2,1,0:T(8,128)} %refs_6_.1) | copy-start | bytes 393220
  7.8 4.5 %copy-start.1 = (f32[8,32,128]{2,1,0:T(8,128)S(1)}, f32[8,32,128]{2,1,0:T(8,128)}, u32[]{:S(2)}) copy-start(f32[8,32,128]{2,1,0:T(8,128)} %refs_7_.1) | copy-start | bytes 393220
  8.2 4.2 %collective-permute-start.3 = (f32[4,32,128]{2,1,0:T(8,128)S(1)}, f32[4,32,128]{2,1,0:T(8,128)S(1)}, u32[]{:S(2)}, u32[]{:S(2)}) collective-permute-start(f32[4,32,128]{2,1,0:T(8,128)S(1)} %get-tuple-element.43), channel_id=1, source_target_pairs={{0,1},{1,0},{2,3},{3,2},{4,5},{5,4},{6,7},{7,6},{8,9},{9,8},{10,11... | collective-permute-start | bytes 196616 | tf_op jit(solution)/shard_map/ppermute | solution.py:711
  9.8 5.4 %collective-permute-start.4 = (f32[21,8,128]{2,1,0:T(8,128)S(1)}, f32[21,8,128]{2,1,0:T(8,128)S(1)}, u32[]{:S(2)}, u32[]{:S(2)}) collective-permute-start(f32[21,8,128]{2,1,0:T(8,128)S(1)} %get-tuple-element.52), channel_id=1, source_target_pairs={{0,2},{1,3},{2,0},{3,1},{4,6},{5,7},{6,4},{7,5},{8,10},{9,11},{10,... | collective-permute-start | bytes 258056 | tf_op jit(solution)/shard_map/ppermute | solution.py:709
  9.9 5.2 %collective-permute-start.5 = (f32[21,8,128]{2,1,0:T(8,128)S(1)}, f32[21,8,128]{2,1,0:T(8,128)S(1)}, u32[]{:S(2)}, u32[]{:S(2)}) collective-permute-start(f32[21,8,128]{2,1,0:T(8,128)S(1)} %get-tuple-element.53), channel_id=1, source_target_pairs={{0,1},{1,0},{2,4},{3,5},{4,2},{5,3},{6,7},{7,6},{8,9},{9,8},{10,12... | collective-permute-start | bytes 258056 | tf_op jit(solution)/shard_map/ppermute | solution.py:710

commit v5 on v4

--- a/solution.py
+++ b/solution.py
@@ -261,7 +261,7 @@
 
 def inner_kernel(*refs):
     fields, from_core = refs[:6], refs[6]
-    wide, part, to_first, to_second = refs[7:]
+    wide, part, to_first, to_second, to_third = refs[7:]
     layers, rows, lanes = fields[0].shape
     tiles = rows // SUB
     sub, lane = iotas(lanes)
@@ -284,7 +284,7 @@
                 wide[f, border + 3 + k, t] = zero
 
     def send(k, low, high):
-        to_first[k] = jnp.where(even, high, low)
+        to_first[k] = to_third[k] = jnp.where(even, high, low)
         to_second[k] = jnp.where(even, low, high)
 
     ends = ((0, True), (tiles - 1, False))
@@ -338,7 +338,7 @@
 
 def turn_kernel(*refs):
     fields, packs, part = refs[:6], refs[6:10], refs[10]
-    to_first, to_second, to_core, edges = refs[13:]
+    to_first, to_second, to_third, to_core, edges = refs[14:]
     layers, rows, lanes = fields[0].shape
     tiles = rows // SUB
     sub, lane = iotas(lanes)
@@ -349,7 +349,7 @@
     groups = packs[0].shape[0]
 
     def send(k, low, high):
-        to_first[k] = jnp.where(even, high, low)
+        to_first[k] = to_third[k] = jnp.where(even, high, low)
         to_second[k] = jnp.where(even, low, high)
 
     def ends(ref, *index):
@@ -504,9 +504,9 @@
 def last_kernel(*refs):
     fields, from_core = refs[:6], refs[6]
     wide, first, first_pack, stiff_pack, buoy_halo, flux_in, sums, done = refs[7:15]
-    edges, from_first, from_second = refs[15:18]
-    outs = refs[18:24]
-    fixed, fixed_halo, ring_buoy, part, made, sems = refs[24:]
+    edges, from_first, from_second, from_third = refs[15:19]
+    outs = refs[19:25]
+    fixed, fixed_halo, ring_buoy, part, made, sems = refs[25:]
     layers, rows, lanes = fields[0].shape
     tiles = rows // SUB
     sub, lane = iotas(lanes)
@@ -527,7 +527,8 @@
         return pl.ds(t * SUB, SUB)
 
     def received(k):
-        one, two = from_first[k], from_second[k]
+        one = jnp.where(place % 4 < 2, from_first[k], from_third[k])
+        two = from_second[k]
         behind, ahead = jnp.where(even, two, one), jnp.where(even, one, two)
         return jnp.where(place > 0, behind, 0.0), jnp.where(place < count - 1, ahead, 0.0)
 
@@ -638,9 +639,9 @@
         copy.wait()
 
 
-def pairs(count, start):
+def pairs(count, start, step):
     partner = {i: i for i in range(count)}
-    for i in range(start, count - 1, 2):
+    for i in range(start, count - 1, step):
         partner[i], partner[i + 1] = i + 1, i
     return [
         (2 * i + core, 2 * j + (core if i != j else 1 - core))
@@ -690,24 +691,26 @@
     pairs_of_groups = -(-groups // 2)
     lat_edge = made(2 * layers + 4 + pairs_of_groups, SUB, lanes)
     packs = [from_left, from_right, to_left, to_right]
-    wide, part, to_first, to_second = call(
+    wide, part, to_first, to_second, to_third = call(
         inner_kernel,
         (
             made(3, layers + 12, tiles, SUB, lanes),
             made(3, layers + 6, tiles, SUB, lanes),
             lat_edge,
             lat_edge,
+            lat_edge,
         ),
         [*fields, from_core],
     )
-    to_first, to_second, to_core, edges = call(
+    to_first, to_second, to_third, to_core, edges = call(
         turn_kernel,
-        (lat_edge, lat_edge, made(4, rows, lanes), made(2, pairs_of_groups, SUB, lanes)),
-        [*fields, *packs, part, to_first, to_second],
-        input_output_aliases={11: 0, 12: 1},
+        (lat_edge, lat_edge, lat_edge, made(4, rows, lanes), made(2, pairs_of_groups, SUB, lanes)),
+        [*fields, *packs, part, to_first, to_second, to_third],
+        input_output_aliases={11: 0, 12: 1, 13: 2},
     )
-    from_first = lax.ppermute(to_first, ("lat", "rad"), pairs(count, 0))
-    from_second = lax.ppermute(to_second, ("lat", "rad"), pairs(count, 1))
+    from_first = lax.ppermute(to_first, ("lat", "rad"), pairs(count, 0, 4))
+    from_second = lax.ppermute(to_second, ("lat", "rad"), pairs(count, 1, 2))
+    from_third = lax.ppermute(to_third, ("lat", "rad"), pairs(count, 2, 4))
     from_core2 = lax.ppermute(to_core, "rad", swap)
     first, first_pack, stiff_pack, buoy_halo, flux, sums, done = call(
         middle_kernel,
@@ -756,6 +759,7 @@
             edges,
             from_first,
             from_second,
+            from_third,
         ],
         out_specs=(hbm,) * 6,
         scratch_shapes=[

time: 17.5 us -> 16.9 us (0.966)
  starting transfers between devices: 6.37 us -> 5.85 us
    ppermute x2 -> x3, starting transfers between devices: 2.61 us -> 2.09 us  [the longest x1 1.19 us: shards(): from_second = lax.ppermute(to_second, ('lat', 'rad'), pairs(count, 1, 2))]
  transfers between devices with their start and end apart: 6 -> 7, of which waited for: 1 -> 1; matrix products, arithmetic and copies ran while one was open for 0% -> 0% of each run, Pallas kernels for 26% -> 27%
where the time goes in v5:
time: 16.9 us; the launch traced here: 16.7 us
  Pallas kernels  8.44 us (50%)
  starting transfers between devices  5.85 us (35%)
  waiting for transfers between devices  1.72 us (10%)
  between operations  0.71 us (4%)
    pallas_call x5, Pallas kernels, call(): pl.pallas_call(kernel, out_shape=out_shape, in_specs=in_specs or [VMEM] *...  8.44 us
    ppermute x1, waiting for transfers between devices, shards(): from_right = lax.ppermute(to_left, 'lon', [(b, a) for a, b in ring])  1.7 us
    ppermute x1, starting transfers between devices, shards(): from_core2 = lax.ppermute(to_core, 'rad', swap)  1.56 us
    ppermute x1, starting transfers between devices, shards(): from_left = lax.ppermute(to_right, 'lon', ring)  1.21 us
    ppermute x1, starting transfers between devices, shards(): from_second = lax.ppermute(to_second, ('lat', 'rad'), pairs(count, 1, 2))  1.19 us
    ppermute x1, starting transfers between devices, shards(): from_core = lax.ppermute(to_core, 'rad', swap)  0.74 us
    ppermute x1, starting transfers between devices, shards(): from_third = lax.ppermute(to_third, ('lat', 'rad'), pairs(count, 2, 4))  0.71 us
  transfers between devices with their start and end apart: 7, of which 1 were waited for; matrix products, arithmetic and copies ran while one was open for 0% of the time, Pallas kernels for 27%

profile of v5, /device:TPU:11, one launch (start us, length us, event | category | flops | bytes accessed | tf_op | source)
XLA Modules:
  0.0 16.7 jit_solution(9011329052148086359)
XLA Ops:
  0.6 1.6 %shard_map.127 = (f32[8,32,128]{2,1,0:T(8,128)S(1)}, f32[8,32,128]{2,1,0:T(8,128)S(1)}, f32[8,32,128]{2,1,0:T(8,128)S(1)}, f32[8,32,128]{2,1,0:T(8,128)S(1)}, f3...) custom-call(f32[8,32,128]{2,1,0:T(8,128)} %refs_0_.1, ...), custom_call_target="tpu_custom_call" | custom-call | tf_op jit(solution)/shard_map/pallas_call | solution.py:654
  2.2 0.7 %collective-permute-start = (f32[27,32,128]{2,1,0:T(8,128)S(1)}, f32[27,32,128]{2,1,0:T(8,128)S(1)}, u32[]{:S(2)}, u32[]{:S(2)}) collective-permute-start(f32[27,32,128]{2,1,0:T(8,128)S(1)} %get-tuple-element.38), channel_id=1, source_target_pairs={{0,1},{1,0},{2,3},{3,2},{4,5},{5,4},{6,7},{7,6},{8,9},{9,8},{10,11... | collective-permute-start | bytes 1327112 | tf_op jit(solution)/shard_map/ppermute | solution.py:690
  3.0 1.2 %collective-permute-start.1 = (f32[2,32,128]{2,1,0:T(8,128)S(1)}, f32[2,32,128]{2,1,0:T(8,128)S(1)}, u32[]{:S(2)}, u32[]{:S(2)}) collective-permute-start(f32[2,32,128]{2,1,0:T(8,128)S(1)} %get-tuple-element.40.refs_9_.refs_11_), channel_id=1, source_target_pairs={{0,8},{8,16},{16,24},{24,0},{1,9},{9,17},{17,25},{25,1},{2,10},{10... | collective-permute-start | bytes 98312 | tf_op jit(solution)/shard_map/ppermute | solution.py:688
  4.2 0.3 %collective-permute-start.2 = (f32[2,32,128]{2,1,0:T(8,128)S(1)}, f32[2,32,128]{2,1,0:T(8,128)S(1)}, u32[]{:S(2)}, u32[]{:S(2)}) collective-permute-start(f32[2,32,128]{2,1,0:T(8,128)S(1)} %get-tuple-element.41.refs_8_.refs_10_), channel_id=1, source_target_pairs={{8,0},{16,8},{24,16},{0,24},{9,1},{17,9},{25,17},{1,25},{10,2},{18... | collective-permute-start | bytes 98312 | tf_op jit(solution)/shard_map/ppermute | solution.py:689
  4.4 0.0 collective-permute-done.refs_6_.refs_12_
  4.4 1.7 %shard_map.128 = (f32[3,20,4,8,128]{4,3,2,1,0:T(8,128)S(1)}, f32[3,14,4,8,128]{4,3,2,1,0:T(8,128)S(1)}, f32[21,8,128]{2,1,0:T(8,128)S(1)}, f32[21,8,128]{2,1,0:T(8,128)S(1)}, f32[21,8,128]{2,1,0:T(8,128)S(1)}) custom-call(f32[8,32,128]{2,1,0:T(8,128)S(1)} %get-tuple-element.32.refs_0_, f32[8,32,128]{2,1,0:T(8,128)S(1)} %get-tuple-element.33.refs_1_, ...), custom_call_target="tpu_custom_call" | custom-call | tf_op jit(solution)/shard_map/pallas_call | solution.py:654
  6.1 0.0 collective-permute-done.1.refs_6_.refs_8_
  6.1 1.7 %collective-permute-done.2.refs_7_.refs_9_ = f32[2,32,128]{2,1,0:T(8,128)S(1)} collective-permute-done((f32[2,32,128]{2,1,0:T(8,128)S(1)}, f32[2,32,128]{2,1,0:T(8,128)S(1)}, u32[]{:S(2)}, u32[]{:S(2)}) %collective-permute-start.2) | collective-permute-done | bytes 32800 | tf_op jit(solution)/shard_map/ppermute | solution.py:689
  7.8 0.0 copy-start
  7.8 0.0 copy-start.1
  7.8 0.3 %shard_map.129 = (f32[21,8,128]{2,1,0:T(8,128)S(1)}, f32[21,8,128]{2,1,0:T(8,128)S(1)}, f32[21,8,128]{2,1,0:T(8,128)S(1)}, f32[4,32,128]{2,1,0:T(8,128)S(1)}, f32[2,1,8,128]{3,2,1,0:T(8,128)S(1)}) custom-call(f32[8,32,128]{2,1,0:T(8,128)S(1)} %get-tuple-element.32.refs_0_, ...), custom_call_target="tpu_custom_call", output_to_operand_aliasing={{0}: (11, {}), {1}: (12, {}), {2}: (13, {})} | custom-call | tf_op jit(solution)/shard_map/pallas_call | solution.py:654
  8.2 1.6 %collective-permute-start.3 = (f32[4,32,128]{2,1,0:T(8,128)S(1)}, f32[4,32,128]{2,1,0:T(8,128)S(1)}, u32[]{:S(2)}, u32[]{:S(2)}) collective-permute-start(f32[4,32,128]{2,1,0:T(8,128)S(1)} %get-tuple-element.46), channel_id=1, source_target_pairs={{0,1},{1,0},{2,3},{3,2},{4,5},{5,4},{6,7},{7,6},{8,9},{9,8},{10,11... | collective-permute-start | bytes 196616 | tf_op jit(solution)/shard_map/ppermute | solution.py:714
  9.8 0.2 %collective-permute-start.4 = (f32[21,8,128]{2,1,0:T(8,128)S(1)}, f32[21,8,128]{2,1,0:T(8,128)S(1)}, u32[]{:S(2)}, u32[]{:S(2)}) collective-permute-start(f32[21,8,128]{2,1,0:T(8,128)S(1)} %get-tuple-element.55), channel_id=1, source_target_pairs={{0,2},{1,3},{2,0},{3,1},{4,5},{5,4},{6,7},{7,6},{8,10},{9,11},{10,... | collective-permute-start | bytes 258056 | tf_op jit(solution)/shard_map/ppermute | solution.py:711
  9.9 1.2 %collective-permute-start.5 = (f32[21,8,128]{2,1,0:T(8,128)S(1)}, f32[21,8,128]{2,1,0:T(8,128)S(1)}, u32[]{:S(2)}, u32[]{:S(2)}) collective-permute-start(f32[21,8,128]{2,1,0:T(8,128)S(1)} %get-tuple-element.56), channel_id=1, source_target_pairs={{0,1},{1,0},{2,4},{3,5},{4,2},{5,3},{6,7},{7,6},{8,9},{9,8},{10,12... | collective-permute-start | bytes 258056 | tf_op jit(solution)/shard_map/ppermute | solution.py:712
  11.1 0.7 %collective-permute-start.6 = (f32[21,8,128]{2,1,0:T(8,128)S(1)}, f32[21,8,128]{2,1,0:T(8,128)S(1)}, u32[]{:S(2)}, u32[]{:S(2)}) collective-permute-start(f32[21,8,128]{2,1,0:T(8,128)S(1)} %get-tuple-element.57), channel_id=1, source_target_pairs={{0,1},{1,0},{2,3},{3,2},{4,6},{5,7},{6,4},{7,5},{8,9},{9,8},{10,11... | collective-permute-start | bytes 258056 | tf_op jit(solution)/shard_map/ppermute | solution.py:713
  11.8 0.0 collective-permute-done.3.refs_13_
  11.9 0.0 copy-done
  11.9 0.0 copy-done.1
  11.9 2.8 %shard_map.130 = (f32[2,14,4,8,128]{4,3,2,1,0:T(8,128)S(1)}, f32[2,2,4,8,128]{4,3,2,1,0:T(8,128)S(1)}, f32[2,4,8,128]{3,2,1,0:T(8,128)S(1)}, f32[8,4,8,128]{3,2,...) custom-call(f32[8,32,128]{2,1,0:T(8,128)S(1)} %get-tuple-element.32., ...), custom_call_target="tpu_custom_call" | custom-call | flops 4000000000 | bytes 1000000 | tf_op jit(solution)/shard_map/pallas_call | solution.py:654
  14.7 0.0 collective-permute-done.4.refs_16_
  14.7 0.0 collective-permute-done.5.refs_17_
  14.7 0.0 collective-permute-done.6.refs_18_
  14.7 2.0 %shard_map.131 = (f32[8,32,128]{2,1,0:T(8,128)}, f32[8,32,128]{2,1,0:T(8,128)}, f32[8,32,128]{2,1,0:T(8,128)}, f32[8,32,128]{2,1,0:T(8,128)}, f32[8,32,128]{2,1,0:T(8,128)}, /*index=5*/f32[8,32,128]{2,1,0:T(8,128)}) custom-call(f32[8,32,128]{2,1,0:T(8,128)S(1)} %get-tuple-element.32.refs_0_, f32[8,32,128]{2,1,0:T(8,128)S(1)} %get-tuple-element.33.refs_1_, ...), custom_call_target="tpu_custom_call" | custom-call | tf_op jit(solution)/shard_map/pallas_call | solution.py:654
Async XLA Ops:
  2.2 2.2 %collective-permute-start = (f32[27,32,128]{2,1,0:T(8,128)S(1)}, f32[27,32,128]{2,1,0:T(8,128)S(1)}, u32[]{:S(2)}, u32[]{:S(2)}) collective-permute-start(f32[27,32,128]{2,1,0:T(8,128)S(1)} %get-tuple-element.38), channel_id=1, source_target_pairs={{0,1},{1,0},{2,3},{3,2},{4,5},{5,4},{6,7},{7,6},{8,9},{9,8},{10,11... | collective-permute-start | bytes 1327112 | tf_op jit(solution)/shard_map/ppermute | solution.py:690
  3.0 3.2 %collective-permute-start.1 = (f32[2,32,128]{2,1,0:T(8,128)S(1)}, f32[2,32,128]{2,1,0:T(8,128)S(1)}, u32[]{:S(2)}, u32[]{:S(2)}) collective-permute-start(f32[2,32,128]{2,1,0:T(8,128)S(1)} %get-tuple-element.40.refs_9_.refs_11_), channel_id=1, source_target_pairs={{0,8},{8,16},{16,24},{24,0},{1,9},{9,17},{17,25},{25,1},{2,10},{10... | collective-permute-start | bytes 98312 | tf_op jit(solution)/shard_map/ppermute | solution.py:688
  4.2 3.7 %collective-permute-start.2 = (f32[2,32,128]{2,1,0:T(8,128)S(1)}, f32[2,32,128]{2,1,0:T(8,128)S(1)}, u32[]{:S(2)}, u32[]{:S(2)}) collective-permute-start(f32[2,32,128]{2,1,0:T(8,128)S(1)} %get-tuple-element.41.refs_8_.refs_10_), channel_id=1, source_target_pairs={{8,0},{16,8},{24,16},{0,24},{9,1},{17,9},{25,17},{1,25},{10,2},{18... | collective-permute-start | bytes 98312 | tf_op jit(solution)/shard_map/ppermute | solution.py:689
  7.8 4.0 %copy-start = (f32[8,32,128]{2,1,0:T(8,128)S(1)}, f32[8,32,128]{2,1,0:T(8,128)}, u32[]{:S(2)}) copy-start(f32[8,32,128]{2,1,0:T(8,128)} %refs_6_.1) | copy-start | bytes 393220
  7.8 4.0 %copy-start.1 = (f32[8,32,128]{2,1,0:T(8,128)S(1)}, f32[8,32,128]{2,1,0:T(8,128)}, u32[]{:S(2)}) copy-start(f32[8,32,128]{2,1,0:T(8,128)} %refs_7_.1) | copy-start | bytes 393220
  8.2 3.7 %collective-permute-start.3 = (f32[4,32,128]{2,1,0:T(8,128)S(1)}, f32[4,32,128]{2,1,0:T(8,128)S(1)}, u32[]{:S(2)}, u32[]{:S(2)}) collective-permute-start(f32[4,32,128]{2,1,0:T(8,128)S(1)} %get-tuple-element.46), channel_id=1, source_target_pairs={{0,1},{1,0},{2,3},{3,2},{4,5},{5,4},{6,7},{7,6},{8,9},{9,8},{10,11... | collective-permute-start | bytes 196616 | tf_op jit(solution)/shard_map/ppermute | solution.py:714
  9.8 4.9 %collective-permute-start.4 = (f32[21,8,128]{2,1,0:T(8,128)S(1)}, f32[21,8,128]{2,1,0:T(8,128)S(1)}, u32[]{:S(2)}, u32[]{:S(2)}) collective-permute-start(f32[21,8,128]{2,1,0:T(8,128)S(1)} %get-tuple-element.55), channel_id=1, source_target_pairs={{0,2},{1,3},{2,0},{3,1},{4,5},{5,4},{6,7},{7,6},{8,10},{9,11},{10,... | collective-permute-start | bytes 258056 | tf_op jit(solution)/shard_map/ppermute | solution.py:711
  9.9 4.7 %collective-permute-start.5 = (f32[21,8,128]{2,1,0:T(8,128)S(1)}, f32[21,8,128]{2,1,0:T(8,128)S(1)}, u32[]{:S(2)}, u32[]{:S(2)}) collective-permute-start(f32[21,8,128]{2,1,0:T(8,128)S(1)} %get-tuple-element.56), channel_id=1, source_target_pairs={{0,1},{1,0},{2,4},{3,5},{4,2},{5,3},{6,7},{7,6},{8,9},{9,8},{10,12... | collective-permute-start | bytes 258056 | tf_op jit(solution)/shard_map/ppermute | solution.py:712
  11.1 3.5 %collective-permute-start.6 = (f32[21,8,128]{2,1,0:T(8,128)S(1)}, f32[21,8,128]{2,1,0:T(8,128)S(1)}, u32[]{:S(2)}, u32[]{:S(2)}) collective-permute-start(f32[21,8,128]{2,1,0:T(8,128)S(1)} %get-tuple-element.57), channel_id=1, source_target_pairs={{0,1},{1,0},{2,3},{3,2},{4,6},{5,7},{6,4},{7,5},{8,9},{9,8},{10,11... | collective-permute-start | bytes 258056 | tf_op jit(solution)/shard_map/ppermute | solution.py:713

commit v6 on v5

--- a/solution.py
+++ b/solution.py
@@ -142,28 +142,28 @@
 def windows(from_left, from_right, to_left, to_right, f, seg):
     offset = OFFSETS[f]
     mask = (seg >= offset) & (seg < offset + WIDTHS[f])
-    return (
-        rolled(jnp.where(mask, from_left, to_left), -offset, 1),
-        rolled(jnp.where(mask, to_right, from_right), -offset, 1),
-    )
-
-
-def lon_flux(adj, fwd, buoy):
-    face = buoy + rolled(buoy, -1, 1)
-    grads = [slope(rolled(x, -1, 1), x, rolled(x, -2, 1), rolled(x, 1, 1)) for x in (adj, fwd)]
+    return jnp.where(mask, from_left, to_left), jnp.where(mask, to_right, from_right)
+
+
+def lon_flux(fields, offsets):
+    def shift(f, by):
+        return rolled(fields[f], -offsets[f] - by, 1)
+
+    face = shift(2, 0) + shift(2, 1)
+    grads = [slope(shift(f, 1), shift(f, 0), shift(f, 2), shift(f, -1)) for f in range(2)]
     flux = [face * g for g in grads]
     return flux[0], flux[1], flux[0] * grads[1]
 
 
-def lon_terms(adj, fwd, buoy, want_rho):
-    flux = lon_flux(adj, fwd, buoy)
+def lon_terms(fields, want_rho, offsets=(0, 0, 0)):
+    flux = lon_flux(fields, offsets)
     terms = [slope(x, rolled(x, 1, 1), rolled(x, -1, 1), rolled(x, 2, 1)) for x in flux[:2]]
     return terms + [flux[2] + rolled(flux[2], 1, 1)] if want_rho else terms
 
 
-def edge_terms(wins, seg, want_rho):
-    left = lon_terms(*(x[0] for x in wins), want_rho)
-    right = lon_terms(*(x[1] for x in wins), want_rho)
+def edge_terms(wins, seg, want_rho, offsets):
+    left = lon_terms([x[0] for x in wins], want_rho, offsets)
+    right = lon_terms([x[1] for x in wins], want_rho, offsets)
     valid = (seg >= 3) & (seg < 9)
     own = [jnp.where(valid, jnp.where(seg < 6, y, x), 0.0) for x, y in zip(left, right)]
     return own, [jnp.where(seg < 6, x, y) for x, y in zip(left[:2], right[:2])]
@@ -171,6 +171,10 @@
 
 def halos_of(wins, seg):
     return [jnp.where(seg < 6, x, y) for x, y in wins]
+
+
+def aligned(wins):
+    return [tuple(rolled(x, -offset, 1) for x in win) for win, offset in zip(wins, OFFSETS)]
 
 
 def spread(x, s):
@@ -317,7 +321,7 @@
         here = [[wide[f, layer + 6, t] for t in range(tiles)] for f in range(3)]
         terms = lat_inner(here, sub, True)
         for t in range(tiles):
-            lon = lon_terms(*(x[t] for x in here), True)
+            lon = lon_terms([x[t] for x in here], True)
             for g in range(3):
                 part[g, layer + 3, t] += terms[t][g] + jnp.where(away, lon[g], 0.0)
         return carry
@@ -328,7 +332,7 @@
         here = [[wide[f, near + 3 + e, t] for t in range(tiles)] for f in range(3)]
         terms = lat_inner(here, sub, False)
         for t in range(tiles):
-            lon = lon_terms(*(x[t] for x in here), False)
+            lon = lon_terms([x[t] for x in here], False)
             for g in range(2):
                 part[g, near + e, t] += terms[t][g] + jnp.where(away, lon[g], 0.0)
         return carry
@@ -362,8 +366,8 @@
     for g in range(groups):
         pack = [ends(x, g) for x in packs]
         wins = [windows(*pack, f, seg) for f in range(3)]
-        laps, _ = edge_terms(wins, seg, False)
-        halos.append(halos_of(wins, seg))
+        laps, _ = edge_terms(wins, seg, False, OFFSETS)
+        halos.append(halos_of(aligned(wins), seg))
         for s in range(min(per, layers - g * per)):
             layer = g * per + s
             here = [ends(x, layer) for x in fields]
@@ -403,27 +407,33 @@
     def edges_at(t, carry):
         sources = [[x[group, at(t), :] for x in packs] for group in range(groups)]
         sources.append([from_core2[k, at(t), :] for k in range(4)])
-        wins = [[windows(*x, f, seg) for f in range(3)] for x in sources]
+        wins = [aligned([windows(*x, f, seg) for f in range(3)]) for x in sources]
         halos = [halos_of(x, seg) for x in wins]
         before = [jnp.where(core == 0, 0.0, x) for x in halos[-1]]
         after = [jnp.where(core == 0, x, 0.0) for x in halos[-1]]
         radials = packed_radial([before, *halos[:-1], after], lane)
-        terms = [edge_terms(x, seg, k < groups) for k, x in enumerate(wins)]
+        terms = [edge_terms(x, seg, True, (0, 0, 0)) for x in wins[:-1]]
         own = [x for x, _ in terms]
-        own[groups] = [
-            jnp.where(core == 0, x, rolled(x, -(per - 3) * SEGMENT, 1)) for x in own[groups]
-        ]
         for group in range(groups):
-            for f in range(3):
-                halo_pack[f, group, t] = halos[group][f]
+            for f, x in enumerate(halos[group]):
+                halo_pack[f, group, t] = x
             for g in range(2):
                 lap_pack[g, group, t] = terms[group][1][g] + radials[group][g]
-        for group in range(groups + 1):
+        for group in range(groups):
             for g, x in enumerate(own[group]):
                 own_pack[g, group, t] = x
         return carry
 
-    lax.fori_loop(0, tiles, edges_at, 0)
+    def other_at(t, carry):
+        other = [from_core2[k, at(t), :] for k in range(4)]
+        wins = aligned([windows(*other, f, seg) for f in range(3)])
+        own, _ = edge_terms(wins, seg, False, (0, 0, 0))
+        for g in range(2):
+            own_pack[g, groups, t] = jnp.where(core == 0, own[g], rolled(own[g], -(per - 3) * SEGMENT, 1))
+        return carry
+
+    lax.fori_loop(0, tiles, edges_at, 0, unroll=2)
+    lax.fori_loop(0, tiles, other_at, 0, unroll=True)
     for group in range(groups):
         halo = [[halo_pack[f, group, t] for t in range(tiles)] for f in range(3)]
         lat = lat_inner(halo, sub, False)
@@ -466,7 +476,7 @@
                 first[g, near + e, t] = 2.0 * wide[g, near + 3 + e, t] - past + stiff * lap
         return carry
 
-    lax.fori_loop(0, tiles, first_at, 0)
+    lax.fori_loop(0, tiles, first_at, 0, unroll=2)
 
     for t in inside:
         terms = radial(lambda f, k: first[f, 3 + k, t], lambda k: wide[2, 6 + k, t], layers)

time: 16.9 us -> 16.7 us (0.988)
  Pallas kernels: 8.44 us -> 8.16 us
    pallas_call x5, Pallas kernels: 8.44 us -> 8.16 us  [call(): pl.pallas_call(kernel, out_shape=out_shape, in_specs=in_specs or [VMEM] *...]
  transfers between devices with their start and end apart: 7 -> 7, of which waited for: 1 -> 1; matrix products, arithmetic and copies ran while one was open for 0% -> 0% of each run, Pallas kernels for 27% -> 26%
where the time goes in v6:
time: 16.7 us; the launch traced here: 16.4 us
  Pallas kernels  8.16 us (49%)
  starting transfers between devices  5.85 us (35%)
  waiting for transfers between devices  1.72 us (10%)
  between operations  0.71 us (4%)
    pallas_call x5, Pallas kernels, call(): pl.pallas_call(kernel, out_shape=out_shape, in_specs=in_specs or [VMEM] *...  8.16 us
    ppermute x1, waiting for transfers between devices, shards(): from_right = lax.ppermute(to_left, 'lon', [(b, a) for a, b in ring])  1.7 us
    ppermute x1, starting transfers between devices, shards(): from_core2 = lax.ppermute(to_core, 'rad', swap)  1.56 us
    ppermute x1, starting transfers between devices, shards(): from_left = lax.ppermute(to_right, 'lon', ring)  1.21 us
    ppermute x1, starting transfers between devices, shards(): from_second = lax.ppermute(to_second, ('lat', 'rad'), pairs(count, 1, 2))  1.19 us
    ppermute x1, starting transfers between devices, shards(): from_core = lax.ppermute(to_core, 'rad', swap)  0.74 us
    ppermute x1, starting transfers between devices, shards(): from_third = lax.ppermute(to_third, ('lat', 'rad'), pairs(count, 2, 4))  0.71 us
  transfers between devices with their start and end apart: 7, of which 1 were waited for; matrix products, arithmetic and copies ran while one was open for 0% of the time, Pallas kernels for 26%

profile of v6, /device:TPU:11, one launch (start us, length us, event | category | flops | bytes accessed | tf_op | source)
XLA Modules:
  0.0 16.4 jit_solution(11691174806577751273)
XLA Ops:
  0.6 1.6 %shard_map.127 = (f32[8,32,128]{2,1,0:T(8,128)S(1)}, f32[8,32,128]{2,1,0:T(8,128)S(1)}, f32[8,32,128]{2,1,0:T(8,128)S(1)}, f32[8,32,128]{2,1,0:T(8,128)S(1)}, f3...) custom-call(f32[8,32,128]{2,1,0:T(8,128)} %refs_0_.1, ...), custom_call_target="tpu_custom_call" | custom-call | tf_op jit(solution)/shard_map/pallas_call | solution.py:664
  2.2 0.7 %collective-permute-start = (f32[27,32,128]{2,1,0:T(8,128)S(1)}, f32[27,32,128]{2,1,0:T(8,128)S(1)}, u32[]{:S(2)}, u32[]{:S(2)}) collective-permute-start(f32[27,32,128]{2,1,0:T(8,128)S(1)} %get-tuple-element.38), channel_id=1, source_target_pairs={{0,1},{1,0},{2,3},{3,2},{4,5},{5,4},{6,7},{7,6},{8,9},{9,8},{10,11... | collective-permute-start | bytes 1327112 | tf_op jit(solution)/shard_map/ppermute | solution.py:700
  3.0 1.2 %collective-permute-start.1 = (f32[2,32,128]{2,1,0:T(8,128)S(1)}, f32[2,32,128]{2,1,0:T(8,128)S(1)}, u32[]{:S(2)}, u32[]{:S(2)}) collective-permute-start(f32[2,32,128]{2,1,0:T(8,128)S(1)} %get-tuple-element.40.refs_9_.refs_11_), channel_id=1, source_target_pairs={{0,8},{8,16},{16,24},{24,0},{1,9},{9,17},{17,25},{25,1},{2,10},{10... | collective-permute-start | bytes 98312 | tf_op jit(solution)/shard_map/ppermute | solution.py:698
  4.2 0.3 %collective-permute-start.2 = (f32[2,32,128]{2,1,0:T(8,128)S(1)}, f32[2,32,128]{2,1,0:T(8,128)S(1)}, u32[]{:S(2)}, u32[]{:S(2)}) collective-permute-start(f32[2,32,128]{2,1,0:T(8,128)S(1)} %get-tuple-element.41.refs_8_.refs_10_), channel_id=1, source_target_pairs={{8,0},{16,8},{24,16},{0,24},{9,1},{17,9},{25,17},{1,25},{10,2},{18... | collective-permute-start | bytes 98312 | tf_op jit(solution)/shard_map/ppermute | solution.py:699
  4.4 0.0 collective-permute-done.refs_6_.refs_12_
  4.4 1.7 %shard_map.128 = (f32[3,20,4,8,128]{4,3,2,1,0:T(8,128)S(1)}, f32[3,14,4,8,128]{4,3,2,1,0:T(8,128)S(1)}, f32[21,8,128]{2,1,0:T(8,128)S(1)}, f32[21,8,128]{2,1,0:T(8,128)S(1)}, f32[21,8,128]{2,1,0:T(8,128)S(1)}) custom-call(f32[8,32,128]{2,1,0:T(8,128)S(1)} %get-tuple-element.32.refs_0_, f32[8,32,128]{2,1,0:T(8,128)S(1)} %get-tuple-element.33.refs_1_, ...), custom_call_target="tpu_custom_call" | custom-call | tf_op jit(solution)/shard_map/pallas_call | solution.py:664
  6.1 0.0 collective-permute-done.1.refs_6_.refs_8_
  6.1 1.7 %collective-permute-done.2.refs_7_.refs_9_ = f32[2,32,128]{2,1,0:T(8,128)S(1)} collective-permute-done((f32[2,32,128]{2,1,0:T(8,128)S(1)}, f32[2,32,128]{2,1,0:T(8,128)S(1)}, u32[]{:S(2)}, u32[]{:S(2)}) %collective-permute-start.2) | collective-permute-done | bytes 32800 | tf_op jit(solution)/shard_map/ppermute | solution.py:699
  7.8 0.0 copy-start
  7.8 0.0 copy-start.1
  7.8 0.3 %shard_map.129 = (f32[21,8,128]{2,1,0:T(8,128)S(1)}, f32[21,8,128]{2,1,0:T(8,128)S(1)}, f32[21,8,128]{2,1,0:T(8,128)S(1)}, f32[4,32,128]{2,1,0:T(8,128)S(1)}, f32[2,1,8,128]{3,2,1,0:T(8,128)S(1)}) custom-call(f32[8,32,128]{2,1,0:T(8,128)S(1)} %get-tuple-element.32.refs_0_, ...), custom_call_target="tpu_custom_call", output_to_operand_aliasing={{0}: (11, {}), {1}: (12, {}), {2}: (13, {})} | custom-call | tf_op jit(solution)/shard_map/pallas_call | solution.py:664
  8.1 1.6 %collective-permute-start.3 = (f32[4,32,128]{2,1,0:T(8,128)S(1)}, f32[4,32,128]{2,1,0:T(8,128)S(1)}, u32[]{:S(2)}, u32[]{:S(2)}) collective-permute-start(f32[4,32,128]{2,1,0:T(8,128)S(1)} %get-tuple-element.46), channel_id=1, source_target_pairs={{0,1},{1,0},{2,3},{3,2},{4,5},{5,4},{6,7},{7,6},{8,9},{9,8},{10,11... | collective-permute-start | bytes 196616 | tf_op jit(solution)/shard_map/ppermute | solution.py:724
  9.7 0.2 %collective-permute-start.4 = (f32[21,8,128]{2,1,0:T(8,128)S(1)}, f32[21,8,128]{2,1,0:T(8,128)S(1)}, u32[]{:S(2)}, u32[]{:S(2)}) collective-permute-start(f32[21,8,128]{2,1,0:T(8,128)S(1)} %get-tuple-element.55), channel_id=1, source_target_pairs={{0,2},{1,3},{2,0},{3,1},{4,5},{5,4},{6,7},{7,6},{8,10},{9,11},{10,... | collective-permute-start | bytes 258056 | tf_op jit(solution)/shard_map/ppermute | solution.py:721
  9.9 1.2 %collective-permute-start.5 = (f32[21,8,128]{2,1,0:T(8,128)S(1)}, f32[21,8,128]{2,1,0:T(8,128)S(1)}, u32[]{:S(2)}, u32[]{:S(2)}) collective-permute-start(f32[21,8,128]{2,1,0:T(8,128)S(1)} %get-tuple-element.56), channel_id=1, source_target_pairs={{0,1},{1,0},{2,4},{3,5},{4,2},{5,3},{6,7},{7,6},{8,9},{9,8},{10,12... | collective-permute-start | bytes 258056 | tf_op jit(solution)/shard_map/ppermute | solution.py:722
  11.1 0.7 %collective-permute-start.6 = (f32[21,8,128]{2,1,0:T(8,128)S(1)}, f32[21,8,128]{2,1,0:T(8,128)S(1)}, u32[]{:S(2)}, u32[]{:S(2)}) collective-permute-start(f32[21,8,128]{2,1,0:T(8,128)S(1)} %get-tuple-element.57), channel_id=1, source_target_pairs={{0,1},{1,0},{2,3},{3,2},{4,6},{5,7},{6,4},{7,5},{8,9},{9,8},{10,11... | collective-permute-start | bytes 258056 | tf_op jit(solution)/shard_map/ppermute | solution.py:723
  11.8 0.0 collective-permute-done.3.refs_13_
  11.8 0.0 copy-done
  11.8 0.0 copy-done.1
  11.8 2.6 %shard_map.130 = (f32[2,14,4,8,128]{4,3,2,1,0:T(8,128)S(1)}, f32[2,2,4,8,128]{4,3,2,1,0:T(8,128)S(1)}, f32[2,4,8,128]{3,2,1,0:T(8,128)S(1)}, f32[8,4,8,128]{3,2,...) custom-call(f32[8,32,128]{2,1,0:T(8,128)S(1)} %get-tuple-element.32., ...), custom_call_target="tpu_custom_call" | custom-call | flops 4000000000 | bytes 1000000 | tf_op jit(solution)/shard_map/pallas_call | solution.py:664
  14.4 0.0 collective-permute-done.4.refs_16_
  14.4 0.0 collective-permute-done.5.refs_17_
  14.4 0.0 collective-permute-done.6.refs_18_
  14.4 2.0 %shard_map.131 = (f32[8,32,128]{2,1,0:T(8,128)}, f32[8,32,128]{2,1,0:T(8,128)}, f32[8,32,128]{2,1,0:T(8,128)}, f32[8,32,128]{2,1,0:T(8,128)}, f32[8,32,128]{2,1,0:T(8,128)}, /*index=5*/f32[8,32,128]{2,1,0:T(8,128)}) custom-call(f32[8,32,128]{2,1,0:T(8,128)S(1)} %get-tuple-element.32.refs_0_, f32[8,32,128]{2,1,0:T(8,128)S(1)} %get-tuple-element.33.refs_1_, ...), custom_call_target="tpu_custom_call" | custom-call | tf_op jit(solution)/shard_map/pallas_call | solution.py:664
Async XLA Ops:
  2.2 2.2 %collective-permute-start = (f32[27,32,128]{2,1,0:T(8,128)S(1)}, f32[27,32,128]{2,1,0:T(8,128)S(1)}, u32[]{:S(2)}, u32[]{:S(2)}) collective-permute-start(f32[27,32,128]{2,1,0:T(8,128)S(1)} %get-tuple-element.38), channel_id=1, source_target_pairs={{0,1},{1,0},{2,3},{3,2},{4,5},{5,4},{6,7},{7,6},{8,9},{9,8},{10,11... | collective-permute-start | bytes 1327112 | tf_op jit(solution)/shard_map/ppermute | solution.py:700
  3.0 3.2 %collective-permute-start.1 = (f32[2,32,128]{2,1,0:T(8,128)S(1)}, f32[2,32,128]{2,1,0:T(8,128)S(1)}, u32[]{:S(2)}, u32[]{:S(2)}) collective-permute-start(f32[2,32,128]{2,1,0:T(8,128)S(1)} %get-tuple-element.40.refs_9_.refs_11_), channel_id=1, source_target_pairs={{0,8},{8,16},{16,24},{24,0},{1,9},{9,17},{17,25},{25,1},{2,10},{10... | collective-permute-start | bytes 98312 | tf_op jit(solution)/shard_map/ppermute | solution.py:698
  4.2 3.7 %collective-permute-start.2 = (f32[2,32,128]{2,1,0:T(8,128)S(1)}, f32[2,32,128]{2,1,0:T(8,128)S(1)}, u32[]{:S(2)}, u32[]{:S(2)}) collective-permute-start(f32[2,32,128]{2,1,0:T(8,128)S(1)} %get-tuple-element.41.refs_8_.refs_10_), channel_id=1, source_target_pairs={{8,0},{16,8},{24,16},{0,24},{9,1},{17,9},{25,17},{1,25},{10,2},{18... | collective-permute-start | bytes 98312 | tf_op jit(solution)/shard_map/ppermute | solution.py:699
  7.8 4.0 %copy-start = (f32[8,32,128]{2,1,0:T(8,128)S(1)}, f32[8,32,128]{2,1,0:T(8,128)}, u32[]{:S(2)}) copy-start(f32[8,32,128]{2,1,0:T(8,128)} %refs_6_.1) | copy-start | bytes 393220
  7.8 4.0 %copy-start.1 = (f32[8,32,128]{2,1,0:T(8,128)S(1)}, f32[8,32,128]{2,1,0:T(8,128)}, u32[]{:S(2)}) copy-start(f32[8,32,128]{2,1,0:T(8,128)} %refs_7_.1) | copy-start | bytes 393220
  8.1 3.7 %collective-permute-start.3 = (f32[4,32,128]{2,1,0:T(8,128)S(1)}, f32[4,32,128]{2,1,0:T(8,128)S(1)}, u32[]{:S(2)}, u32[]{:S(2)}) collective-permute-start(f32[4,32,128]{2,1,0:T(8,128)S(1)} %get-tuple-element.46), channel_id=1, source_target_pairs={{0,1},{1,0},{2,3},{3,2},{4,5},{5,4},{6,7},{7,6},{8,9},{9,8},{10,11... | collective-permute-start | bytes 196616 | tf_op jit(solution)/shard_map/ppermute | solution.py:724
  9.7 4.7 %collective-permute-start.4 = (f32[21,8,128]{2,1,0:T(8,128)S(1)}, f32[21,8,128]{2,1,0:T(8,128)S(1)}, u32[]{:S(2)}, u32[]{:S(2)}) collective-permute-start(f32[21,8,128]{2,1,0:T(8,128)S(1)} %get-tuple-element.55), channel_id=1, source_target_pairs={{0,2},{1,3},{2,0},{3,1},{4,5},{5,4},{6,7},{7,6},{8,10},{9,11},{10,... | collective-permute-start | bytes 258056 | tf_op jit(solution)/shard_map/ppermute | solution.py:721
  9.9 4.5 %collective-permute-start.5 = (f32[21,8,128]{2,1,0:T(8,128)S(1)}, f32[21,8,128]{2,1,0:T(8,128)S(1)}, u32[]{:S(2)}, u32[]{:S(2)}) collective-permute-start(f32[21,8,128]{2,1,0:T(8,128)S(1)} %get-tuple-element.56), channel_id=1, source_target_pairs={{0,1},{1,0},{2,4},{3,5},{4,2},{5,3},{6,7},{7,6},{8,9},{9,8},{10,12... | collective-permute-start | bytes 258056 | tf_op jit(solution)/shard_map/ppermute | solution.py:722
  11.1 3.3 %collective-permute-start.6 = (f32[21,8,128]{2,1,0:T(8,128)S(1)}, f32[21,8,128]{2,1,0:T(8,128)S(1)}, u32[]{:S(2)}, u32[]{:S(2)}) collective-permute-start(f32[21,8,128]{2,1,0:T(8,128)S(1)} %get-tuple-element.57), channel_id=1, source_target_pairs={{0,1},{1,0},{2,3},{3,2},{4,6},{5,7},{6,4},{7,5},{8,9},{9,8},{10,11... | collective-permute-start | bytes 258056 | tf_op jit(solution)/shard_map/ppermute | solution.py:723

commit v7 on v6

--- a/solution.py
+++ b/solution.py
@@ -612,36 +612,33 @@
             for g in range(3):
                 part[g, k, n] = term[g]
 
-    def last(layer, carry):
-        buoys = [wide[2, layer + 6, t] for t in (0, 1, tiles - 2, tiles - 1)]
-        rings = [
-            [fixed[f, layer + 3, 2], fixed[f, layer + 3, 0], first[f, layer + 3, 1]]
-            + [first[f, layer + 3, tiles - 2], fixed[f, layer + 3, 1]]
-            for f in range(2)
-        ] + [[ring_buoy[layer], *buoys]]
-        flux = [None] * 5
-        for t in (0, 1, 4):
-            flux[t] = lat_flux(rings, t, sub)
-        for n in range(2):
-            flux[2 + n] = [flux_in[k, n, layer] for k in range(3)]
-        for n, (t, _) in enumerate(ends):
-            k = (1, 4)[n]
-            here = [x[k] for x in rings]
-            lat = lat_terms(flux, k, sub, True)
-            there = [fixed_halo[0, layer, n], fixed_halo[1, layer, n], buoy_halo[layer, t]]
-            laps, rho = longitudinal(here, there, lane, False, True)
-            stiff = fields[5][layer, at(t), :] * LAP_SCALE
-            for g in range(2):
-                update = stiff * (part[g, layer, n] + lat[g] + laps[0][g])
-                made[2 * g, layer, n] = 2.0 * here[g] - fields[g][layer, at(t), :] + update
-                made[2 * g + 1, layer, n] = here[g]
-            made[4, layer, n] += here[0] * update
-            made[5, layer, n] += RHO_SCALE * (part[2, layer, n] + lat[2] + rho)
-        return carry
-
-    lax.fori_loop(0, layers, last, 0, unroll=True)
-    for k, out in enumerate(outs):
-        for n, (t, _) in enumerate(ends):
+    def last(layer, n):
+        t = ends[n][0]
+        rings = [[fixed[f, layer + 3, 2], fixed[f, layer + 3, n]] for f in range(2)]
+        rings.append([ring_buoy[layer], wide[2, layer + 6, t]])
+        beside = [first[f, layer + 3, (1, tiles - 2)[n]] for f in range(2)]
+        beside.append(wide[2, layer + 6, (1, tiles - 2)[n]])
+        rings = [[x[0], x[1], y] if n == 0 else [y, x[1], x[0]] for x, y in zip(rings, beside)]
+        flux = [None] * 3
+        flux[1] = lat_flux(rings, 1, sub)
+        flux[2 * n] = lat_flux(rings, 2 * n, sub)
+        flux[2 - 2 * n] = [flux_in[k, n, layer] for k in range(3)]
+        here = [x[1] for x in rings]
+        lat = lat_terms(flux, 1, sub, True)
+        there = [fixed_halo[0, layer, n], fixed_halo[1, layer, n], buoy_halo[layer, t]]
+        laps, rho = longitudinal(here, there, lane, False, True)
+        stiff = fields[5][layer, at(t), :] * LAP_SCALE
+        for g in range(2):
+            update = stiff * (part[g, layer, n] + lat[g] + laps[0][g])
+            made[2 * g, layer, n] = 2.0 * here[g] - fields[g][layer, at(t), :] + update
+            made[2 * g + 1, layer, n] = here[g]
+        made[4, layer, n] += here[0] * update
+        made[5, layer, n] += RHO_SCALE * (part[2, layer, n] + lat[2] + rho)
+
+    for n, (t, _) in enumerate(ends):
+        for layer in range(layers):
+            last(layer, n)
+        for k, out in enumerate(outs):
             copy = pltpu.make_async_copy(made.at[k, :, n], out.at[:, at(t), :], sems.at[k, 1 + n])
             copy.start()
             copies.append(copy)

time: 16.7 us -> 16.5 us (0.988)
  Pallas kernels: 8.16 us -> 7.98 us
    pallas_call x5, Pallas kernels: 8.16 us -> 7.98 us  [call(): pl.pallas_call(kernel, out_shape=out_shape, in_specs=in_specs or [VMEM] *...]
where the time goes in v7:
time: 16.5 us; the launch traced here: 16.3 us
  Pallas kernels  7.98 us (48%)
  starting transfers between devices  5.85 us (35%)
  waiting for transfers between devices  1.72 us (10%)
  between operations  0.71 us (4%)
    pallas_call x5, Pallas kernels, call(): pl.pallas_call(kernel, out_shape=out_shape, in_specs=in_specs or [VMEM] *...  7.98 us
    ppermute x1, waiting for transfers between devices, shards(): from_right = lax.ppermute(to_left, 'lon', [(b, a) for a, b in ring])  1.7 us
    ppermute x1, starting transfers between devices, shards(): from_core2 = lax.ppermute(to_core, 'rad', swap)  1.56 us
    ppermute x1, starting transfers between devices, shards(): from_left = lax.ppermute(to_right, 'lon', ring)  1.21 us
    ppermute x1, starting transfers between devices, shards(): from_second = lax.ppermute(to_second, ('lat', 'rad'), pairs(count, 1, 2))  1.19 us
    ppermute x1, starting transfers between devices, shards(): from_core = lax.ppermute(to_core, 'rad', swap)  0.74 us
    ppermute x1, starting transfers between devices, shards(): from_third = lax.ppermute(to_third, ('lat', 'rad'), pairs(count, 2, 4))  0.71 us
  transfers between devices with their start and end apart: 7, of which 1 were waited for; matrix products, arithmetic and copies ran while one was open for 0% of the time, Pallas kernels for 26%

profile of v7, /device:TPU:11, one launch (start us, length us, event | category | flops | bytes accessed | tf_op | source)
XLA Modules:
  0.0 16.3 jit_solution(2029349058749220432)
XLA Ops:
  0.6 1.6 %shard_map.127 = (f32[8,32,128]{2,1,0:T(8,128)S(1)}, f32[8,32,128]{2,1,0:T(8,128)S(1)}, f32[8,32,128]{2,1,0:T(8,128)S(1)}, f32[8,32,128]{2,1,0:T(8,128)S(1)}, f3...) custom-call(f32[8,32,128]{2,1,0:T(8,128)} %refs_0_.1, ...), custom_call_target="tpu_custom_call" | custom-call | tf_op jit(solution)/shard_map/pallas_call | solution.py:661
  2.2 0.7 %collective-permute-start = (f32[27,32,128]{2,1,0:T(8,128)S(1)}, f32[27,32,128]{2,1,0:T(8,128)S(1)}, u32[]{:S(2)}, u32[]{:S(2)}) collective-permute-start(f32[27,32,128]{2,1,0:T(8,128)S(1)} %get-tuple-element.38), channel_id=1, source_target_pairs={{0,1},{1,0},{2,3},{3,2},{4,5},{5,4},{6,7},{7,6},{8,9},{9,8},{10,11... | collective-permute-start | bytes 1327112 | tf_op jit(solution)/shard_map/ppermute | solution.py:697
  3.0 1.2 %collective-permute-start.1 = (f32[2,32,128]{2,1,0:T(8,128)S(1)}, f32[2,32,128]{2,1,0:T(8,128)S(1)}, u32[]{:S(2)}, u32[]{:S(2)}) collective-permute-start(f32[2,32,128]{2,1,0:T(8,128)S(1)} %get-tuple-element.40.refs_9_.refs_11_), channel_id=1, source_target_pairs={{0,8},{8,16},{16,24},{24,0},{1,9},{9,17},{17,25},{25,1},{2,10},{10... | collective-permute-start | bytes 98312 | tf_op jit(solution)/shard_map/ppermute | solution.py:695
  4.2 0.3 %collective-permute-start.2 = (f32[2,32,128]{2,1,0:T(8,128)S(1)}, f32[2,32,128]{2,1,0:T(8,128)S(1)}, u32[]{:S(2)}, u32[]{:S(2)}) collective-permute-start(f32[2,32,128]{2,1,0:T(8,128)S(1)} %get-tuple-element.41.refs_8_.refs_10_), channel_id=1, source_target_pairs={{8,0},{16,8},{24,16},{0,24},{9,1},{17,9},{25,17},{1,25},{10,2},{18... | collective-permute-start | bytes 98312 | tf_op jit(solution)/shard_map/ppermute | solution.py:696
  4.4 0.0 collective-permute-done.refs_6_.refs_12_
  4.4 1.7 %shard_map.128 = (f32[3,20,4,8,128]{4,3,2,1,0:T(8,128)S(1)}, f32[3,14,4,8,128]{4,3,2,1,0:T(8,128)S(1)}, f32[21,8,128]{2,1,0:T(8,128)S(1)}, f32[21,8,128]{2,1,0:T(8,128)S(1)}, f32[21,8,128]{2,1,0:T(8,128)S(1)}) custom-call(f32[8,32,128]{2,1,0:T(8,128)S(1)} %get-tuple-element.32.refs_0_, f32[8,32,128]{2,1,0:T(8,128)S(1)} %get-tuple-element.33.refs_1_, ...), custom_call_target="tpu_custom_call" | custom-call | tf_op jit(solution)/shard_map/pallas_call | solution.py:661
  6.1 0.0 collective-permute-done.1.refs_6_.refs_8_
  6.1 1.7 %collective-permute-done.2.refs_7_.refs_9_ = f32[2,32,128]{2,1,0:T(8,128)S(1)} collective-permute-done((f32[2,32,128]{2,1,0:T(8,128)S(1)}, f32[2,32,128]{2,1,0:T(8,128)S(1)}, u32[]{:S(2)}, u32[]{:S(2)}) %collective-permute-start.2) | collective-permute-done | bytes 32800 | tf_op jit(solution)/shard_map/ppermute | solution.py:696
  7.8 0.0 copy-start
  7.8 0.0 copy-start.1
  7.8 0.3 %shard_map.129 = (f32[21,8,128]{2,1,0:T(8,128)S(1)}, f32[21,8,128]{2,1,0:T(8,128)S(1)}, f32[21,8,128]{2,1,0:T(8,128)S(1)}, f32[4,32,128]{2,1,0:T(8,128)S(1)}, f32[2,1,8,128]{3,2,1,0:T(8,128)S(1)}) custom-call(f32[8,32,128]{2,1,0:T(8,128)S(1)} %get-tuple-element.32.refs_0_, ...), custom_call_target="tpu_custom_call", output_to_operand_aliasing={{0}: (11, {}), {1}: (12, {}), {2}: (13, {})} | custom-call | tf_op jit(solution)/shard_map/pallas_call | solution.py:661
  8.1 1.6 %collective-permute-start.3 = (f32[4,32,128]{2,1,0:T(8,128)S(1)}, f32[4,32,128]{2,1,0:T(8,128)S(1)}, u32[]{:S(2)}, u32[]{:S(2)}) collective-permute-start(f32[4,32,128]{2,1,0:T(8,128)S(1)} %get-tuple-element.46), channel_id=1, source_target_pairs={{0,1},{1,0},{2,3},{3,2},{4,5},{5,4},{6,7},{7,6},{8,9},{9,8},{10,11... | collective-permute-start | bytes 196616 | tf_op jit(solution)/shard_map/ppermute | solution.py:721
  9.7 0.2 %collective-permute-start.4 = (f32[21,8,128]{2,1,0:T(8,128)S(1)}, f32[21,8,128]{2,1,0:T(8,128)S(1)}, u32[]{:S(2)}, u32[]{:S(2)}) collective-permute-start(f32[21,8,128]{2,1,0:T(8,128)S(1)} %get-tuple-element.55), channel_id=1, source_target_pairs={{0,2},{1,3},{2,0},{3,1},{4,5},{5,4},{6,7},{7,6},{8,10},{9,11},{10,... | collective-permute-start | bytes 258056 | tf_op jit(solution)/shard_map/ppermute | solution.py:718
  9.9 1.2 %collective-permute-start.5 = (f32[21,8,128]{2,1,0:T(8,128)S(1)}, f32[21,8,128]{2,1,0:T(8,128)S(1)}, u32[]{:S(2)}, u32[]{:S(2)}) collective-permute-start(f32[21,8,128]{2,1,0:T(8,128)S(1)} %get-tuple-element.56), channel_id=1, source_target_pairs={{0,1},{1,0},{2,4},{3,5},{4,2},{5,3},{6,7},{7,6},{8,9},{9,8},{10,12... | collective-permute-start | bytes 258056 | tf_op jit(solution)/shard_map/ppermute | solution.py:719
  11.1 0.7 %collective-permute-start.6 = (f32[21,8,128]{2,1,0:T(8,128)S(1)}, f32[21,8,128]{2,1,0:T(8,128)S(1)}, u32[]{:S(2)}, u32[]{:S(2)}) collective-permute-start(f32[21,8,128]{2,1,0:T(8,128)S(1)} %get-tuple-element.57), channel_id=1, source_target_pairs={{0,1},{1,0},{2,3},{3,2},{4,6},{5,7},{6,4},{7,5},{8,9},{9,8},{10,11... | collective-permute-start | bytes 258056 | tf_op jit(solution)/shard_map/ppermute | solution.py:720
  11.8 0.0 collective-permute-done.3.refs_13_
  11.8 0.0 copy-done
  11.8 0.0 copy-done.1
  11.8 2.6 %shard_map.130 = (f32[2,14,4,8,128]{4,3,2,1,0:T(8,128)S(1)}, f32[2,2,4,8,128]{4,3,2,1,0:T(8,128)S(1)}, f32[2,4,8,128]{3,2,1,0:T(8,128)S(1)}, f32[8,4,8,128]{3,2,...) custom-call(f32[8,32,128]{2,1,0:T(8,128)S(1)} %get-tuple-element.32., ...), custom_call_target="tpu_custom_call" | custom-call | flops 4000000000 | bytes 1000000 | tf_op jit(solution)/shard_map/pallas_call | solution.py:661
  14.4 0.0 collective-permute-done.4.refs_16_
  14.4 0.0 collective-permute-done.5.refs_17_
  14.4 0.0 collective-permute-done.6.refs_18_
  14.4 1.9 %shard_map.131 = (f32[8,32,128]{2,1,0:T(8,128)}, f32[8,32,128]{2,1,0:T(8,128)}, f32[8,32,128]{2,1,0:T(8,128)}, f32[8,32,128]{2,1,0:T(8,128)}, f32[8,32,128]{2,1,0:T(8,128)}, /*index=5*/f32[8,32,128]{2,1,0:T(8,128)}) custom-call(f32[8,32,128]{2,1,0:T(8,128)S(1)} %get-tuple-element.32.refs_0_, f32[8,32,128]{2,1,0:T(8,128)S(1)} %get-tuple-element.33.refs_1_, ...), custom_call_target="tpu_custom_call" | custom-call | tf_op jit(solution)/shard_map/pallas_call | solution.py:661
Async XLA Ops:
  2.2 2.2 %collective-permute-start = (f32[27,32,128]{2,1,0:T(8,128)S(1)}, f32[27,32,128]{2,1,0:T(8,128)S(1)}, u32[]{:S(2)}, u32[]{:S(2)}) collective-permute-start(f32[27,32,128]{2,1,0:T(8,128)S(1)} %get-tuple-element.38), channel_id=1, source_target_pairs={{0,1},{1,0},{2,3},{3,2},{4,5},{5,4},{6,7},{7,6},{8,9},{9,8},{10,11... | collective-permute-start | bytes 1327112 | tf_op jit(solution)/shard_map/ppermute | solution.py:697
  3.0 3.2 %collective-permute-start.1 = (f32[2,32,128]{2,1,0:T(8,128)S(1)}, f32[2,32,128]{2,1,0:T(8,128)S(1)}, u32[]{:S(2)}, u32[]{:S(2)}) collective-permute-start(f32[2,32,128]{2,1,0:T(8,128)S(1)} %get-tuple-element.40.refs_9_.refs_11_), channel_id=1, source_target_pairs={{0,8},{8,16},{16,24},{24,0},{1,9},{9,17},{17,25},{25,1},{2,10},{10... | collective-permute-start | bytes 98312 | tf_op jit(solution)/shard_map/ppermute | solution.py:695
  4.2 3.7 %collective-permute-start.2 = (f32[2,32,128]{2,1,0:T(8,128)S(1)}, f32[2,32,128]{2,1,0:T(8,128)S(1)}, u32[]{:S(2)}, u32[]{:S(2)}) collective-permute-start(f32[2,32,128]{2,1,0:T(8,128)S(1)} %get-tuple-element.41.refs_8_.refs_10_), channel_id=1, source_target_pairs={{8,0},{16,8},{24,16},{0,24},{9,1},{17,9},{25,17},{1,25},{10,2},{18... | collective-permute-start | bytes 98312 | tf_op jit(solution)/shard_map/ppermute | solution.py:696
  7.8 4.0 %copy-start = (f32[8,32,128]{2,1,0:T(8,128)S(1)}, f32[8,32,128]{2,1,0:T(8,128)}, u32[]{:S(2)}) copy-start(f32[8,32,128]{2,1,0:T(8,128)} %refs_6_.1) | copy-start | bytes 393220
  7.8 4.0 %copy-start.1 = (f32[8,32,128]{2,1,0:T(8,128)S(1)}, f32[8,32,128]{2,1,0:T(8,128)}, u32[]{:S(2)}) copy-start(f32[8,32,128]{2,1,0:T(8,128)} %refs_7_.1) | copy-start | bytes 393220
  8.1 3.7 %collective-permute-start.3 = (f32[4,32,128]{2,1,0:T(8,128)S(1)}, f32[4,32,128]{2,1,0:T(8,128)S(1)}, u32[]{:S(2)}, u32[]{:S(2)}) collective-permute-start(f32[4,32,128]{2,1,0:T(8,128)S(1)} %get-tuple-element.46), channel_id=1, source_target_pairs={{0,1},{1,0},{2,3},{3,2},{4,5},{5,4},{6,7},{7,6},{8,9},{9,8},{10,11... | collective-permute-start | bytes 196616 | tf_op jit(solution)/shard_map/ppermute | solution.py:721
  9.7 4.7 %collective-permute-start.4 = (f32[21,8,128]{2,1,0:T(8,128)S(1)}, f32[21,8,128]{2,1,0:T(8,128)S(1)}, u32[]{:S(2)}, u32[]{:S(2)}) collective-permute-start(f32[21,8,128]{2,1,0:T(8,128)S(1)} %get-tuple-element.55), channel_id=1, source_target_pairs={{0,2},{1,3},{2,0},{3,1},{4,5},{5,4},{6,7},{7,6},{8,10},{9,11},{10,... | collective-permute-start | bytes 258056 | tf_op jit(solution)/shard_map/ppermute | solution.py:718
  9.9 4.5 %collective-permute-start.5 = (f32[21,8,128]{2,1,0:T(8,128)S(1)}, f32[21,8,128]{2,1,0:T(8,128)S(1)}, u32[]{:S(2)}, u32[]{:S(2)}) collective-permute-start(f32[21,8,128]{2,1,0:T(8,128)S(1)} %get-tuple-element.56), channel_id=1, source_target_pairs={{0,1},{1,0},{2,4},{3,5},{4,2},{5,3},{6,7},{7,6},{8,9},{9,8},{10,12... | collective-permute-start | bytes 258056 | tf_op jit(solution)/shard_map/ppermute | solution.py:719
  11.1 3.3 %collective-permute-start.6 = (f32[21,8,128]{2,1,0:T(8,128)S(1)}, f32[21,8,128]{2,1,0:T(8,128)S(1)}, u32[]{:S(2)}, u32[]{:S(2)}) collective-permute-start(f32[21,8,128]{2,1,0:T(8,128)S(1)} %get-tuple-element.57), channel_id=1, source_target_pairs={{0,1},{1,0},{2,3},{3,2},{4,6},{5,7},{6,4},{7,5},{8,9},{9,8},{10,11... | collective-permute-start | bytes 258056 | tf_op jit(solution)/shard_map/ppermute | solution.py:720

commit v8 on v7

--- a/solution.py
+++ b/solution.py
@@ -67,28 +67,28 @@
     _, lane = iotas(lanes)
     core = lax.axis_index("rad")
     per = lanes // SEGMENT
+    for copy in copies:
+        copy.wait()
+    for group in range(to_right.shape[0]):
+        for t in range(rows // SUB):
+            at = pl.ds(t * SUB, SUB)
+            right = left = None
+            for layer in range(group * per, min(layers, (group + 1) * per)):
+                for f, (width, offset) in enumerate(zip(WIDTHS, OFFSETS)):
+                    first = (layer - group * per) * SEGMENT + offset
+                    second = first + width
+                    x = rolled(fields[f][layer, at, :], second, 1)
+                    mask = lane >= second
+                    if second + width > lanes:
+                        mask = mask | (lane < second + width - lanes)
+                    right = x if right is None else jnp.where(lane >= first, x, right)
+                    left = x if left is None else jnp.where(mask, x, left)
+            to_right[group, at, :] = right
+            to_left[group, at, :] = left
     row = 0
-    packed = {}
-    for f, (width, offset) in enumerate(zip(WIDTHS, OFFSETS)):
-        copies[f].wait()
-        for layer in range(layers):
-            group, s = divmod(layer, per)
-            first = s * SEGMENT + offset
-            second = first + width
-            mask = lane >= second
-            if second + width > lanes:
-                mask = mask | (lane < second + width - lanes)
-            mine = (lane >= first) & (lane < second)
-            theirs = mask & (lane < second + width) if second + width <= lanes else mask
-            for t in range(rows // SUB):
-                x = rolled(fields[f][layer, pl.ds(t * SUB, SUB), :], second, 1)
-                right, left = packed.get((group, t), (x, x))
-                packed[group, t] = jnp.where(mine, x, right), jnp.where(theirs, x, left)
+    for f, width in enumerate(WIDTHS):
         to_core[row : row + width] = fields[f][pl.ds((layers - width) * (1 - core), width)]
         row += width
-    for (group, t), (right, left) in packed.items():
-        to_right[group, pl.ds(t * SUB, SUB), :] = right
-        to_left[group, pl.ds(t * SUB, SUB), :] = left
 
 
 def radial(p_at, b_at, layers):

time: 16.5 us -> 16.5 us (level)
  no operation moved by 1% of the time
where the time goes in v8:
time: 16.5 us; the launch traced here: 16.2 us
  Pallas kernels  7.94 us (48%)
  starting transfers between devices  5.85 us (35%)
  waiting for transfers between devices  1.72 us (10%)
  between operations  0.71 us (4%)
    pallas_call x5, Pallas kernels, call(): pl.pallas_call(kernel, out_shape=out_shape, in_specs=in_specs or [VMEM] *...  7.94 us
    ppermute x1, waiting for transfers between devices, shards(): from_right = lax.ppermute(to_left, 'lon', [(b, a) for a, b in ring])  1.7 us
    ppermute x1, starting transfers between devices, shards(): from_core2 = lax.ppermute(to_core, 'rad', swap)  1.56 us
    ppermute x1, starting transfers between devices, shards(): from_left = lax.ppermute(to_right, 'lon', ring)  1.21 us
    ppermute x1, starting transfers between devices, shards(): from_second = lax.ppermute(to_second, ('lat', 'rad'), pairs(count, 1, 2))  1.19 us
    ppermute x1, starting transfers between devices, shards(): from_core = lax.ppermute(to_core, 'rad', swap)  0.74 us
    ppermute x1, starting transfers between devices, shards(): from_third = lax.ppermute(to_third, ('lat', 'rad'), pairs(count, 2, 4))  0.71 us
  transfers between devices with their start and end apart: 7, of which 1 were waited for; matrix products, arithmetic and copies ran while one was open for 0% of the time, Pallas kernels for 26%

profile of v8, /device:TPU:11, one launch (start us, length us, event | category | flops | bytes accessed | tf_op | source)
XLA Modules:
  0.0 16.2 jit_solution(2632975645950802060)
XLA Ops:
  0.6 1.6 %shard_map.127 = (f32[8,32,128]{2,1,0:T(8,128)S(1)}, f32[8,32,128]{2,1,0:T(8,128)S(1)}, f32[8,32,128]{2,1,0:T(8,128)S(1)}, f32[8,32,128]{2,1,0:T(8,128)S(1)}, f3...) custom-call(f32[8,32,128]{2,1,0:T(8,128)} %refs_0_.1, ...), custom_call_target="tpu_custom_call" | custom-call | tf_op jit(solution)/shard_map/pallas_call | solution.py:661
  2.2 0.7 %collective-permute-start = (f32[27,32,128]{2,1,0:T(8,128)S(1)}, f32[27,32,128]{2,1,0:T(8,128)S(1)}, u32[]{:S(2)}, u32[]{:S(2)}) collective-permute-start(f32[27,32,128]{2,1,0:T(8,128)S(1)} %get-tuple-element.38), channel_id=1, source_target_pairs={{0,1},{1,0},{2,3},{3,2},{4,5},{5,4},{6,7},{7,6},{8,9},{9,8},{10,11... | collective-permute-start | bytes 1327112 | tf_op jit(solution)/shard_map/ppermute | solution.py:697
  2.9 1.2 %collective-permute-start.1 = (f32[2,32,128]{2,1,0:T(8,128)S(1)}, f32[2,32,128]{2,1,0:T(8,128)S(1)}, u32[]{:S(2)}, u32[]{:S(2)}) collective-permute-start(f32[2,32,128]{2,1,0:T(8,128)S(1)} %get-tuple-element.40.refs_9_.refs_11_), channel_id=1, source_target_pairs={{0,8},{8,16},{16,24},{24,0},{1,9},{9,17},{17,25},{25,1},{2,10},{10... | collective-permute-start | bytes 98312 | tf_op jit(solution)/shard_map/ppermute | solution.py:695
  4.1 0.3 %collective-permute-start.2 = (f32[2,32,128]{2,1,0:T(8,128)S(1)}, f32[2,32,128]{2,1,0:T(8,128)S(1)}, u32[]{:S(2)}, u32[]{:S(2)}) collective-permute-start(f32[2,32,128]{2,1,0:T(8,128)S(1)} %get-tuple-element.41.refs_8_.refs_10_), channel_id=1, source_target_pairs={{8,0},{16,8},{24,16},{0,24},{9,1},{17,9},{25,17},{1,25},{10,2},{18... | collective-permute-start | bytes 98312 | tf_op jit(solution)/shard_map/ppermute | solution.py:696
  4.4 0.0 collective-permute-done.refs_6_.refs_12_
  4.4 1.7 %shard_map.128 = (f32[3,20,4,8,128]{4,3,2,1,0:T(8,128)S(1)}, f32[3,14,4,8,128]{4,3,2,1,0:T(8,128)S(1)}, f32[21,8,128]{2,1,0:T(8,128)S(1)}, f32[21,8,128]{2,1,0:T(8,128)S(1)}, f32[21,8,128]{2,1,0:T(8,128)S(1)}) custom-call(f32[8,32,128]{2,1,0:T(8,128)S(1)} %get-tuple-element.32.refs_0_, f32[8,32,128]{2,1,0:T(8,128)S(1)} %get-tuple-element.33.refs_1_, ...), custom_call_target="tpu_custom_call" | custom-call | tf_op jit(solution)/shard_map/pallas_call | solution.py:661
  6.1 0.0 collective-permute-done.1.refs_6_.refs_8_
  6.1 1.7 %collective-permute-done.2.refs_7_.refs_9_ = f32[2,32,128]{2,1,0:T(8,128)S(1)} collective-permute-done((f32[2,32,128]{2,1,0:T(8,128)S(1)}, f32[2,32,128]{2,1,0:T(8,128)S(1)}, u32[]{:S(2)}, u32[]{:S(2)}) %collective-permute-start.2) | collective-permute-done | bytes 32800 | tf_op jit(solution)/shard_map/ppermute | solution.py:696
  7.8 0.0 copy-start
  7.8 0.0 copy-start.1
  7.8 0.3 %shard_map.129 = (f32[21,8,128]{2,1,0:T(8,128)S(1)}, f32[21,8,128]{2,1,0:T(8,128)S(1)}, f32[21,8,128]{2,1,0:T(8,128)S(1)}, f32[4,32,128]{2,1,0:T(8,128)S(1)}, f32[2,1,8,128]{3,2,1,0:T(8,128)S(1)}) custom-call(f32[8,32,128]{2,1,0:T(8,128)S(1)} %get-tuple-element.32.refs_0_, ...), custom_call_target="tpu_custom_call", output_to_operand_aliasing={{0}: (11, {}), {1}: (12, {}), {2}: (13, {})} | custom-call | tf_op jit(solution)/shard_map/pallas_call | solution.py:661
  8.1 1.6 %collective-permute-start.3 = (f32[4,32,128]{2,1,0:T(8,128)S(1)}, f32[4,32,128]{2,1,0:T(8,128)S(1)}, u32[]{:S(2)}, u32[]{:S(2)}) collective-permute-start(f32[4,32,128]{2,1,0:T(8,128)S(1)} %get-tuple-element.46), channel_id=1, source_target_pairs={{0,1},{1,0},{2,3},{3,2},{4,5},{5,4},{6,7},{7,6},{8,9},{9,8},{10,11... | collective-permute-start | bytes 196616 | tf_op jit(solution)/shard_map/ppermute | solution.py:721
  9.7 0.2 %collective-permute-start.4 = (f32[21,8,128]{2,1,0:T(8,128)S(1)}, f32[21,8,128]{2,1,0:T(8,128)S(1)}, u32[]{:S(2)}, u32[]{:S(2)}) collective-permute-start(f32[21,8,128]{2,1,0:T(8,128)S(1)} %get-tuple-element.55), channel_id=1, source_target_pairs={{0,2},{1,3},{2,0},{3,1},{4,5},{5,4},{6,7},{7,6},{8,10},{9,11},{10,... | collective-permute-start | bytes 258056 | tf_op jit(solution)/shard_map/ppermute | solution.py:718
  9.9 1.2 %collective-permute-start.5 = (f32[21,8,128]{2,1,0:T(8,128)S(1)}, f32[21,8,128]{2,1,0:T(8,128)S(1)}, u32[]{:S(2)}, u32[]{:S(2)}) collective-permute-start(f32[21,8,128]{2,1,0:T(8,128)S(1)} %get-tuple-element.56), channel_id=1, source_target_pairs={{0,1},{1,0},{2,4},{3,5},{4,2},{5,3},{6,7},{7,6},{8,9},{9,8},{10,12... | collective-permute-start | bytes 258056 | tf_op jit(solution)/shard_map/ppermute | solution.py:719
  11.1 0.7 %collective-permute-start.6 = (f32[21,8,128]{2,1,0:T(8,128)S(1)}, f32[21,8,128]{2,1,0:T(8,128)S(1)}, u32[]{:S(2)}, u32[]{:S(2)}) collective-permute-start(f32[21,8,128]{2,1,0:T(8,128)S(1)} %get-tuple-element.57), channel_id=1, source_target_pairs={{0,1},{1,0},{2,3},{3,2},{4,6},{5,7},{6,4},{7,5},{8,9},{9,8},{10,11... | collective-permute-start | bytes 258056 | tf_op jit(solution)/shard_map/ppermute | solution.py:720
  11.8 0.0 collective-permute-done.3.refs_13_
  11.8 0.0 copy-done
  11.8 0.0 copy-done.1
  11.8 2.6 %shard_map.130 = (f32[2,14,4,8,128]{4,3,2,1,0:T(8,128)S(1)}, f32[2,2,4,8,128]{4,3,2,1,0:T(8,128)S(1)}, f32[2,4,8,128]{3,2,1,0:T(8,128)S(1)}, f32[8,4,8,128]{3,2,...) custom-call(f32[8,32,128]{2,1,0:T(8,128)S(1)} %get-tuple-element.32., ...), custom_call_target="tpu_custom_call" | custom-call | flops 4000000000 | bytes 1000000 | tf_op jit(solution)/shard_map/pallas_call | solution.py:661
  14.3 0.0 collective-permute-done.4.refs_16_
  14.4 0.0 collective-permute-done.5.refs_17_
  14.4 0.0 collective-permute-done.6.refs_18_
  14.4 1.9 %shard_map.131 = (f32[8,32,128]{2,1,0:T(8,128)}, f32[8,32,128]{2,1,0:T(8,128)}, f32[8,32,128]{2,1,0:T(8,128)}, f32[8,32,128]{2,1,0:T(8,128)}, f32[8,32,128]{2,1,0:T(8,128)}, /*index=5*/f32[8,32,128]{2,1,0:T(8,128)}) custom-call(f32[8,32,128]{2,1,0:T(8,128)S(1)} %get-tuple-element.32.refs_0_, f32[8,32,128]{2,1,0:T(8,128)S(1)} %get-tuple-element.33.refs_1_, ...), custom_call_target="tpu_custom_call" | custom-call | tf_op jit(solution)/shard_map/pallas_call | solution.py:661
Async XLA Ops:
  2.2 2.2 %collective-permute-start = (f32[27,32,128]{2,1,0:T(8,128)S(1)}, f32[27,32,128]{2,1,0:T(8,128)S(1)}, u32[]{:S(2)}, u32[]{:S(2)}) collective-permute-start(f32[27,32,128]{2,1,0:T(8,128)S(1)} %get-tuple-element.38), channel_id=1, source_target_pairs={{0,1},{1,0},{2,3},{3,2},{4,5},{5,4},{6,7},{7,6},{8,9},{9,8},{10,11... | collective-permute-start | bytes 1327112 | tf_op jit(solution)/shard_map/ppermute | solution.py:697
  2.9 3.2 %collective-permute-start.1 = (f32[2,32,128]{2,1,0:T(8,128)S(1)}, f32[2,32,128]{2,1,0:T(8,128)S(1)}, u32[]{:S(2)}, u32[]{:S(2)}) collective-permute-start(f32[2,32,128]{2,1,0:T(8,128)S(1)} %get-tuple-element.40.refs_9_.refs_11_), channel_id=1, source_target_pairs={{0,8},{8,16},{16,24},{24,0},{1,9},{9,17},{17,25},{25,1},{2,10},{10... | collective-permute-start | bytes 98312 | tf_op jit(solution)/shard_map/ppermute | solution.py:695
  4.1 3.7 %collective-permute-start.2 = (f32[2,32,128]{2,1,0:T(8,128)S(1)}, f32[2,32,128]{2,1,0:T(8,128)S(1)}, u32[]{:S(2)}, u32[]{:S(2)}) collective-permute-start(f32[2,32,128]{2,1,0:T(8,128)S(1)} %get-tuple-element.41.refs_8_.refs_10_), channel_id=1, source_target_pairs={{8,0},{16,8},{24,16},{0,24},{9,1},{17,9},{25,17},{1,25},{10,2},{18... | collective-permute-start | bytes 98312 | tf_op jit(solution)/shard_map/ppermute | solution.py:696
  7.8 4.0 %copy-start = (f32[8,32,128]{2,1,0:T(8,128)S(1)}, f32[8,32,128]{2,1,0:T(8,128)}, u32[]{:S(2)}) copy-start(f32[8,32,128]{2,1,0:T(8,128)} %refs_6_.1) | copy-start | bytes 393220
  7.8 4.0 %copy-start.1 = (f32[8,32,128]{2,1,0:T(8,128)S(1)}, f32[8,32,128]{2,1,0:T(8,128)}, u32[]{:S(2)}) copy-start(f32[8,32,128]{2,1,0:T(8,128)} %refs_7_.1) | copy-start | bytes 393220
  8.1 3.7 %collective-permute-start.3 = (f32[4,32,128]{2,1,0:T(8,128)S(1)}, f32[4,32,128]{2,1,0:T(8,128)S(1)}, u32[]{:S(2)}, u32[]{:S(2)}) collective-permute-start(f32[4,32,128]{2,1,0:T(8,128)S(1)} %get-tuple-element.46), channel_id=1, source_target_pairs={{0,1},{1,0},{2,3},{3,2},{4,5},{5,4},{6,7},{7,6},{8,9},{9,8},{10,11... | collective-permute-start | bytes 196616 | tf_op jit(solution)/shard_map/ppermute | solution.py:721
  9.7 4.7 %collective-permute-start.4 = (f32[21,8,128]{2,1,0:T(8,128)S(1)}, f32[21,8,128]{2,1,0:T(8,128)S(1)}, u32[]{:S(2)}, u32[]{:S(2)}) collective-permute-start(f32[21,8,128]{2,1,0:T(8,128)S(1)} %get-tuple-element.55), channel_id=1, source_target_pairs={{0,2},{1,3},{2,0},{3,1},{4,5},{5,4},{6,7},{7,6},{8,10},{9,11},{10,... | collective-permute-start | bytes 258056 | tf_op jit(solution)/shard_map/ppermute | solution.py:718
  9.9 4.5 %collective-permute-start.5 = (f32[21,8,128]{2,1,0:T(8,128)S(1)}, f32[21,8,128]{2,1,0:T(8,128)S(1)}, u32[]{:S(2)}, u32[]{:S(2)}) collective-permute-start(f32[21,8,128]{2,1,0:T(8,128)S(1)} %get-tuple-element.56), channel_id=1, source_target_pairs={{0,1},{1,0},{2,4},{3,5},{4,2},{5,3},{6,7},{7,6},{8,9},{9,8},{10,12... | collective-permute-start | bytes 258056 | tf_op jit(solution)/shard_map/ppermute | solution.py:719
  11.1 3.3 %collective-permute-start.6 = (f32[21,8,128]{2,1,0:T(8,128)S(1)}, f32[21,8,128]{2,1,0:T(8,128)S(1)}, u32[]{:S(2)}, u32[]{:S(2)}) collective-permute-start(f32[21,8,128]{2,1,0:T(8,128)S(1)} %get-tuple-element.57), channel_id=1, source_target_pairs={{0,1},{1,0},{2,3},{3,2},{4,6},{5,7},{6,4},{7,5},{8,9},{9,8},{10,11... | collective-permute-start | bytes 258056 | tf_op jit(solution)/shard_map/ppermute | solution.py:720

commit v9 on v8

--- a/solution.py
+++ b/solution.py
@@ -264,8 +264,8 @@
 
 
 def inner_kernel(*refs):
-    fields, from_core = refs[:6], refs[6]
-    wide, part, to_first, to_second, to_third = refs[7:]
+    fields, (bulk_in, density_in), from_core = refs[:6], refs[6:8], refs[8]
+    wide, part, base, to_first, to_second, to_third = refs[9:]
     layers, rows, lanes = fields[0].shape
     tiles = rows // SUB
     sub, lane = iotas(lanes)
@@ -322,8 +322,16 @@
         terms = lat_inner(here, sub, True)
         for t in range(tiles):
             lon = lon_terms([x[t] for x in here], True)
-            for g in range(3):
-                part[g, layer + 3, t] += terms[t][g] + jnp.where(away, lon[g], 0.0)
+            total = [
+                part[g, layer + 3, t] + terms[t][g] + jnp.where(away, lon[g], 0.0) for g in range(3)
+            ]
+            stiff = fields[5][layer, at(t), :] * LAP_SCALE
+            for g in range(2):
+                part[g, layer + 3, t] = total[g]
+                update = stiff * total[g]
+                base[g, layer, t] = 2.0 * here[g][t] - fields[3 + g][layer, at(t), :] + update
+            base[2, layer, t] = bulk_in[layer, at(t), :] + here[0][t] * update
+            base[3, layer, t] = density_in[layer, at(t), :] + RHO_SCALE * total[2]
         return carry
 
     lax.fori_loop(0, layers, own, 0, unroll=2)
@@ -386,10 +394,10 @@
 
 
 def middle_kernel(*refs):
-    fields, (bulk_in, density_in) = refs[:6], refs[6:8]
-    packs, from_core, from_core2, wide, part = refs[8:12], refs[12], refs[13], refs[14], refs[15]
-    first, first_pack, stiff_pack, buoy_halo, flux_out, sums, done = refs[16:23]
-    first_halo, own_pack, part_last, halo_pack, lap_pack = refs[23:]
+    fields, base = refs[:6], refs[6]
+    packs, from_core, from_core2, wide, part = refs[7:11], refs[11], refs[12], refs[13], refs[14]
+    first, first_pack, stiff_pack, buoy_halo, flux_out, sums, done = refs[15:22]
+    first_halo, own_pack, part_last, halo_pack, lap_pack = refs[22:]
     layers, rows, lanes = fields[0].shape
     tiles = rows // SUB
     sub, lane = iotas(lanes)
@@ -459,15 +467,13 @@
             group, s = divmod(layer, per)
             buoy_halo[layer, t] = spread(halo_pack[2, group, t], s)
             stiff = fields[5][layer, at(t), :] * LAP_SCALE
-            here = [wide[f, layer + 6, t] for f in range(2)]
             for g in range(2):
                 first_halo[g, layer, t] = spread(first_pack[g, group, t], s)
-                lap = part[g, layer + 3, t] + at_ends(own_pack[g, group, t], s, lane)
-                update = stiff * lap
-                first[g, layer + 3, t] = 2.0 * here[g] - fields[3 + g][layer, at(t), :] + update
-            sums[0, layer, t] = bulk_in[layer, at(t), :] + here[0] * update
-            rho = part[2, layer + 3, t] + at_ends(own_pack[2, group, t], s, lane)
-            sums[1, layer, t] = density_in[layer, at(t), :] + RHO_SCALE * rho
+                update = stiff * at_ends(own_pack[g, group, t], s, lane)
+                first[g, layer + 3, t] = base[g, layer, t] + update
+            sums[0, layer, t] = base[2, layer, t] + wide[0, layer + 6, t] * update
+            rho = at_ends(own_pack[2, group, t], s, lane)
+            sums[1, layer, t] = base[3, layer, t] + RHO_SCALE * rho
         for e in range(3):
             stiff = from_core[24 + e, at(t), :] * LAP_SCALE
             for g in range(2):
@@ -698,16 +704,17 @@
     pairs_of_groups = -(-groups // 2)
     lat_edge = made(2 * layers + 4 + pairs_of_groups, SUB, lanes)
     packs = [from_left, from_right, to_left, to_right]
-    wide, part, to_first, to_second, to_third = call(
+    wide, part, base, to_first, to_second, to_third = call(
         inner_kernel,
         (
             made(3, layers + 12, tiles, SUB, lanes),
             made(3, layers + 6, tiles, SUB, lanes),
+            made(4, layers, tiles, SUB, lanes),
             lat_edge,
             lat_edge,
             lat_edge,
         ),
-        [*fields, from_core],
+        [*fields, kernel_bulk_in, kernel_density_in, from_core],
     )
     to_first, to_second, to_third, to_core, edges = call(
         turn_kernel,
@@ -732,8 +739,7 @@
         ),
         [
             *fields,
-            kernel_bulk_in,
-            kernel_density_in,
+            base,
             *packs,
             from_core,
             from_core2,

time: 16.5 us -> 16.6 us (level)
  transfers between devices with their start and end apart: 7 -> 7, of which waited for: 1 -> 1; matrix products, arithmetic and copies ran while one was open for 0% -> 0% of each run, Pallas kernels for 26% -> 25%
where the time goes in v9:
time: 16.6 us; the launch traced here: 16.3 us
  Pallas kernels  7.87 us (47%)
  starting transfers between devices  5.85 us (35%)
  waiting for transfers between devices  1.81 us (11%)
  between operations  0.72 us (4%)
    pallas_call x5, Pallas kernels, call(): pl.pallas_call(kernel, out_shape=out_shape, in_specs=in_specs or [VMEM] *...  7.87 us
    ppermute x1, waiting for transfers between devices, shards(): from_right = lax.ppermute(to_left, 'lon', [(b, a) for a, b in ring])  1.79 us
    ppermute x1, starting transfers between devices, shards(): from_core2 = lax.ppermute(to_core, 'rad', swap)  1.56 us
    ppermute x1, starting transfers between devices, shards(): from_left = lax.ppermute(to_right, 'lon', ring)  1.21 us
    ppermute x1, starting transfers between devices, shards(): from_second = lax.ppermute(to_second, ('lat', 'rad'), pairs(count, 1, 2))  1.19 us
    ppermute x1, starting transfers between devices, shards(): from_core = lax.ppermute(to_core, 'rad', swap)  0.74 us
    ppermute x1, starting transfers between devices, shards(): from_third = lax.ppermute(to_third, ('lat', 'rad'), pairs(count, 2, 4))  0.71 us
  transfers between devices with their start and end apart: 7, of which 1 were waited for; matrix products, arithmetic and copies ran while one was open for 0% of the time, Pallas kernels for 25%

profile of v9, /device:TPU:11, one launch (start us, length us, event | category | flops | bytes accessed | tf_op | source)
XLA Modules:
  0.0 16.3 jit_solution(8778449716909590806)
XLA Ops:
  0.6 0.0 copy-start.1
  0.6 0.0 copy-start
  0.7 1.6 %shard_map.127 = (f32[8,32,128]{2,1,0:T(8,128)S(1)}, f32[8,32,128]{2,1,0:T(8,128)S(1)}, f32[8,32,128]{2,1,0:T(8,128)S(1)}, f32[8,32,128]{2,1,0:T(8,128)S(1)}, f3...) custom-call(f32[8,32,128]{2,1,0:T(8,128)} %refs_0_.1, ...), custom_call_target="tpu_custom_call" | custom-call | tf_op jit(solution)/shard_map/pallas_call | solution.py:667
  2.3 0.7 %collective-permute-start = (f32[27,32,128]{2,1,0:T(8,128)S(1)}, f32[27,32,128]{2,1,0:T(8,128)S(1)}, u32[]{:S(2)}, u32[]{:S(2)}) collective-permute-start(f32[27,32,128]{2,1,0:T(8,128)S(1)} %get-tuple-element.39), channel_id=1, source_target_pairs={{0,1},{1,0},{2,3},{3,2},{4,5},{5,4},{6,7},{7,6},{8,9},{9,8},{10,11... | collective-permute-start | bytes 1327112 | tf_op jit(solution)/shard_map/ppermute | solution.py:703
  3.0 1.2 %collective-permute-start.1 = (f32[2,32,128]{2,1,0:T(8,128)S(1)}, f32[2,32,128]{2,1,0:T(8,128)S(1)}, u32[]{:S(2)}, u32[]{:S(2)}) collective-permute-start(f32[2,32,128]{2,1,0:T(8,128)S(1)} %get-tuple-element.42.refs_9_.refs_10_), channel_id=1, source_target_pairs={{0,8},{8,16},{16,24},{24,0},{1,9},{9,17},{17,25},{25,1},{2,10},{10... | collective-permute-start | bytes 98312 | tf_op jit(solution)/shard_map/ppermute | solution.py:701
  4.2 0.3 %collective-permute-start.2 = (f32[2,32,128]{2,1,0:T(8,128)S(1)}, f32[2,32,128]{2,1,0:T(8,128)S(1)}, u32[]{:S(2)}, u32[]{:S(2)}) collective-permute-start(f32[2,32,128]{2,1,0:T(8,128)S(1)} %get-tuple-element.43.refs_8_.refs_9_), channel_id=1, source_target_pairs={{8,0},{16,8},{24,16},{0,24},{9,1},{17,9},{25,17},{1,25},{10,2},{18... | collective-permute-start | bytes 98312 | tf_op jit(solution)/shard_map/ppermute | solution.py:702
  4.5 0.0 collective-permute-done.refs_8_.refs_11_.refs_6_
  4.5 0.0 copy-done.1
  4.5 0.0 copy-done
  4.5 1.6 %shard_map.128 = (f32[3,20,4,8,128]{4,3,2,1,0:T(8,128)S(1)}, f32[3,14,4,8,128]{4,3,2,1,0:T(8,128)S(1)}, f32[4,8,4,8,128]{4,3,2,1,0:T(8,128)S(1)}, f32[21,8,128]{...) custom-call(f32[8,32,128]{2,1,0:T(8,128)S(1)} %get-tuple-element.33.refs_0_, ...), custom_call_target="tpu_custom_call" | custom-call | tf_op jit(solution)/shard_map/pallas_call | solution.py:667
  6.1 0.0 collective-permute-done.1.refs_6_.refs_7_
  6.1 1.8 %collective-permute-done.2.refs_7_.refs_8_ = f32[2,32,128]{2,1,0:T(8,128)S(1)} collective-permute-done((f32[2,32,128]{2,1,0:T(8,128)S(1)}, f32[2,32,128]{2,1,0:T(8,128)S(1)}, u32[]{:S(2)}, u32[]{:S(2)}) %collective-permute-start.2) | collective-permute-done | bytes 32800 | tf_op jit(solution)/shard_map/ppermute | solution.py:702
  7.9 0.3 %shard_map.129 = (f32[21,8,128]{2,1,0:T(8,128)S(1)}, f32[21,8,128]{2,1,0:T(8,128)S(1)}, f32[21,8,128]{2,1,0:T(8,128)S(1)}, f32[4,32,128]{2,1,0:T(8,128)S(1)}, f32[2,1,8,128]{3,2,1,0:T(8,128)S(1)}) custom-call(f32[8,32,128]{2,1,0:T(8,128)S(1)} %get-tuple-element.33.refs_0_, ...), custom_call_target="tpu_custom_call", output_to_operand_aliasing={{0}: (11, {}), {1}: (12, {}), {2}: (13, {})} | custom-call | tf_op jit(solution)/shard_map/pallas_call | solution.py:667
  8.2 1.6 %collective-permute-start.3 = (f32[4,32,128]{2,1,0:T(8,128)S(1)}, f32[4,32,128]{2,1,0:T(8,128)S(1)}, u32[]{:S(2)}, u32[]{:S(2)}) collective-permute-start(f32[4,32,128]{2,1,0:T(8,128)S(1)} %get-tuple-element.48), channel_id=1, source_target_pairs={{0,1},{1,0},{2,3},{3,2},{4,5},{5,4},{6,7},{7,6},{8,9},{9,8},{10,11... | collective-permute-start | bytes 196616 | tf_op jit(solution)/shard_map/ppermute | solution.py:728
  9.7 0.2 %collective-permute-start.4 = (f32[21,8,128]{2,1,0:T(8,128)S(1)}, f32[21,8,128]{2,1,0:T(8,128)S(1)}, u32[]{:S(2)}, u32[]{:S(2)}) collective-permute-start(f32[21,8,128]{2,1,0:T(8,128)S(1)} %get-tuple-element.57), channel_id=1, source_target_pairs={{0,2},{1,3},{2,0},{3,1},{4,5},{5,4},{6,7},{7,6},{8,10},{9,11},{10,... | collective-permute-start | bytes 258056 | tf_op jit(solution)/shard_map/ppermute | solution.py:725
  9.9 1.2 %collective-permute-start.5 = (f32[21,8,128]{2,1,0:T(8,128)S(1)}, f32[21,8,128]{2,1,0:T(8,128)S(1)}, u32[]{:S(2)}, u32[]{:S(2)}) collective-permute-start(f32[21,8,128]{2,1,0:T(8,128)S(1)} %get-tuple-element.58), channel_id=1, source_target_pairs={{0,1},{1,0},{2,4},{3,5},{4,2},{5,3},{6,7},{7,6},{8,9},{9,8},{10,12... | collective-permute-start | bytes 258056 | tf_op jit(solution)/shard_map/ppermute | solution.py:726
  11.1 0.7 %collective-permute-start.6 = (f32[21,8,128]{2,1,0:T(8,128)S(1)}, f32[21,8,128]{2,1,0:T(8,128)S(1)}, u32[]{:S(2)}, u32[]{:S(2)}) collective-permute-start(f32[21,8,128]{2,1,0:T(8,128)S(1)} %get-tuple-element.59), channel_id=1, source_target_pairs={{0,1},{1,0},{2,3},{3,2},{4,6},{5,7},{6,4},{7,5},{8,9},{9,8},{10,11... | collective-permute-start | bytes 258056 | tf_op jit(solution)/shard_map/ppermute | solution.py:727
  11.8 0.0 collective-permute-done.3.refs_12_
  11.8 2.5 %shard_map.130 = (f32[2,14,4,8,128]{4,3,2,1,0:T(8,128)S(1)}, f32[2,2,4,8,128]{4,3,2,1,0:T(8,128)S(1)}, f32[2,4,8,128]{3,2,1,0:T(8,128)S(1)}, f32[8,4,8,128]{3,2,...) custom-call(f32[8,32,128]{2,1,0:T(8,128)S(1)} %get-tuple-element.33., ...), custom_call_target="tpu_custom_call" | custom-call | flops 4000000000 | bytes 1000000 | tf_op jit(solution)/shard_map/pallas_call | solution.py:667
  14.4 0.0 collective-permute-done.4.refs_16_
  14.4 0.0 collective-permute-done.5.refs_17_
  14.4 0.0 collective-permute-done.6.refs_18_
  14.4 1.8 %shard_map.131 = (f32[8,32,128]{2,1,0:T(8,128)}, f32[8,32,128]{2,1,0:T(8,128)}, f32[8,32,128]{2,1,0:T(8,128)}, f32[8,32,128]{2,1,0:T(8,128)}, f32[8,32,128]{2,1,0:T(8,128)}, /*index=5*/f32[8,32,128]{2,1,0:T(8,128)}) custom-call(f32[8,32,128]{2,1,0:T(8,128)S(1)} %get-tuple-element.33.refs_0_, f32[8,32,128]{2,1,0:T(8,128)S(1)} %get-tuple-element.34.refs_1_, ...), custom_call_target="tpu_custom_call" | custom-call | tf_op jit(solution)/shard_map/pallas_call | solution.py:667
Async XLA Ops:
  0.6 3.8 %copy-start.1 = (f32[8,32,128]{2,1,0:T(8,128)S(1)}, f32[8,32,128]{2,1,0:T(8,128)}, u32[]{:S(2)}) copy-start(f32[8,32,128]{2,1,0:T(8,128)} %refs_7_.1) | copy-start | bytes 393220
  0.6 3.8 %copy-start = (f32[8,32,128]{2,1,0:T(8,128)S(1)}, f32[8,32,128]{2,1,0:T(8,128)}, u32[]{:S(2)}) copy-start(f32[8,32,128]{2,1,0:T(8,128)} %refs_6_.1) | copy-start | bytes 393220
  2.3 2.2 %collective-permute-start = (f32[27,32,128]{2,1,0:T(8,128)S(1)}, f32[27,32,128]{2,1,0:T(8,128)S(1)}, u32[]{:S(2)}, u32[]{:S(2)}) collective-permute-start(f32[27,32,128]{2,1,0:T(8,128)S(1)} %get-tuple-element.39), channel_id=1, source_target_pairs={{0,1},{1,0},{2,3},{3,2},{4,5},{5,4},{6,7},{7,6},{8,9},{9,8},{10,11... | collective-permute-start | bytes 1327112 | tf_op jit(solution)/shard_map/ppermute | solution.py:703
  3.0 3.1 %collective-permute-start.1 = (f32[2,32,128]{2,1,0:T(8,128)S(1)}, f32[2,32,128]{2,1,0:T(8,128)S(1)}, u32[]{:S(2)}, u32[]{:S(2)}) collective-permute-start(f32[2,32,128]{2,1,0:T(8,128)S(1)} %get-tuple-element.42.refs_9_.refs_10_), channel_id=1, source_target_pairs={{0,8},{8,16},{16,24},{24,0},{1,9},{9,17},{17,25},{25,1},{2,10},{10... | collective-permute-start | bytes 98312 | tf_op jit(solution)/shard_map/ppermute | solution.py:701
  4.2 3.7 %collective-permute-start.2 = (f32[2,32,128]{2,1,0:T(8,128)S(1)}, f32[2,32,128]{2,1,0:T(8,128)S(1)}, u32[]{:S(2)}, u32[]{:S(2)}) collective-permute-start(f32[2,32,128]{2,1,0:T(8,128)S(1)} %get-tuple-element.43.refs_8_.refs_9_), channel_id=1, source_target_pairs={{8,0},{16,8},{24,16},{0,24},{9,1},{17,9},{25,17},{1,25},{10,2},{18... | collective-permute-start | bytes 98312 | tf_op jit(solution)/shard_map/ppermute | solution.py:702
  8.2 3.7 %collective-permute-start.3 = (f32[4,32,128]{2,1,0:T(8,128)S(1)}, f32[4,32,128]{2,1,0:T(8,128)S(1)}, u32[]{:S(2)}, u32[]{:S(2)}) collective-permute-start(f32[4,32,128]{2,1,0:T(8,128)S(1)} %get-tuple-element.48), channel_id=1, source_target_pairs={{0,1},{1,0},{2,3},{3,2},{4,5},{5,4},{6,7},{7,6},{8,9},{9,8},{10,11... | collective-permute-start | bytes 196616 | tf_op jit(solution)/shard_map/ppermute | solution.py:728
  9.7 4.7 %collective-permute-start.4 = (f32[21,8,128]{2,1,0:T(8,128)S(1)}, f32[21,8,128]{2,1,0:T(8,128)S(1)}, u32[]{:S(2)}, u32[]{:S(2)}) collective-permute-start(f32[21,8,128]{2,1,0:T(8,128)S(1)} %get-tuple-element.57), channel_id=1, source_target_pairs={{0,2},{1,3},{2,0},{3,1},{4,5},{5,4},{6,7},{7,6},{8,10},{9,11},{10,... | collective-permute-start | bytes 258056 | tf_op jit(solution)/shard_map/ppermute | solution.py:725
  9.9 4.5 %collective-permute-start.5 = (f32[21,8,128]{2,1,0:T(8,128)S(1)}, f32[21,8,128]{2,1,0:T(8,128)S(1)}, u32[]{:S(2)}, u32[]{:S(2)}) collective-permute-start(f32[21,8,128]{2,1,0:T(8,128)S(1)} %get-tuple-element.58), channel_id=1, source_target_pairs={{0,1},{1,0},{2,4},{3,5},{4,2},{5,3},{6,7},{7,6},{8,9},{9,8},{10,12... | collective-permute-start | bytes 258056 | tf_op jit(solution)/shard_map/ppermute | solution.py:726
  11.1 3.3 %collective-permute-start.6 = (f32[21,8,128]{2,1,0:T(8,128)S(1)}, f32[21,8,128]{2,1,0:T(8,128)S(1)}, u32[]{:S(2)}, u32[]{:S(2)}) collective-permute-start(f32[21,8,128]{2,1,0:T(8,128)S(1)} %get-tuple-element.59), channel_id=1, source_target_pairs={{0,1},{1,0},{2,3},{3,2},{4,6},{5,7},{6,4},{7,5},{8,9},{9,8},{10,11... | collective-permute-start | bytes 258056 | tf_op jit(solution)/shard_map/ppermute | solution.py:727

commit v10 on v9

--- a/solution.py
+++ b/solution.py
@@ -522,7 +522,7 @@
     wide, first, first_pack, stiff_pack, buoy_halo, flux_in, sums, done = refs[7:15]
     edges, from_first, from_second, from_third = refs[15:19]
     outs = refs[19:25]
-    fixed, fixed_halo, ring_buoy, part, made, sems = refs[25:]
+    fixed, fixed_halo, ring_buoy, made, sems = refs[25:]
     layers, rows, lanes = fields[0].shape
     tiles = rows // SUB
     sub, lane = iotas(lanes)
@@ -612,13 +612,8 @@
             fixed[g, layer + 3, 2] = join(*x) + stiff * LAP_SCALE * lap
         ring_buoy[layer] = join(*halos[2])
 
-    for n, (t, _) in enumerate(ends):
-        terms = radial(lambda f, k: fixed[f, 3 + k, n], lambda k: wide[2, 6 + k, t], layers)
-        for k, term in enumerate(terms):
-            for g in range(3):
-                part[g, k, n] = term[g]
-
-    def last(layer, n):
+
+    def last(layer, n, radials):
         t = ends[n][0]
         rings = [[fixed[f, layer + 3, 2], fixed[f, layer + 3, n]] for f in range(2)]
         rings.append([ring_buoy[layer], wide[2, layer + 6, t]])
@@ -635,17 +630,18 @@
         laps, rho = longitudinal(here, there, lane, False, True)
         stiff = fields[5][layer, at(t), :] * LAP_SCALE
         for g in range(2):
-            update = stiff * (part[g, layer, n] + lat[g] + laps[0][g])
+            update = stiff * (radials[g] + lat[g] + laps[0][g])
             made[2 * g, layer, n] = 2.0 * here[g] - fields[g][layer, at(t), :] + update
-            made[2 * g + 1, layer, n] = here[g]
         made[4, layer, n] += here[0] * update
-        made[5, layer, n] += RHO_SCALE * (part[2, layer, n] + lat[2] + rho)
+        made[5, layer, n] += RHO_SCALE * (radials[2] + lat[2] + rho)
 
     for n, (t, _) in enumerate(ends):
+        terms = radial(lambda f, k: fixed[f, 3 + k, n], lambda k: wide[2, 6 + k, t], layers)
         for layer in range(layers):
-            last(layer, n)
+            last(layer, n, terms[layer])
         for k, out in enumerate(outs):
-            copy = pltpu.make_async_copy(made.at[k, :, n], out.at[:, at(t), :], sems.at[k, 1 + n])
+            source = fixed.at[k // 2, pl.ds(3, layers), n] if k in (1, 3) else made.at[k, :, n]
+            copy = pltpu.make_async_copy(source, out.at[:, at(t), :], sems.at[k, 1 + n])
             copy.start()
             copies.append(copy)
     for copy in copies:
@@ -779,7 +775,6 @@
             made(2, layers + 6, 3, SUB, lanes),
             made(2, layers, 2, SUB, lanes),
             made(layers, SUB, lanes),
-            made(3, layers, 2, SUB, lanes),
             made(6, layers, 2, SUB, lanes),
             pltpu.SemaphoreType.DMA((6, 3)),
         ],

time: 16.6 us -> 16.5 us (level)
  transfers between devices with their start and end apart: 7 -> 7, of which waited for: 1 -> 1; matrix products, arithmetic and copies ran while one was open for 0% -> 0% of each run, Pallas kernels for 25% -> 26%
where the time goes in v10:
time: 16.5 us; the launch traced here: 16.2 us
  Pallas kernels  7.85 us (48%)
  starting transfers between devices  5.85 us (35%)
  waiting for transfers between devices  1.81 us (11%)
  between operations  0.72 us (4%)
    pallas_call x5, Pallas kernels, call(): pl.pallas_call(kernel, out_shape=out_shape, in_specs=in_specs or [VMEM] *...  7.85 us
    ppermute x1, waiting for transfers between devices, shards(): from_right = lax.ppermute(to_left, 'lon', [(b, a) for a, b in ring])  1.79 us
    ppermute x1, starting transfers between devices, shards(): from_core2 = lax.ppermute(to_core, 'rad', swap)  1.56 us
    ppermute x1, starting transfers between devices, shards(): from_left = lax.ppermute(to_right, 'lon', ring)  1.21 us
    ppermute x1, starting transfers between devices, shards(): from_second = lax.ppermute(to_second, ('lat', 'rad'), pairs(count, 1, 2))  1.19 us
    ppermute x1, starting transfers between devices, shards(): from_core = lax.ppermute(to_core, 'rad', swap)  0.74 us
    ppermute x1, starting transfers between devices, shards(): from_third = lax.ppermute(to_third, ('lat', 'rad'), pairs(count, 2, 4))  0.71 us
  transfers between devices with their start and end apart: 7, of which 1 were waited for; matrix products, arithmetic and copies ran while one was open for 0% of the time, Pallas kernels for 26%

profile of v10, /device:TPU:11, one launch (start us, length us, event | category | flops | bytes accessed | tf_op | source)
XLA Modules:
  0.0 16.2 jit_solution(7501939965784705289)
XLA Ops:
  0.6 0.0 copy-start.1
  0.6 0.0 copy-start
  0.7 1.6 %shard_map.127 = (f32[8,32,128]{2,1,0:T(8,128)S(1)}, f32[8,32,128]{2,1,0:T(8,128)S(1)}, f32[8,32,128]{2,1,0:T(8,128)S(1)}, f32[8,32,128]{2,1,0:T(8,128)S(1)}, f3...) custom-call(f32[8,32,128]{2,1,0:T(8,128)} %refs_0_.1, ...), custom_call_target="tpu_custom_call" | custom-call | tf_op jit(solution)/shard_map/pallas_call | solution.py:663
  2.3 0.7 %collective-permute-start = (f32[27,32,128]{2,1,0:T(8,128)S(1)}, f32[27,32,128]{2,1,0:T(8,128)S(1)}, u32[]{:S(2)}, u32[]{:S(2)}) collective-permute-start(f32[27,32,128]{2,1,0:T(8,128)S(1)} %get-tuple-element.39), channel_id=1, source_target_pairs={{0,1},{1,0},{2,3},{3,2},{4,5},{5,4},{6,7},{7,6},{8,9},{9,8},{10,11... | collective-permute-start | bytes 1327112 | tf_op jit(solution)/shard_map/ppermute | solution.py:699
  3.0 1.2 %collective-permute-start.1 = (f32[2,32,128]{2,1,0:T(8,128)S(1)}, f32[2,32,128]{2,1,0:T(8,128)S(1)}, u32[]{:S(2)}, u32[]{:S(2)}) collective-permute-start(f32[2,32,128]{2,1,0:T(8,128)S(1)} %get-tuple-element.42.refs_9_.refs_10_), channel_id=1, source_target_pairs={{0,8},{8,16},{16,24},{24,0},{1,9},{9,17},{17,25},{25,1},{2,10},{10... | collective-permute-start | bytes 98312 | tf_op jit(solution)/shard_map/ppermute | solution.py:697
  4.2 0.3 %collective-permute-start.2 = (f32[2,32,128]{2,1,0:T(8,128)S(1)}, f32[2,32,128]{2,1,0:T(8,128)S(1)}, u32[]{:S(2)}, u32[]{:S(2)}) collective-permute-start(f32[2,32,128]{2,1,0:T(8,128)S(1)} %get-tuple-element.43.refs_8_.refs_9_), channel_id=1, source_target_pairs={{8,0},{16,8},{24,16},{0,24},{9,1},{17,9},{25,17},{1,25},{10,2},{18... | collective-permute-start | bytes 98312 | tf_op jit(solution)/shard_map/ppermute | solution.py:698
  4.5 0.0 collective-permute-done.refs_8_.refs_11_.refs_6_
  4.5 0.0 copy-done.1
  4.5 0.0 copy-done
  4.5 1.6 %shard_map.128 = (f32[3,20,4,8,128]{4,3,2,1,0:T(8,128)S(1)}, f32[3,14,4,8,128]{4,3,2,1,0:T(8,128)S(1)}, f32[4,8,4,8,128]{4,3,2,1,0:T(8,128)S(1)}, f32[21,8,128]{...) custom-call(f32[8,32,128]{2,1,0:T(8,128)S(1)} %get-tuple-element.33.refs_0_, ...), custom_call_target="tpu_custom_call" | custom-call | tf_op jit(solution)/shard_map/pallas_call | solution.py:663
  6.1 0.0 collective-permute-done.1.refs_6_.refs_7_
  6.1 1.8 %collective-permute-done.2.refs_7_.refs_8_ = f32[2,32,128]{2,1,0:T(8,128)S(1)} collective-permute-done((f32[2,32,128]{2,1,0:T(8,128)S(1)}, f32[2,32,128]{2,1,0:T(8,128)S(1)}, u32[]{:S(2)}, u32[]{:S(2)}) %collective-permute-start.2) | collective-permute-done | bytes 32800 | tf_op jit(solution)/shard_map/ppermute | solution.py:698
  7.9 0.3 %shard_map.129 = (f32[21,8,128]{2,1,0:T(8,128)S(1)}, f32[21,8,128]{2,1,0:T(8,128)S(1)}, f32[21,8,128]{2,1,0:T(8,128)S(1)}, f32[4,32,128]{2,1,0:T(8,128)S(1)}, f32[2,1,8,128]{3,2,1,0:T(8,128)S(1)}) custom-call(f32[8,32,128]{2,1,0:T(8,128)S(1)} %get-tuple-element.33.refs_0_, ...), custom_call_target="tpu_custom_call", output_to_operand_aliasing={{0}: (11, {}), {1}: (12, {}), {2}: (13, {})} | custom-call | tf_op jit(solution)/shard_map/pallas_call | solution.py:663
  8.2 1.6 %collective-permute-start.3 = (f32[4,32,128]{2,1,0:T(8,128)S(1)}, f32[4,32,128]{2,1,0:T(8,128)S(1)}, u32[]{:S(2)}, u32[]{:S(2)}) collective-permute-start(f32[4,32,128]{2,1,0:T(8,128)S(1)} %get-tuple-element.48), channel_id=1, source_target_pairs={{0,1},{1,0},{2,3},{3,2},{4,5},{5,4},{6,7},{7,6},{8,9},{9,8},{10,11... | collective-permute-start | bytes 196616 | tf_op jit(solution)/shard_map/ppermute | solution.py:724
  9.7 0.2 %collective-permute-start.4 = (f32[21,8,128]{2,1,0:T(8,128)S(1)}, f32[21,8,128]{2,1,0:T(8,128)S(1)}, u32[]{:S(2)}, u32[]{:S(2)}) collective-permute-start(f32[21,8,128]{2,1,0:T(8,128)S(1)} %get-tuple-element.57), channel_id=1, source_target_pairs={{0,2},{1,3},{2,0},{3,1},{4,5},{5,4},{6,7},{7,6},{8,10},{9,11},{10,... | collective-permute-start | bytes 258056 | tf_op jit(solution)/shard_map/ppermute | solution.py:721
  9.9 1.2 %collective-permute-start.5 = (f32[21,8,128]{2,1,0:T(8,128)S(1)}, f32[21,8,128]{2,1,0:T(8,128)S(1)}, u32[]{:S(2)}, u32[]{:S(2)}) collective-permute-start(f32[21,8,128]{2,1,0:T(8,128)S(1)} %get-tuple-element.58), channel_id=1, source_target_pairs={{0,1},{1,0},{2,4},{3,5},{4,2},{5,3},{6,7},{7,6},{8,9},{9,8},{10,12... | collective-permute-start | bytes 258056 | tf_op jit(solution)/shard_map/ppermute | solution.py:722
  11.1 0.7 %collective-permute-start.6 = (f32[21,8,128]{2,1,0:T(8,128)S(1)}, f32[21,8,128]{2,1,0:T(8,128)S(1)}, u32[]{:S(2)}, u32[]{:S(2)}) collective-permute-start(f32[21,8,128]{2,1,0:T(8,128)S(1)} %get-tuple-element.59), channel_id=1, source_target_pairs={{0,1},{1,0},{2,3},{3,2},{4,6},{5,7},{6,4},{7,5},{8,9},{9,8},{10,11... | collective-permute-start | bytes 258056 | tf_op jit(solution)/shard_map/ppermute | solution.py:723
  11.8 0.0 collective-permute-done.3.refs_12_
  11.8 2.5 %shard_map.130 = (f32[2,14,4,8,128]{4,3,2,1,0:T(8,128)S(1)}, f32[2,2,4,8,128]{4,3,2,1,0:T(8,128)S(1)}, f32[2,4,8,128]{3,2,1,0:T(8,128)S(1)}, f32[8,4,8,128]{3,2,...) custom-call(f32[8,32,128]{2,1,0:T(8,128)S(1)} %get-tuple-element.33., ...), custom_call_target="tpu_custom_call" | custom-call | flops 4000000000 | bytes 1000000 | tf_op jit(solution)/shard_map/pallas_call | solution.py:663
  14.4 0.0 collective-permute-done.4.refs_16_
  14.4 0.0 collective-permute-done.5.refs_17_
  14.4 0.0 collective-permute-done.6.refs_18_
  14.4 1.8 %shard_map.131 = (f32[8,32,128]{2,1,0:T(8,128)}, f32[8,32,128]{2,1,0:T(8,128)}, f32[8,32,128]{2,1,0:T(8,128)}, f32[8,32,128]{2,1,0:T(8,128)}, f32[8,32,128]{2,1,0:T(8,128)}, /*index=5*/f32[8,32,128]{2,1,0:T(8,128)}) custom-call(f32[8,32,128]{2,1,0:T(8,128)S(1)} %get-tuple-element.33.refs_0_, f32[8,32,128]{2,1,0:T(8,128)S(1)} %get-tuple-element.34.refs_1_, ...), custom_call_target="tpu_custom_call" | custom-call | tf_op jit(solution)/shard_map/pallas_call | solution.py:663
Async XLA Ops:
  0.6 3.8 %copy-start.1 = (f32[8,32,128]{2,1,0:T(8,128)S(1)}, f32[8,32,128]{2,1,0:T(8,128)}, u32[]{:S(2)}) copy-start(f32[8,32,128]{2,1,0:T(8,128)} %refs_7_.1) | copy-start | bytes 393220
  0.6 3.8 %copy-start = (f32[8,32,128]{2,1,0:T(8,128)S(1)}, f32[8,32,128]{2,1,0:T(8,128)}, u32[]{:S(2)}) copy-start(f32[8,32,128]{2,1,0:T(8,128)} %refs_6_.1) | copy-start | bytes 393220
  2.3 2.2 %collective-permute-start = (f32[27,32,128]{2,1,0:T(8,128)S(1)}, f32[27,32,128]{2,1,0:T(8,128)S(1)}, u32[]{:S(2)}, u32[]{:S(2)}) collective-permute-start(f32[27,32,128]{2,1,0:T(8,128)S(1)} %get-tuple-element.39), channel_id=1, source_target_pairs={{0,1},{1,0},{2,3},{3,2},{4,5},{5,4},{6,7},{7,6},{8,9},{9,8},{10,11... | collective-permute-start | bytes 1327112 | tf_op jit(solution)/shard_map/ppermute | solution.py:699
  3.0 3.1 %collective-permute-start.1 = (f32[2,32,128]{2,1,0:T(8,128)S(1)}, f32[2,32,128]{2,1,0:T(8,128)S(1)}, u32[]{:S(2)}, u32[]{:S(2)}) collective-permute-start(f32[2,32,128]{2,1,0:T(8,128)S(1)} %get-tuple-element.42.refs_9_.refs_10_), channel_id=1, source_target_pairs={{0,8},{8,16},{16,24},{24,0},{1,9},{9,17},{17,25},{25,1},{2,10},{10... | collective-permute-start | bytes 98312 | tf_op jit(solution)/shard_map/ppermute | solution.py:697
  4.2 3.7 %collective-permute-start.2 = (f32[2,32,128]{2,1,0:T(8,128)S(1)}, f32[2,32,128]{2,1,0:T(8,128)S(1)}, u32[]{:S(2)}, u32[]{:S(2)}) collective-permute-start(f32[2,32,128]{2,1,0:T(8,128)S(1)} %get-tuple-element.43.refs_8_.refs_9_), channel_id=1, source_target_pairs={{8,0},{16,8},{24,16},{0,24},{9,1},{17,9},{25,17},{1,25},{10,2},{18... | collective-permute-start | bytes 98312 | tf_op jit(solution)/shard_map/ppermute | solution.py:698
  8.2 3.7 %collective-permute-start.3 = (f32[4,32,128]{2,1,0:T(8,128)S(1)}, f32[4,32,128]{2,1,0:T(8,128)S(1)}, u32[]{:S(2)}, u32[]{:S(2)}) collective-permute-start(f32[4,32,128]{2,1,0:T(8,128)S(1)} %get-tuple-element.48), channel_id=1, source_target_pairs={{0,1},{1,0},{2,3},{3,2},{4,5},{5,4},{6,7},{7,6},{8,9},{9,8},{10,11... | collective-permute-start | bytes 196616 | tf_op jit(solution)/shard_map/ppermute | solution.py:724
  9.7 4.7 %collective-permute-start.4 = (f32[21,8,128]{2,1,0:T(8,128)S(1)}, f32[21,8,128]{2,1,0:T(8,128)S(1)}, u32[]{:S(2)}, u32[]{:S(2)}) collective-permute-start(f32[21,8,128]{2,1,0:T(8,128)S(1)} %get-tuple-element.57), channel_id=1, source_target_pairs={{0,2},{1,3},{2,0},{3,1},{4,5},{5,4},{6,7},{7,6},{8,10},{9,11},{10,... | collective-permute-start | bytes 258056 | tf_op jit(solution)/shard_map/ppermute | solution.py:721
  9.9 4.5 %collective-permute-start.5 = (f32[21,8,128]{2,1,0:T(8,128)S(1)}, f32[21,8,128]{2,1,0:T(8,128)S(1)}, u32[]{:S(2)}, u32[]{:S(2)}) collective-permute-start(f32[21,8,128]{2,1,0:T(8,128)S(1)} %get-tuple-element.58), channel_id=1, source_target_pairs={{0,1},{1,0},{2,4},{3,5},{4,2},{5,3},{6,7},{7,6},{8,9},{9,8},{10,12... | collective-permute-start | bytes 258056 | tf_op jit(solution)/shard_map/ppermute | solution.py:722
  11.1 3.3 %collective-permute-start.6 = (f32[21,8,128]{2,1,0:T(8,128)S(1)}, f32[21,8,128]{2,1,0:T(8,128)S(1)}, u32[]{:S(2)}, u32[]{:S(2)}) collective-permute-start(f32[21,8,128]{2,1,0:T(8,128)S(1)} %get-tuple-element.59), channel_id=1, source_target_pairs={{0,1},{1,0},{2,3},{3,2},{4,6},{5,7},{6,4},{7,5},{8,9},{9,8},{10,11... | collective-permute-start | bytes 258056 | tf_op jit(solution)/shard_map/ppermute | solution.py:723
